TPU v7x, 256 devices: a whole 4x4x8 slice. The times are simulated.
256 devices in a mesh: cuts: 32 (over z, y_lo, core), out: 8 (over y_hi, x).
Axes of the slice: x: 4, y: 4 (y_hi: 2, y_lo: 2; y = y_hi * 2 + y_lo), z: 8, core: 2. Of those that a mesh axis runs over, the one named last changes fastest.
Arguments:
- panels: bfloat16 [128, 128, 2, 128], P('out', 'cuts'), may hold values from -0.015625 to 0.015625
- leaf_tables: bfloat16 [512, 2, 64, 2, 128], P('cuts', None, 'out'), may hold values from -4 to 4
- leaf_codes: int32 [128, 128], P('out'), may hold values from 0 to 4095
- branch_table: bfloat16 [384, 2, 128, 128], P('cuts'), may hold values from -0.375 to 0.375
- fetch_list: int32 [32, 32, 2], P('cuts'), may hold values from 0 to 11
- slice_terms: int32 [512, 2], P('cuts'), may hold values from 0 to 63
Outputs:
- amplitudes: float32 [128, 128, 2], P('out', 'cuts')
All inputs are finite; a program needn't handle non-finite values.
Results may differ from a plain program's by a relative error of at most 0.0029.
Values may be sent and summed in bfloat16 or wider, within the bound.
No kernel may reach another device: no remote copies, remote signals or barrier semaphores. Data moves between devices by JAX's collectives and lax.ppermute only.
A program may use at most 128 MiB of HBM per device.

v0:
```python
import jax
import jax.numpy as jnp
from jax import lax
from jax.sharding import PartitionSpec as P


def body(panels, leaf_tables, leaf_codes, branch_table, fetch_list, slice_terms):
    cut_count = lax.axis_size("cuts")
    owned_blocks = branch_table.shape[0]
    bond_width = branch_table.shape[2]
    capacity = fetch_list.shape[2]
    slot_count = cut_count * capacity
    owner_index = lax.broadcasted_iota(jnp.int32, (cut_count, capacity), 0)
    wanted_ids = (owner_index * owned_blocks + fetch_list[0]).reshape(slot_count)
    empty_slots = jnp.zeros((slot_count, 2, bond_width, bond_width), jnp.bfloat16)
    piece = lax.all_gather(branch_table, "cuts", axis=0, tiled=True)
    count = piece.shape[0]
    inside = (wanted_ids >= 0) & (wanted_ids < count)
    local_rows = jnp.clip(wanted_ids, 0, count - 1)
    taken = piece[local_rows]
    fetched = jnp.where(inside[:, None, None, None], taken, empty_slots)
    left_block = fetched[slice_terms[:, 0]]
    right_block = fetched[slice_terms[:, 1]]
    real_part = jnp.einsum(
        "sij,sjk->sik", left_block[:, 0], right_block[:, 0], preferred_element_type=jnp.float32
    ) - jnp.einsum(
        "sij,sjk->sik", left_block[:, 1], right_block[:, 1], preferred_element_type=jnp.float32
    )
    imag_part = jnp.einsum(
        "sij,sjk->sik", left_block[:, 0], right_block[:, 1], preferred_element_type=jnp.float32
    ) + jnp.einsum(
        "sij,sjk->sik", left_block[:, 1], right_block[:, 0], preferred_element_type=jnp.float32
    )
    real_part = real_part.astype(jnp.bfloat16)
    imag_part = imag_part.astype(jnp.bfloat16)
    upper = jnp.concatenate([real_part, imag_part], axis=2)
    lower = jnp.concatenate([-imag_part, real_part], axis=2)
    product_big = jnp.concatenate([upper, lower], axis=1)
    slice_count = product_big.shape[0]
    groups = slice_count // 4
    product_groups = product_big.reshape(groups, 4, 2 * bond_width, 2 * bond_width)
    all_leaves = lax.all_gather(leaf_tables, "out", axis=2, tiled=True)
    leaf_states = all_leaves.shape[2]
    leaf_groups = all_leaves.reshape(groups, 4, 2, leaf_states, 2 * bond_width)
    piece = lax.all_gather(panels, "cuts", axis=1, tiled=True)
    block_count = piece.shape[0]
    row_count = piece.shape[1]
    flat_rows = block_count * row_count
    panel_rows = piece.reshape(flat_rows, 2 * bond_width)
    codes_here = leaf_codes.reshape(flat_rows)
    states = lax.broadcasted_iota(jnp.int32, (1, leaf_states), 1)
    low_pick = ((codes_here % leaf_states)[:, None] == states).astype(jnp.bfloat16)
    high_pick = ((codes_here // leaf_states)[:, None] == states).astype(jnp.bfloat16)

    def one_group(running, inputs):
        product_here, table_here = inputs
        mixed = jnp.einsum(
            "ra,sab->srb", panel_rows, product_here, preferred_element_type=jnp.float32
        )
        low_rows = jnp.einsum(
            "rl,slx->srx", low_pick, table_here[:, 0], preferred_element_type=jnp.float32
        )
        high_rows = jnp.einsum(
            "rl,slx->srx", high_pick, table_here[:, 1], preferred_element_type=jnp.float32
        )
        low_re = low_rows[:, :, :bond_width]
        low_im = low_rows[:, :, bond_width:]
        high_re = high_rows[:, :, :bond_width]
        high_im = high_rows[:, :, bond_width:]
        weight_re = low_re * high_re - low_im * high_im
        weight_im = low_re * high_im + low_im * high_re
        mixed_re = mixed[:, :, :bond_width]
        mixed_im = mixed[:, :, bond_width:]
        sum_re = jnp.sum(mixed_re * weight_re - mixed_im * weight_im, axis=(0, 2))
        sum_im = jnp.sum(mixed_re * weight_im + mixed_im * weight_re, axis=(0, 2))
        return ((running[0] + sum_re, running[1] + sum_im), None)

    start_sums = (jnp.zeros((flat_rows,), jnp.float32), jnp.zeros((flat_rows,), jnp.float32))
    final_sums, _ = lax.scan(one_group, start_sums, (product_groups, leaf_groups))
    partial_amps = jnp.stack([final_sums[0], final_sums[1]], axis=-1).reshape(
        block_count, row_count, 2
    )
    return lax.psum_scatter(partial_amps, "cuts", scatter_dimension=1, tiled=True)


def solution(mesh):
    return jax.shard_map(
        body,
        mesh=mesh,
        in_specs=(
            P("out", "cuts", None, None),
            P("cuts", None, "out", None, None),
            P("out", None),
            P("cuts", None, None, None),
            P("cuts", None, None),
            P("cuts", None),
        ),
        out_specs=P("out", "cuts", None),
        check_vma=False,
    )
```

profile of v0, /device:TPU:1, one launch (start us, length us, event | category | flops | bytes accessed | tf_op | source)
XLA Modules:
  0.0 444.1 jit_solution(6290105099023783427)
XLA Ops:
  6.5 0.7 all-gather.8.cloned.1.call-update
  7.3 0.7 all-gather.6.cloned.1.call-update
  8.1 0.7 all-gather.4.cloned.1.call-update
  9.0 0.8 copy.17
  10.0 1.4 dynamic-slice
  12.1 0.8 fusion.25
  12.9 0.7 add_select_fusion
  13.6 52.0 %all-gather.8.cloned.1.call-done = bf16[16,2,64,2,128]{4,3,2,1,0:T(2,128)(2,1)} async-done(((bf16[16,2,8,2,128]{4,3,2,1,0:T(2,128)(2,1)}), bf16[16,2,64,2,128]{4,3,2,1,0:T(2,128)(2,1)}) %all-gather.8.cloned.1.call-update) | async-done | bytes 1048592 | tf_op jit(solution)/shard_map/all_gather | solution.py:42
  65.6 2.5 reshape.112
  68.1 62.3 %all-gather.6.cloned.1.call-done = bf16[16,128,2,128]{3,2,1,0:T(2,128)(2,1)} async-done(((bf16[16,4,2,128]{3,2,1,0:T(2,128)(2,1)}), bf16[16,128,2,128]{3,2,1,0:T(2,128)(2,1)}) %all-gather.6.cloned.1.call-update) | async-done | bytes 1048592 | tf_op jit(solution)/shard_map/all_gather | solution.py:45
  130.4 1.4 copy.33
  131.8 140.8 %all-gather.4.cloned.1.call-done = bf16[384,2,128,128]{3,2,1,0:T(8,128)(2,1)} async-done(((bf16[12,2,128,128]{3,2,1,0:T(8,128)(2,1)}), bf16[384,2,128,128]{3,2,1,0:T(8,128)(2,1)}) %all-gather.4.cloned.1.call-update) | async-done | bytes 25165840 | tf_op jit(solution)/shard_map/all_gather | solution.py:16
  272.6 11.2 %gather_fusion = bf16[64,2,128,128]{3,2,1,0:T(8,128)(2,1)} fusion(bf16[384,2,128,128]{3,2,1,0:T(8,128)(2,1)} %all-gather.4.cloned.1.call-done, s32[1024]{0:T(1024)S(1)} %pad_clamp_fusion.2), kind=kCustom, calls=%fused_computation | custom fusion | bytes 8388864 | tf_op jit(solution)/shard_map/gather | solution.py:20
  283.8 4.5 %broadcast_select_fusion = bf16[64,2,128,128]{3,2,1,0:T(8,128)(2,1)} fusion(bf16[64,2,128,128]{3,2,1,0:T(8,128)(2,1)} %gather_fusion, pred[64]{0:T(512)(128)(4,1)S(1)} %compare_and_fusion), kind=kLoop, calls=%fused_computation.30 | loop fusion | flops 2097152 | bytes 8388672 | tf_op jit(solution)/shard_map/jit(_where)/select_n | solution.py:21
  288.3 2.9 gather_fusion.2
  291.2 2.9 gather_fusion.1
  294.2 0.5 fusion.18
  294.7 0.5 fusion.19
  295.2 0.5 fusion.26
  295.7 0.5 fusion.16
  296.2 0.3 maximum_maximum_fusion
  296.5 36.2 %while.13 = (s32[]{:T(128)}, f32[2048]{0:T(1024)S(1)}, f32[2048]{0:T(1024)S(1)}, bf16[4,4,256,256]{2,3,1,0:T(8,128)(2,1)S(1)}, bf16[2048,256]{1,0:T(8,128)(2,1)S...) while((s32[]{:T(128)}, f32[2048]{0:T(1024)S(1)}, ...), condition=%wide.region_3.4_spmd.clone, body=%wide.region_0.3_spmd.clone.sunk | while | flops 1625821184 | bytes 69550704 | solution.py:79
  296.6 1.0 copy_bitcast_fusion.3
  297.5 1.3 convolution_bitcast_fusion.6
  298.8 1.3 convolution_bitcast_fusion.7
  300.1 2.6 multiply_add_fusion.2
  302.7 1.3 convolution_bitcast_fusion.8
  304.0 1.6 add_reduce_fusion.2
  305.6 1.0 copy_bitcast_fusion.3
  306.6 1.3 convolution_bitcast_fusion.6
  307.9 1.3 convolution_bitcast_fusion.7
  309.1 2.6 multiply_add_fusion.2
  311.7 1.3 convolution_bitcast_fusion.8
  313.0 1.6 add_reduce_fusion.2
  314.6 1.0 copy_bitcast_fusion.3
  315.6 1.3 convolution_bitcast_fusion.6
  316.9 1.3 convolution_bitcast_fusion.7
  318.2 2.6 multiply_add_fusion.2
  320.7 1.3 convolution_bitcast_fusion.8
  322.0 1.6 add_reduce_fusion.2
  323.7 1.0 copy_bitcast_fusion.3
  324.7 1.3 convolution_bitcast_fusion.6
  325.9 1.3 convolution_bitcast_fusion.7
  327.2 2.6 multiply_add_fusion.2
  329.8 1.3 convolution_bitcast_fusion.8
  331.1 1.6 add_reduce_fusion.2
  332.9 104.1 %all-reduce = f32[16,128,2]{0,2,1:T(2,128)S(1)} all-reduce(f32[16,128,2]{0,2,1:T(2,128)S(1)} %copy.24), channel_id=2, replica_groups=mesh['cuts'=32,'out'=8] {'cuts'}, use_global_device_ids=true, to_apply=%region_4.5.clone | all-reduce | flops 4096 | bytes 32768
  437.0 0.6 constant_dynamic-slice_fusion.1
  (21 shorter events, 0.8 us)
Async XLA Ops:
  6.5 59.0 %all-gather.8.cloned.1.call-start = ((), (), s32[]{:S(2)}) async-start(), calls=%async_computation.2 | async-start | bytes 1179648 | tf_op jit(solution)/shard_map/all_gather | solution.py:42
  7.3 123.1 %all-gather.6.cloned.1.call-start = ((), (), s32[]{:S(2)}) async-start(), calls=%async_computation.1 | async-start | bytes 1081344 | tf_op jit(solution)/shard_map/all_gather | solution.py:45
  8.0 264.6 %all-gather.4.cloned.1.call-start = ((), (), s32[]{:S(2)}) async-start(), calls=%async_computation | async-start | bytes 25952256 | tf_op jit(solution)/shard_map/all_gather | solution.py:16
Sparse Core Ops, SparseCore 0:
  9.8 55.6 all-gather.7
  67.3 63.0 all-gather.5
  132.3 140.2 all-gather.3
where the time goes:
time: 448 us; the launch traced here: 444 us
  waiting for transfers between devices  257 us (57%)
  blocking collectives  104 us (23%)
  local copies, waits for them, and re-layouts  28.2 us (6%)
  other arithmetic  23 us (5%)
  matrix products  17.4 us (4%)
  between operations  13.9 us (3%)
    all_gather x1, waiting for transfers between devices, body(): piece = lax.all_gather(branch_table, 'cuts', axis=0, tiled=True)  141 us
    unnamed x1, blocking collectives  104 us
    all_gather x1, waiting for transfers between devices, body(): piece = lax.all_gather(panels, 'cuts', axis=1, tiled=True)  62.3 us
    all_gather x1, waiting for transfers between devices, body(): all_leaves = lax.all_gather(leaf_tables, 'out', axis=2, tiled=True)  52 us
    gather x1, local copies, waits for them, and re-layouts, body(): taken = piece[local_rows]  11.2 us
    add x4, other arithmetic, one_group(): weight_im = low_re * high_im + low_im * high_re  10.3 us
  transfers between devices with their start and end apart: 3, of which 3 were waited for; matrix products, arithmetic and copies ran while one was open for 2% of the time, Pallas kernels for 0%

commit v1 on v0

v1 whole, which is shorter than its diff:
```python
import jax
import jax.numpy as jnp
from jax import lax
from jax.experimental import pallas as pl
from jax.experimental.pallas import tpu as pltpu
from jax.sharding import Mesh, PartitionSpec as P

BF = jnp.bfloat16
F32 = jnp.float32
CUTS = ("z", "yl", "core")
OUT = ("yh", "x")
SPLIT = 2
ROW_TILE = 512
VMEM = 48 * 1024 * 1024


def swap(a, axis):
    return lax.ppermute(a, axis, [(0, 1), (1, 0)])


def pack_kernel(ids, part, table, send):
    for q in range(send.shape[0] * send.shape[1]):
        send[q // 2, q % 2] = table[ids[q]]


def pack(ids, part, table, takers):
    blocks, _, width, _ = table.shape
    rows = width // 8
    return pl.pallas_call(
        pack_kernel,
        out_shape=jax.ShapeDtypeStruct((takers, 2, 2, rows, width), BF),
        grid_spec=pltpu.PrefetchScalarGridSpec(
            num_scalar_prefetch=2,
            grid=(1,),
            in_specs=[
                pl.BlockSpec((blocks, 2, rows, width), lambda i, ids, part: (0, 0, part[0], 0))
            ],
            out_specs=pl.BlockSpec(
                (takers, 2, 2, rows, width), lambda i, ids, part: (0, 0, 0, 0, 0)
            ),
        ),
        compiler_params=pltpu.CompilerParams(vmem_limit_bytes=VMEM),
        name="pack",
    )(ids, part, table)


def choose_kernel(terms, slots, send):
    peers, slices = send.shape[0], send.shape[1]
    for half in range(SPLIT):
        for s in range(slices):
            for t in range(2):
                block = slots[terms[(half * slices + s) * 2 + t]]
                for p in range(peers // SPLIT):
                    send[half * (peers // SPLIT) + p, s, t] = block


def choose(terms, slots, peers):
    count, _, rows, width = slots.shape
    slices = terms.shape[0] // 2 // SPLIT
    shape = (peers, slices, 2, 2, rows, width)
    return pl.pallas_call(
        choose_kernel,
        out_shape=jax.ShapeDtypeStruct(shape, BF),
        grid_spec=pltpu.PrefetchScalarGridSpec(
            num_scalar_prefetch=1,
            grid=(1,),
            in_specs=[pl.BlockSpec((count, 2, rows, width), lambda i, terms: (0, 0, 0, 0))],
            out_specs=pl.BlockSpec(shape, lambda i, terms: (0, 0, 0, 0, 0, 0)),
        ),
        compiler_params=pltpu.CompilerParams(vmem_limit_bytes=VMEM),
        name="choose",
    )(terms, slots)


def weight_kernel(low, high, leaf, weights):
    width = leaf.shape[3] // 2
    for s in range(leaf.shape[1]):
        table = leaf[:, s].reshape(leaf.shape[0] * leaf.shape[2], 2 * width)
        a = jnp.dot(low[...], table, preferred_element_type=F32)
        b = jnp.dot(high[...], table, preferred_element_type=F32)
        a_re, a_im, b_re, b_im = a[:, :width], a[:, width:], b[:, :width], b[:, width:]
        at = s * 2 * width
        weights[:, at : at + width] = (a_re * b_re - a_im * b_im).astype(BF)
        weights[:, at + width : at + 2 * width] = (a_re * b_im + a_im * b_re).astype(BF)


def weigh(low, high, leaf):
    rows, picks = low.shape
    depth = leaf.shape[1] * leaf.shape[3]
    return pl.pallas_call(
        weight_kernel,
        out_shape=jax.ShapeDtypeStruct((rows, depth), BF),
        grid=(rows // ROW_TILE,),
        in_specs=[
            pl.BlockSpec((ROW_TILE, picks), lambda i: (i, 0)),
            pl.BlockSpec((ROW_TILE, picks), lambda i: (i, 0)),
            pl.BlockSpec(leaf.shape, lambda i: (0, 0, 0, 0)),
        ],
        out_specs=pl.BlockSpec((ROW_TILE, depth), lambda i: (i, 0)),
        compiler_params=pltpu.CompilerParams(vmem_limit_bytes=VMEM),
        cost_estimate=pl.CostEstimate(
            flops=8 * rows * 256 * depth, bytes_accessed=2 * rows * depth, transcendentals=0
        ),
        name="weigh",
    )(low, high, leaf)


def amp_kernel(blocks, weights, panels, amps, product):
    parts, slices, _, _, rows, width = blocks.shape

    @pl.when(pl.program_id(0) == 0)
    def _():
        for s in range(slices):
            f = [
                [blocks[:, s, t, c].reshape(parts * rows, width) for c in range(2)]
                for t in range(2)
            ]
            left = jnp.concatenate(f[0], axis=1)
            right = jnp.concatenate(
                [
                    jnp.concatenate([f[1][0], f[1][1]], axis=1),
                    jnp.concatenate([-f[1][1], f[1][0]], axis=1),
                ],
                axis=0,
            )
            both = jnp.dot(left, right, preferred_element_type=F32).T
            re, im = both[:width].astype(BF), both[width:].astype(BF)
            at = s * 2 * width
            product[at : at + width, :width] = re
            product[at : at + width, width:] = im
            product[at + width : at + 2 * width, :width] = -im
            product[at + width : at + 2 * width, width:] = re

    y = jnp.dot(weights[...], product[...], preferred_element_type=F32)
    p_re = panels[:, :width].astype(F32)
    p_im = panels[:, width:].astype(F32)
    y_re, y_im = y[:, :width], y[:, width:]
    amps[0:1, :] = jnp.sum((p_re * y_re - p_im * y_im).T, axis=0, keepdims=True)
    amps[1:2, :] = jnp.sum((p_re * y_im + p_im * y_re).T, axis=0, keepdims=True)


def amplitudes_of(blocks, weights, panels):
    rows, depth = weights.shape
    width = blocks.shape[-1]
    return pl.pallas_call(
        amp_kernel,
        out_shape=jax.ShapeDtypeStruct((2, rows), F32),
        grid=(rows // ROW_TILE,),
        in_specs=[
            pl.BlockSpec(blocks.shape, lambda i: (0,) * 6),
            pl.BlockSpec((ROW_TILE, depth), lambda i: (i, 0)),
            pl.BlockSpec((ROW_TILE, 2 * width), lambda i: (i, 0)),
        ],
        out_specs=pl.BlockSpec((2, ROW_TILE), lambda i: (0, i)),
        scratch_shapes=[pltpu.VMEM((depth, 2 * width), BF)],
        compiler_params=pltpu.CompilerParams(vmem_limit_bytes=VMEM),
        name="amplitudes",
    )(blocks, weights, panels)


def body(panels, leaf_tables, leaf_codes, branch_table, fetch_list, slice_terms):
    cut_count = lax.axis_size(CUTS)
    peers = lax.axis_size(OUT)
    zs, yls = lax.axis_size("z"), lax.axis_size("yl")
    core, yl, yh = lax.axis_index("core"), lax.axis_index("yl"), lax.axis_index("yh")
    blocks, local_rows, _, width = panels.shape
    own = blocks * local_rows
    states = leaf_tables.shape[2]

    wanted = lax.all_to_all(fetch_list[0], CUTS, 0, 0, tiled=True).reshape(-1)
    part = lax.axis_index(OUT).astype(jnp.int32).reshape(1)
    sent = pack(wanted, part, branch_table, cut_count)
    slots = lax.all_to_all(sent, CUTS, 0, 0, tiled=True)
    slots = slots.reshape((2 * cut_count,) + slots.shape[2:])
    chosen = choose(slice_terms.reshape(-1), slots, peers)
    fetched = lax.all_to_all(chosen, OUT, 0, 0, tiled=True)

    slices = leaf_tables.shape[0] // SPLIT
    leaf = leaf_tables.reshape(SPLIT, 1, slices, 2 * states, 2 * width)
    leaf = jnp.broadcast_to(leaf, (SPLIT, peers // SPLIT) + leaf.shape[2:])
    leaf = leaf.reshape((peers,) + leaf.shape[2:])
    leaf = lax.all_to_all(leaf, OUT, 0, 0, tiled=True)

    rows_here = panels.transpose(1, 0, 2, 3).reshape(own, 2 * width)
    rows_here = jnp.stack([rows_here, swap(rows_here, "yh")])
    other = swap(rows_here, "yl")
    rows_here = jnp.where(
        yl == 0, jnp.stack([rows_here, other]), jnp.stack([other, rows_here])
    )
    rows_here = lax.all_gather(rows_here, "z", axis=0, tiled=True)
    rows_here = rows_here.reshape(-1, 2 * width)
    rows_all = jnp.concatenate([rows_here, swap(rows_here, "core")], axis=0)

    codes = leaf_codes.reshape(blocks, zs, yls, 2, local_rows).transpose(3, 1, 2, 4, 0)
    codes = codes.reshape(2, zs, yls, 1, own)
    codes = jnp.concatenate([codes, swap(codes, "yh")], axis=3)
    codes = jnp.where(core == 0, codes, codes[::-1]).reshape(-1, 1)
    leaf_states = states * peers
    low, high = codes % leaf_states, codes // leaf_states
    low = (low // states) * (2 * states) + low % states
    high = (high // states) * (2 * states) + states + high % states
    column = lax.broadcasted_iota(jnp.int32, (1, 2 * leaf_states), 1)
    low = (low == column).astype(BF)
    high = (high == column).astype(BF)
    weights = weigh(low, high, leaf)

    amps = amplitudes_of(fetched, weights, rows_all)
    amps = amps.reshape(2, 2, zs * yls, 2, own)
    amps = amps[:, 0] + swap(amps[:, 1], "core")
    amps = amps.transpose(1, 2, 0, 3)
    amps = jnp.where(yh == 0, amps, amps[:, ::-1])
    amps = lax.all_to_all(
        amps.reshape(zs * yls * 2, 2 * own), ("z", "yl", "yh"), 0, 0, tiled=True
    )
    amps = jnp.sum(amps, axis=0).reshape(2, local_rows, blocks)
    return amps.transpose(2, 1, 0)


def solution(mesh):
    fine = Mesh(mesh.devices.reshape(8, 2, 2, 2, 4), CUTS + OUT)
    return jax.shard_map(
        body,
        mesh=fine,
        in_specs=(
            P(OUT, CUTS, None, None),
            P(CUTS, None, OUT, None, None),
            P(OUT, None),
            P(CUTS, None, None, None),
            P(CUTS, None, None),
            P(CUTS, None),
        ),
        out_specs=P(OUT, CUTS, None),
        check_vma=False,
    )
```

time: 448 us -> 143 us (0.32)
  waiting for transfers between devices: 257 us -> 34.8 us
  blocking collectives: 104 us -> 12.7 us
  starting transfers between devices: 0.08 us -> 42.7 us
  Pallas kernels: 0 us -> 26 us
  local copies, waits for them, and re-layouts: 28.2 us -> 7.55 us
  other arithmetic: 23 us -> 5.28 us
  matrix products: 17.4 us -> 0 us
    all_gather x3 -> x1, waiting for transfers between devices: 255 us -> 8.84 us  [body(): rows_here = lax.all_gather(rows_here, 'z', axis=0, tiled=True)]
    unnamed x1 -> x0, blocking collectives: 104 us -> none
    all_to_all x0 -> x4, starting transfers between devices: none -> 28 us  [the longest x1 10.7 us: body(): wanted = lax.all_to_all(fetch_list[0], CUTS, 0, 0, tiled=True).reshape(-1)]
    pallas_call x0 -> x4, Pallas kernels: none -> 26 us  [the longest x1 11.6 us: weigh(): pl.pallas_call(weight_kernel, out_shape=jax.ShapeDtypeStruct((rows, depth...]
    all_to_all x0 -> x4, waiting for transfers between devices: none -> 22.3 us  [the longest x1 11.3 us: body(): slots = lax.all_to_all(sent, CUTS, 0, 0, tiled=True)]
    dot_general x16 -> x0, matrix products: 17.4 us -> none  [the longest x4 5.15 us: one_group(): jnp.einsum('ra,sab->srb', panel_rows, product_here, preferred_element_typ...]
    gather x3 -> x0, local copies, waits for them, and re-layouts: 17.1 us -> none  [the longest x1 11.2 us: body(): taken = piece[local_rows]]
    ppermute x0 -> x5, starting transfers between devices: none -> 14.6 us  [swap(): return lax.ppermute(a, axis, [(0, 1), (1, 0)])]
  transfers between devices with their start and end apart: 3 -> 10, of which waited for: 3 -> 7; matrix products, arithmetic and copies ran while one was open for 2% -> 6% of each run, Pallas kernels for 0% -> 10%
where the time goes in v1:
time: 143 us
  starting transfers between devices  42.7 us (30%)
  waiting for transfers between devices  34.8 us (24%)
  Pallas kernels  26 us (18%)
  between operations  13.6 us (10%)
  blocking collectives  12.7 us (9%)
  local copies, waits for them, and re-layouts  7.55 us (5%)
  other arithmetic  5.28 us (4%)
    ppermute x5, starting transfers between devices, swap(): return lax.ppermute(a, axis, [(0, 1), (1, 0)])  14.6 us
    all_to_all x1, blocking collectives, body(): lax.all_to_all(amps.reshape(zs * yls * 2, 2 * own), ('z', 'yl', 'yh'), 0,...  12.7 us
    pallas_call x1, Pallas kernels, weigh(): pl.pallas_call(weight_kernel, out_shape=jax.ShapeDtypeStruct((rows, depth...  11.6 us
    pallas_call x1, Pallas kernels, amplitudes_of(): pl.pallas_call(amp_kernel, out_shape=jax.ShapeDtypeStruct((2, rows), F32)...  11.4 us
    all_to_all x1, waiting for transfers between devices, body(): slots = lax.all_to_all(sent, CUTS, 0, 0, tiled=True)  11.3 us
    all_to_all x1, starting transfers between devices, body(): wanted = lax.all_to_all(fetch_list[0], CUTS, 0, 0, tiled=True).reshape(-1)  10.7 us
    all_gather x1, waiting for transfers between devices, body(): rows_here = lax.all_gather(rows_here, 'z', axis=0, tiled=True)  8.84 us
    all_to_all x1, waiting for transfers between devices, body(): wanted = lax.all_to_all(fetch_list[0], CUTS, 0, 0, tiled=True).reshape(-1)  7.85 us
  transfers between devices with their start and end apart: 10, of which 7 were waited for; matrix products, arithmetic and copies ran while one was open for 6% of the time, Pallas kernels for 10%

profile of v1, /device:TPU:1, one launch (start us, length us, event | category | flops | bytes accessed | tf_op | source)
XLA Modules:
  0.0 142.6 jit_solution(7293690006043719771)
XLA Ops:
  6.5 0.8 copy.35
  7.4 3.8 %collective-permute-start.1 = (bf16[64,256]{1,0:T(8,128)(2,1)S(1)}, bf16[64,256]{1,0:T(8,128)(2,1)S(1)}, u32[]{:S(2)}, u32[]{:S(2)}) collective-permute-start(bf16[64,256]{1,0:T(8,128)(2,1)S(1)} %bitcast.42), channel_id=1, source_target_pairs={{0,4},{4,0},{1,5},{5,1},{2,6},{6,2},{3,7},{7,3},{8,12},{12,8},{9,1... | collective-permute-start | bytes 98312 | tf_op jit(solution)/shard_map/ppermute | solution.py:18
  11.2 1.3 collective-permute-done.1
  12.5 1.4 %collective-permute-start.2 = (bf16[2,64,256]{2,1,0:T(8,128)(2,1)S(1)}, bf16[2,64,256]{2,1,0:T(8,128)(2,1)S(1)}, u32[]{:S(2)}, u32[]{:S(2)}) collective-permute-start(bf16[2,64,256]{2,1,0:T(8,128)(2,1)S(1)} %get-tuple-element.8), channel_id=1, source_target_pairs={{0,16},{16,0},{1,17},{17,1},{2,18},{18,2},{3,19},{19,3},{4,20},{20... | collective-permute-start | bytes 196616 | tf_op jit(solution)/shard_map/ppermute | solution.py:18
  14.0 1.4 copy.31
  15.3 10.7 %all-to-all-start = ((s32[32,1,2]{2,1,0:T(1,128)}), s32[32,1,2]{2,1,0:T(1,128)S(1)}, u32[]{:S(2)}, u32[]{:S(2)}) async-start(s32[32,1,2]{2,1,0:T(1,128)} %copy.31), calls=%async_computation | async-start | bytes 32768 | tf_op jit(solution)/shard_map/all_to_all | solution.py:170
  26.1 7.8 %all-to-all-done = s32[32,1,2]{2,1,0:T(1,128)S(1)} async-done(((s32[32,1,2]{2,1,0:T(1,128)}), s32[32,1,2]{2,1,0:T(1,128)S(1)}, u32[]{:S(2)}, u32[]{:S(2)}) %all-to-all-start) | async-done | bytes 288 | tf_op jit(solution)/shard_map/all_to_all | solution.py:170
  33.9 0.5 broadcast.219
  34.4 0.7 reduce.4
  35.1 0.1 reshape.244.ids
  35.2 0.0 copy-start.1
  35.2 1.1 copy-done.1
  36.4 1.4 pack.1
  37.8 4.2 %all-to-all-start.1 = ((bf16[32,2,2,16,128]{4,3,2,1,0:T(8,128)(2,1)}), bf16[32,2,2,16,128]{4,3,2,1,0:T(8,128)(2,1)S(1)}, u32[]{:S(2)}, u32[]{:S(2)}) async-start(bf16[32,2,2,16,128]{4,3,2,1,0:T(8,128)(2,1)} %pack.1), calls=%async_computation.1 | async-start | bytes 1048576 | tf_op jit(solution)/shard_map/all_to_all | solution.py:173
  41.9 0.0 all-gather.2.cloned.1.call-start
  42.0 0.0 collective-permute-done.2
  42.0 0.7 maximum_select_fusion
  42.7 0.0 all-gather.2.cloned.1.call-update
  42.7 0.1 copy.32
  42.8 0.1 reshape.255
  42.9 2.9 %collective-permute-start = (s32[2,8,2,1,64]{4,1,2,0,3:T(8,128)S(1)}, s32[2,8,2,1,64]{4,1,2,0,3:T(8,128)S(1)}, u32[]{:S(2)}, u32[]{:S(2)}) collective-permute-start(s32[2,8,2,1,64]{4,1,2,0,3:T(8,128)S(1)} %get-tuple-element.11), channel_id=1, source_target_pairs={{0,4},{4,0},{1,5},{5,1},{2,6},{6,2},{3,7},{7,3},{8,12},{12,8},{9,1... | collective-permute-start | bytes 24584 | tf_op jit(solution)/shard_map/ppermute | solution.py:18
  45.8 0.1 broadcast_in_dim.7
  45.9 0.1 copy.30
  46.0 0.1 reshape.243.terms
  46.1 1.5 %collective-permute-done = s32[2,8,2,1,64]{4,1,2,0,3:T(8,128)S(1)} collective-permute-done((s32[2,8,2,1,64]{4,1,2,0,3:T(8,128)S(1)}, s32[2,8,2,1,64]{4,1,2,0,3:T(8,128)S(1)}, u32[]{:S(2)}, u32[]{:S(2)}) %collective-permute-start) | collective-permute-done | bytes 8224 | tf_op jit(solution)/shard_map/ppermute | solution.py:18
  47.6 0.1 reshape.249
  47.7 0.1 fusion.8
  47.7 11.3 %all-to-all-done.1 = bf16[32,2,2,16,128]{4,3,2,1,0:T(8,128)(2,1)S(1)} async-done(((bf16[32,2,2,16,128]{4,3,2,1,0:T(8,128)(2,1)}), bf16[32,2,2,16,128]{4,3,2,1,0:T(8,128)(2,1)S(1)}, u32[]{:S(2)}, u32[]{:S(2)}) %all-to-all-start.1) | async-done | bytes 524320 | tf_op jit(solution)/shard_map/all_to_all | solution.py:173
  59.0 0.8 broadcast_in_dim.8
  59.9 6.5 %all-to-all-start.3 = ((bf16[8,8,16,256]{3,2,1,0:T(8,128)(2,1)}), bf16[8,8,16,256]{3,2,1,0:T(8,128)(2,1)S(1)}, u32[]{:S(2)}, u32[]{:S(2)}) async-start(bf16[8,8,16,256]{3,2,1,0:T(8,128)(2,1)} %bitcast.6), calls=%async_computation.3 | async-start | bytes 1048576 | tf_op jit(solution)/shard_map/all_to_all | solution.py:182
  66.4 2.4 %fusion = (bf16[4096,128]{1,0:T(8,128)(2,1)S(1)}, bf16[4096,128]{1,0:T(8,128)(2,1)}) fusion(s32[4096]{0:T(1024)S(1)} %get-tuple-element.10, s32[4096]{0:T(1024)S(1)} %get-tuple-element.9), kind=kLoop, calls=%fused_computation.3 | loop fusion | flops 2097152 | bytes 2129920 | tf_op jit(solution)/shard_map/convert_element_type | solution.py:203
  68.8 1.6 %choose.1 = bf16[8,8,2,2,16,128]{5,4,3,2,1,0:T(8,128)(2,1)} custom-call(s32[32]{0:T(128)S(1)} %reshape.243.terms, bf16[64,2,16,128]{3,2,1,0:T(8,128)(2,1)S(1)} %bitcast.33), custom_call_target="tpu_custom_call" | custom-call | tf_op jit(solution)/shard_map/choose/pallas_call | solution.py:61
  70.4 8.8 %all-gather.2.cloned.1.call-done = bf16[16,2,64,256]{3,2,1,0:T(8,128)(2,1)} async-done(((bf16[2,2,64,256]{3,2,1,0:T(8,128)(2,1)}), bf16[16,2,64,256]{3,2,1,0:T(8,128)(2,1)}) %all-gather.2.cloned.1.call-update) | async-done | bytes 1048592 | tf_op jit(solution)/shard_map/all_gather | solution.py:190
  79.3 5.6 %collective-permute-start.3 = (bf16[2048,256]{1,0:T(8,128)(2,1)}, bf16[2048,256]{1,0:T(8,128)(2,1)}, u32[]{:S(2)}, u32[]{:S(2)}) collective-permute-start(bf16[2048,256]{1,0:T(8,128)(2,1)} %bitcast.34), channel_id=1, source_target_pairs={{0,8},{8,0},{1,9},{9,1},{2,10},{10,2},{3,11},{11,3},{4,12},{12,4},... | collective-permute-start | bytes 3145736 | tf_op jit(solution)/shard_map/ppermute | solution.py:18
  84.9 6.6 %all-to-all-start.2 = ((bf16[8,8,2,2,16,128]{5,4,3,2,1,0:T(8,128)(2,1)}), bf16[8,8,2,2,16,128]{5,4,3,2,1,0:T(8,128)(2,1)S(1)}, u32[]{:S(2)}, u32[]{:S(2)}) async-start(bf16[8,8,2,2,16,128]{5,4,3,2,1,0:T(8,128)(2,1)} %choose.1), calls=%async_computation.2 | async-start | bytes 2097152 | tf_op jit(solution)/shard_map/all_to_all | solution.py:176
  91.5 1.2 copy-done
  92.7 11.6 %weigh.1.weights = bf16[4096,2048]{1,0:T(8,128)(2,1)} custom-call(bf16[4096,128]{1,0:T(8,128)(2,1)S(1)} %get-tuple-element.13.low, bf16[4096,128]{1,0:T(8,128)(2,1)S(1)} %copy-done, bf16[8,8,16,256]{3,2,1,0:T(8,128)(2,1)S(1)} %all-to-all-done.3.leaf), custom_call_target="tpu_custom_call" | custom-call | flops 17179869184 | bytes 16777216 | tf_op jit(solution)/shard_map/weigh/pallas_call | solution.py:90
  104.3 1.4 pad_maximum_fusion.panels
  105.7 3.2 %all-to-all-done.2.blocks = bf16[8,8,2,2,16,128]{5,4,3,2,1,0:T(8,128)(2,1)S(1)} async-done(((bf16[8,8,2,2,16,128]{5,4,3,2,1,0:T(8,128)(2,1)}), bf16[8,8,2,2,16,128]{5,4,3,2,1,0:T(8,128)(2,1)S(1)}, u32[]{:S(2)}, u32[]{:S(2)}) %all-to-all-start.2) | async-done | bytes 1048608 | tf_op jit(solution)/shard_map/all_to_all | solution.py:176
  108.9 11.4 %amplitudes.1 = f32[2,4096]{1,0:T(2,128)S(1)} custom-call(bf16[8,8,2,2,16,128]{5,4,3,2,1,0:T(8,128)(2,1)S(1)} %all-to-all-done.2.blocks, bf16[4096,2048]{1,0:T(8,128)(2,1)} %weigh.1.weights, bf16[4096,256]{1,0:T(8,128)(2,1)S(1)} %pad_maximum_fusion.panels), custom_call_target="tpu_custom_call" | custom-call | tf_op jit(solution)/shard_map/amplitudes/pallas_call | solution.py:145
  120.2 0.1 reshape.253
  120.4 0.8 collective-permute-start.4
  121.2 0.9 collective-permute-done.4
  122.2 0.1 all_to_all.26
  122.3 12.7 %all_to_all.33 = f32[32,1,128]{2,1,0:T(1,128)S(1)} all-to-all(f32[32,1,128]{2,1,0:T(1,128)S(1)} %bitcast.38), channel_id=1, replica_groups=mesh['z'=8,'yl'=2,'core'=2,'yh'=2,'x'=4] {'z','yl','yh'}, dimensions={0} | all-to-all | bytes 32768 | tf_op jit(solution)/shard_map/all_to_all | solution.py:212
  135.0 0.1 reduce_sum.9
  135.1 0.1 reshape.254
  135.1 0.6 copy.40
  (22 shorter events, 0.2 us)
Async XLA Ops:
  6.5 36.2 %copy-start.4 = (s32[16,128]{1,0:T(8,128)S(1)}, s32[16,128]{1,0:T(8,128)}, u32[]{:S(2)}) copy-start(s32[16,128]{1,0:T(8,128)} %param.8) | copy-start | bytes 24580
  6.5 39.3 %copy-start.3 = (bf16[16,2,8,2,128]{4,3,2,1,0:T(2,128)(2,1)S(1)}, bf16[16,2,8,2,128]{4,3,2,1,0:T(2,128)(2,1)}, u32[]{:S(2)}) copy-start(bf16[16,2,8,2,128]{4,3,2,1,0:T(2,128)(2,1)} %param.7) | copy-start | bytes 393220
  6.5 39.4 %copy-start.5 = (s32[16,2]{0,1:T(2,128)S(1)}, s32[16,2]{0,1:T(2,128)}, u32[]{:S(2)}) copy-start(s32[16,2]{0,1:T(2,128)} %param.11) | copy-start | bytes 388
  7.4 5.1 %collective-permute-start.1 = (bf16[64,256]{1,0:T(8,128)(2,1)S(1)}, bf16[64,256]{1,0:T(8,128)(2,1)S(1)}, u32[]{:S(2)}, u32[]{:S(2)}) collective-permute-start(bf16[64,256]{1,0:T(8,128)(2,1)S(1)} %bitcast.42), channel_id=1, source_target_pairs={{0,4},{4,0},{1,5},{5,1},{2,6},{6,2},{3,7},{7,3},{8,12},{12,8},{9,1... | collective-permute-start | bytes 98312 | tf_op jit(solution)/shard_map/ppermute | solution.py:18
  12.5 29.5 %collective-permute-start.2 = (bf16[2,64,256]{2,1,0:T(8,128)(2,1)S(1)}, bf16[2,64,256]{2,1,0:T(8,128)(2,1)S(1)}, u32[]{:S(2)}, u32[]{:S(2)}) collective-permute-start(bf16[2,64,256]{2,1,0:T(8,128)(2,1)S(1)} %get-tuple-element.8), channel_id=1, source_target_pairs={{0,16},{16,0},{1,17},{17,1},{2,18},{18,2},{3,19},{19,3},{4,20},{20... | collective-permute-start | bytes 196616 | tf_op jit(solution)/shard_map/ppermute | solution.py:18
  15.3 18.6 %all-to-all-start = ((s32[32,1,2]{2,1,0:T(1,128)}), s32[32,1,2]{2,1,0:T(1,128)S(1)}, u32[]{:S(2)}, u32[]{:S(2)}) async-start(s32[32,1,2]{2,1,0:T(1,128)} %copy.31), calls=%async_computation | async-start | bytes 32768 | tf_op jit(solution)/shard_map/all_to_all | solution.py:170
  35.2 1.1 copy-start.1
  37.8 21.2 %all-to-all-start.1 = ((bf16[32,2,2,16,128]{4,3,2,1,0:T(8,128)(2,1)}), bf16[32,2,2,16,128]{4,3,2,1,0:T(8,128)(2,1)S(1)}, u32[]{:S(2)}, u32[]{:S(2)}) async-start(bf16[32,2,2,16,128]{4,3,2,1,0:T(8,128)(2,1)} %pack.1), calls=%async_computation.1 | async-start | bytes 1048576 | tf_op jit(solution)/shard_map/all_to_all | solution.py:173
  41.9 37.3 %all-gather.2.cloned.1.call-start = ((), (), s32[]{:S(2)}) async-start(), calls=%async_computation.5 | async-start | bytes 1179648 | tf_op jit(solution)/shard_map/all_gather | solution.py:190
  42.9 4.6 %collective-permute-start = (s32[2,8,2,1,64]{4,1,2,0,3:T(8,128)S(1)}, s32[2,8,2,1,64]{4,1,2,0,3:T(8,128)S(1)}, u32[]{:S(2)}, u32[]{:S(2)}) collective-permute-start(s32[2,8,2,1,64]{4,1,2,0,3:T(8,128)S(1)} %get-tuple-element.11), channel_id=1, source_target_pairs={{0,4},{4,0},{1,5},{5,1},{2,6},{6,2},{3,7},{7,3},{8,12},{12,8},{9,1... | collective-permute-start | bytes 24584 | tf_op jit(solution)/shard_map/ppermute | solution.py:18
  59.9 25.0 %all-to-all-start.3 = ((bf16[8,8,16,256]{3,2,1,0:T(8,128)(2,1)}), bf16[8,8,16,256]{3,2,1,0:T(8,128)(2,1)S(1)}, u32[]{:S(2)}, u32[]{:S(2)}) async-start(bf16[8,8,16,256]{3,2,1,0:T(8,128)(2,1)} %bitcast.6), calls=%async_computation.3 | async-start | bytes 1048576 | tf_op jit(solution)/shard_map/all_to_all | solution.py:182
  79.3 25.0 %collective-permute-start.3 = (bf16[2048,256]{1,0:T(8,128)(2,1)}, bf16[2048,256]{1,0:T(8,128)(2,1)}, u32[]{:S(2)}, u32[]{:S(2)}) collective-permute-start(bf16[2048,256]{1,0:T(8,128)(2,1)} %bitcast.34), channel_id=1, source_target_pairs={{0,8},{8,0},{1,9},{9,1},{2,10},{10,2},{3,11},{11,3},{4,12},{12,4},... | collective-permute-start | bytes 3145736 | tf_op jit(solution)/shard_map/ppermute | solution.py:18
  84.9 24.0 %all-to-all-start.2 = ((bf16[8,8,2,2,16,128]{5,4,3,2,1,0:T(8,128)(2,1)}), bf16[8,8,2,2,16,128]{5,4,3,2,1,0:T(8,128)(2,1)S(1)}, u32[]{:S(2)}, u32[]{:S(2)}) async-start(bf16[8,8,2,2,16,128]{5,4,3,2,1,0:T(8,128)(2,1)} %choose.1), calls=%async_computation.2 | async-start | bytes 2097152 | tf_op jit(solution)/shard_map/all_to_all | solution.py:176
  91.5 1.2 copy-start
  92.7 11.6 %copy-start.2 = (bf16[16,2,64,256]{3,2,1,0:T(8,128)(2,1)S(1)}, bf16[16,2,64,256]{3,2,1,0:T(8,128)(2,1)}, u32[]{:S(2)}) copy-start(bf16[16,2,64,256]{3,2,1,0:T(8,128)(2,1)} %all-gather.2.cloned.1.call-done) | copy-start | bytes 3145732
  120.4 1.7 %collective-permute-start.4 = (f32[2,16,2,64]{3,0,2,1:T(2,128)S(1)}, f32[2,16,2,64]{3,0,2,1:T(2,128)S(1)}, u32[]{:S(2)}, u32[]{:S(2)}) collective-permute-start(f32[2,16,2,64]{3,0,2,1:T(2,128)S(1)} %bitcast.41), channel_id=1, source_target_pairs={{0,8},{8,0},{1,9},{9,1},{2,10},{10,2},{3,11},{11,3},{4,12},{12,4},... | collective-permute-start | bytes 49160 | tf_op jit(solution)/shard_map/ppermute | solution.py:18
Sparse Core Ops, SparseCore 0:
  44.6 34.6 all-gather.1

commit v2 on v1

v2 whole, which is shorter than its diff:
```python
import jax
import jax.numpy as jnp
from jax import lax
from jax.experimental import pallas as pl
from jax.experimental.pallas import tpu as pltpu
from jax.sharding import Mesh, PartitionSpec as P

BF = jnp.bfloat16
F32 = jnp.float32
CUTS = ("z4", "z2", "z1", "yl", "core")
OUT = ("yh", "x")
PARTS = 8
SPLIT = 2
ROW_TILE = 1024
WEIGHT_TILE = 2048
VMEM = 20 * 1024 * 1024
IN_VMEM = pl.BlockSpec(memory_space=pltpu.VMEM)


def swap(a, axis, bit=1):
    count = lax.axis_size(axis)
    return lax.ppermute(a, axis, [(i, i ^ bit) for i in range(count)])


def pack_kernel(me, part, wanted, table, codes, send, ordered):
    takers, capacity = send.shape[0], send.shape[1]
    for d in range(takers):
        ordered[d : d + 1, :] = codes[pl.ds(d ^ me[1], 1), :]
    for d in range(takers):
        for c in range(capacity):
            send[d, c] = table[wanted[d, c, me[0]]]


def pack(me, part, wanted, table, codes):
    blocks, _, width, _ = table.shape
    rows = width // PARTS
    takers, capacity, _ = wanted.shape
    shape = (takers, capacity, 2, rows, width)
    return pl.pallas_call(
        pack_kernel,
        out_shape=(
            jax.ShapeDtypeStruct(shape, BF),
            jax.ShapeDtypeStruct(codes.shape, codes.dtype),
        ),
        grid_spec=pltpu.PrefetchScalarGridSpec(
            num_scalar_prefetch=2,
            grid=(1,),
            in_specs=[
                pl.BlockSpec(memory_space=pltpu.SMEM),
                pl.BlockSpec((blocks, 2, rows, width), lambda i, me, part: (0, 0, part[0], 0)),
                pl.BlockSpec(codes.shape, lambda i, me, part: (0, 0)),
            ],
            out_specs=(
                pl.BlockSpec(shape, lambda i, me, part: (0, 0, 0, 0, 0)),
                pl.BlockSpec(codes.shape, lambda i, me, part: (0, 0)),
            ),
        ),
        compiler_params=pltpu.CompilerParams(vmem_limit_bytes=VMEM),
        name="pack",
    )(me, part, wanted, pltpu.with_memory_space_constraint(table, pltpu.HBM), codes)


def choose_kernel(terms, half, slots, first_rows, second_rows, *refs):
    kept, given, rows = refs[-3:]
    slices = kept.shape[0]
    for out, first in ((kept, half[0] * slices), (given, (1 - half[0]) * slices)):
        for s in range(slices):
            for t in range(2):
                out[s, t] = slots[terms[(first + s) * 2 + t]]
    count = first_rows.shape[0]
    rows[:count] = first_rows[...]
    rows[count:] = second_rows[...]


def choose(terms, half, slots, first_rows, second_rows, ready):
    shape = (terms.shape[0] // 2 // SPLIT, 2) + slots.shape[1:]
    count, pair = first_rows.shape
    scalars = [pl.BlockSpec(memory_space=pltpu.SMEM)] * 2
    return pl.pallas_call(
        choose_kernel,
        out_shape=(jax.ShapeDtypeStruct(shape, BF),) * 2
        + (jax.ShapeDtypeStruct((2 * count, pair), BF),),
        in_specs=scalars + [IN_VMEM] * 3 + [pl.BlockSpec(memory_space=pl.ANY)] * len(ready),
        out_specs=(IN_VMEM,) * 3,
        compiler_params=pltpu.CompilerParams(vmem_limit_bytes=VMEM),
        name="choose",
    )(terms, half, slots, first_rows, second_rows, *ready)


def weight_kernel(low, high, *refs):
    leaf, weights = refs[:-2], refs[-1]
    halves, slices, _, pair = leaf[0].shape
    width = pair // 2

    def tile(i, carry):
        here = pl.ds(pl.multiple_of(i * WEIGHT_TILE, WEIGHT_TILE), WEIGHT_TILE)
        pick_low, pick_high = low[here, :], high[here, :]
        for s in range(slices):
            table = jnp.concatenate([piece[h, s] for h in range(halves) for piece in leaf], axis=0)
            a = jnp.dot(pick_low, table, preferred_element_type=F32)
            b = jnp.dot(pick_high, table, preferred_element_type=F32)
            a_re, a_im, b_re, b_im = a[:, :width], a[:, width:], b[:, :width], b[:, width:]
            at = s * pair
            weights[here, at : at + width] = (a_re * b_re - a_im * b_im).astype(BF)
            weights[here, at + width : at + pair] = (a_re * b_im + a_im * b_re).astype(BF)
        return carry

    lax.fori_loop(0, low.shape[0] // WEIGHT_TILE, tile, 0)


def weigh(low, high, leaf, chosen):
    rows = low.shape[0]
    depth = leaf[0].shape[1] * leaf[0].shape[3]
    return pl.pallas_call(
        weight_kernel,
        out_shape=pltpu.VMEM((rows, depth), BF),
        in_specs=[IN_VMEM] * (2 + len(leaf)) + [pl.BlockSpec(memory_space=pl.ANY)],
        out_specs=IN_VMEM,
        compiler_params=pltpu.CompilerParams(vmem_limit_bytes=VMEM),
        cost_estimate=pl.CostEstimate(
            flops=8 * rows * 256 * depth, bytes_accessed=2 * rows * depth, transcendentals=0
        ),
        name="weigh",
    )(low, high, *leaf, chosen)


def amp_kernel(me, weights, *refs):
    parts = PARTS
    pieces, refs = refs[:parts], refs[parts:]
    panels, (mine, theirs, blocks, product) = refs[:-4], refs[-4:]
    _, slices, _, _, rows, width = blocks.shape
    for r in range(parts):
        blocks[r ^ me[1]] = pieces[r][...]
    for s in range(slices):
        f = [
            [blocks[:, s, t, c].reshape(parts * rows, width) for c in range(2)] for t in range(2)
        ]
        left = jnp.concatenate(f[0], axis=1)
        right = jnp.concatenate(
            [
                jnp.concatenate([f[1][0], f[1][1]], axis=1),
                jnp.concatenate([-f[1][1], f[1][0]], axis=1),
            ],
            axis=0,
        )
        both = jnp.dot(left, right, preferred_element_type=F32).T
        re, im = both[:width].astype(BF), both[width:].astype(BF)
        at = s * 2 * width
        product[at : at + width, :width] = re
        product[at : at + width, width:] = im
        product[at + width : at + 2 * width, :width] = -im
        product[at + width : at + 2 * width, width:] = re

    lines, each = mine.shape[0], mine.shape[1] // 2
    group = panels[0].shape[0]
    for i in range(weights.shape[0] // ROW_TILE):
        here = slice(i * ROW_TILE, (i + 1) * ROW_TILE)
        y = jnp.dot(weights[here, :], product[...], preferred_element_type=F32)
        there = slice(here.start % group, here.start % group + ROW_TILE)
        p_re = panels[here.start // group][there, :width].astype(F32)
        p_im = panels[here.start // group][there, width:].astype(F32)
        y_re, y_im = y[:, :width], y[:, width:]
        re = jnp.sum((p_re * y_re - p_im * y_im).T, axis=0, keepdims=True)
        im = jnp.sum((p_re * y_im + p_im * y_re).T, axis=0, keepdims=True)
        for k in range(ROW_TILE // each):
            line = here.start // each + k
            amps = theirs if line // lines else mine
            to = pl.ds((line % lines) ^ me[0], 1)
            amps[to, :each] = re[:, k * each : (k + 1) * each]
            amps[to, each:] = im[:, k * each : (k + 1) * each]


def amplitudes_of(me, weights, pieces, panels, each):
    rows, depth = weights.shape
    width = pieces[0].shape[-1]
    return pl.pallas_call(
        amp_kernel,
        out_shape=(jax.ShapeDtypeStruct((rows // each // 2, 2 * each), F32),) * 2,
        in_specs=[pl.BlockSpec(memory_space=pltpu.SMEM)]
        + [IN_VMEM] * (1 + len(pieces) + len(panels)),
        out_specs=(IN_VMEM,) * 2,
        scratch_shapes=[
            pltpu.VMEM((len(pieces),) + pieces[0].shape, BF),
            pltpu.VMEM((depth, 2 * width), BF),
        ],
        compiler_params=pltpu.CompilerParams(vmem_limit_bytes=VMEM),
        name="amplitudes",
    )(me, pltpu.with_memory_space_constraint(weights, pltpu.VMEM), *pieces, *panels)


def body(panels, leaf_tables, leaf_codes, branch_table, fetch_list, slice_terms):
    cut_count = lax.axis_size(CUTS)
    peers = lax.axis_size(OUT)
    yh = lax.axis_index("yh").astype(jnp.int32)
    part = lax.axis_index(OUT).astype(jnp.int32)
    blocks, local_rows, _, width = panels.shape
    own = blocks * local_rows
    states = leaf_tables.shape[2]
    order = ("z1", "yh", "yl", "z4", "z2")

    wanted = fetch_list.transpose(0, 2, 1)
    wanted = jnp.broadcast_to(wanted, (cut_count,) + wanted.shape[1:])
    wanted = lax.all_to_all(wanted, CUTS, 0, 0, tiled=True)
    codes = leaf_codes.reshape(blocks, 2, 2, 2, 2, 2, local_rows).transpose(5, 3, 4, 1, 2, 6, 0)
    codes = codes.reshape(cut_count, own)
    me = [lax.axis_index(CUTS), lax.axis_index(("core", "z1", "yl", "z4", "z2"))]
    sent, codes = pack(
        jnp.stack(me).astype(jnp.int32), part.reshape(1), wanted, branch_table, codes
    )
    slots = lax.all_to_all(sent, CUTS, 0, 0, tiled=True)
    slots = slots.reshape((-1,) + slots.shape[2:])

    slices = leaf_tables.shape[0] // SPLIT
    leaf = leaf_tables.reshape(SPLIT, slices, 2 * states, 2 * width)
    kept = jnp.where(yh == 0, leaf[0], leaf[1])
    given = jnp.where(yh == 0, leaf[1], leaf[0])
    leaf = jnp.stack([kept, swap(given, "yh")])
    leaf = [leaf] + [swap(leaf, "x", bit) for bit in range(1, lax.axis_size("x"))]

    rows_here = panels.transpose(1, 0, 2, 3).reshape(own, 2 * width)
    rows_here = jnp.concatenate(
        [rows_here] + [swap(rows_here, ("z4", "z2"), bit) for bit in range(1, 4)], axis=0
    )
    rows_here = jnp.concatenate([rows_here, swap(rows_here, "yl")], axis=0)
    rows_there = swap(rows_here, "yh")

    codes = codes.reshape(4, 1, cut_count // 4, own)
    codes = jnp.concatenate([codes, swap(codes, "yh")], axis=1).reshape(-1, 1)
    leaf_states = states * peers
    low, high = codes % leaf_states, codes // leaf_states
    low = ((low // states) ^ part) * (2 * states) + low % states
    high = ((high // states) ^ part) * (2 * states) + states + high % states
    column = lax.broadcasted_iota(jnp.int32, (1, 2 * leaf_states), 1)
    low = (low == column).astype(BF)
    high = (high == column).astype(BF)

    kept, given, rows_here = choose(
        slice_terms.reshape(-1),
        yh.reshape(1),
        slots,
        rows_here,
        rows_there,
        (low, high, *leaf),
    )
    got = swap(given, "yh")
    pieces = []
    for piece in (kept, got):
        pieces += [piece] + [swap(piece, "x", bit) for bit in range(1, lax.axis_size("x"))]
    weights = weigh(low, high, leaf, kept)

    rows_here = [rows_here, swap(rows_here, "z1")]
    rows_here = rows_here + [swap(a, "core") for a in rows_here]

    place = jnp.stack([lax.axis_index(order).astype(jnp.int32), part])
    mine, theirs = amplitudes_of(place, weights, pieces, rows_here, own)
    amps = mine + swap(theirs, "core")
    amps = lax.all_to_all(amps, order, 0, 0, tiled=True)
    amps = jnp.sum(amps, axis=0).reshape(2, local_rows, blocks)
    return amps.transpose(2, 1, 0)


def solution(mesh):
    fine = Mesh(mesh.devices.reshape(2, 2, 2, 2, 2, 2, 4), CUTS + OUT)
    return jax.shard_map(
        body,
        mesh=fine,
        in_specs=(
            P(OUT, CUTS, None, None),
            P(CUTS, None, OUT, None, None),
            P(OUT, None),
            P(CUTS, None, None, None),
            P(CUTS, None, None),
            P(CUTS, None),
        ),
        out_specs=P(OUT, CUTS, None),
        check_vma=False,
    )
```

time: 143 us -> 116 us (0.81)
  waiting for transfers between devices: 34.8 us -> 12.5 us
  between operations: 13.6 us -> 0.24 us
  starting transfers between devices: 42.7 us -> 50.7 us
  Pallas kernels: 26 us -> 19.5 us
  local copies, waits for them, and re-layouts: 7.55 us -> 13.7 us
  blocking collectives: 12.7 us -> 15.6 us
  other arithmetic: 5.28 us -> 2.67 us
    ppermute x5 -> x21, starting transfers between devices: 14.6 us -> 37.7 us  [swap(): return lax.ppermute(a, axis, [(i, i ^ bit) for i in range(count)])]
    all_to_all x3 -> x1, starting transfers between devices: 23.9 us -> 8.7 us  [body(): wanted = lax.all_to_all(wanted, CUTS, 0, 0, tiled=True)]
    all_to_all x1, waiting for transfers between devices: 11.3 us -> 0.01 us  [body(): slots = lax.all_to_all(sent, CUTS, 0, 0, tiled=True)]
    all_gather x1 -> x0, waiting for transfers between devices: 8.84 us -> none  [body(): rows_here = lax.all_gather(rows_here, 'z', axis=0, tiled=True)]
    unnamed x16 -> x29, local copies, waits for them, and re-layouts: 2.59 us -> 10.6 us
    all_to_all x3 -> x1, waiting for transfers between devices: 11.1 us -> 3.38 us  [body(): wanted = lax.all_to_all(wanted, CUTS, 0, 0, tiled=True)]
    pallas_call x4, Pallas kernels: 26 us -> 19.5 us  [the longest x1 9.04 us: weigh(): pl.pallas_call(weight_kernel, out_shape=pltpu.VMEM((rows, depth), BF), in...]
    ppermute x5 -> x21, waiting for transfers between devices: 3.6 us -> 9.15 us  [swap(): return lax.ppermute(a, axis, [(i, i ^ bit) for i in range(count)])]
  transfers between devices with their start and end apart: 10 -> 23, of which waited for: 7 -> 8; matrix products, arithmetic and copies ran while one was open for 6% -> 5% of each run, Pallas kernels for 10% -> 10%
where the time goes in v2:
time: 116 us; the launch traced here: 115 us
  starting transfers between devices  50.7 us (44%)
  Pallas kernels  19.5 us (17%)
  blocking collectives  15.6 us (13%)
  local copies, waits for them, and re-layouts  13.7 us (12%)
  waiting for transfers between devices  12.5 us (11%)
  other arithmetic  2.67 us (2%)
    ppermute x21, starting transfers between devices, swap(): return lax.ppermute(a, axis, [(i, i ^ bit) for i in range(count)])  37.7 us
    all_to_all x1, blocking collectives, body(): amps = lax.all_to_all(amps, order, 0, 0, tiled=True)  15.6 us
    unnamed x29, local copies, waits for them, and re-layouts  10.6 us
    ppermute x21, waiting for transfers between devices, swap(): return lax.ppermute(a, axis, [(i, i ^ bit) for i in range(count)])  9.15 us
    pallas_call x1, Pallas kernels, weigh(): pl.pallas_call(weight_kernel, out_shape=pltpu.VMEM((rows, depth), BF), in...  9.04 us
    all_to_all x1, starting transfers between devices, body(): wanted = lax.all_to_all(wanted, CUTS, 0, 0, tiled=True)  8.7 us
    pallas_call x1, Pallas kernels, amplitudes_of(): pl.pallas_call(amp_kernel, out_shape=(jax.ShapeDtypeStruct((rows // each...  6.71 us
    all_to_all x1, starting transfers between devices, body(): slots = lax.all_to_all(sent, CUTS, 0, 0, tiled=True)  4.23 us
  transfers between devices with their start and end apart: 23, of which 8 were waited for; matrix products, arithmetic and copies ran while one was open for 5% of the time, Pallas kernels for 10%

profile of v2, /device:TPU:1, one launch (start us, length us, event | category | flops | bytes accessed | tf_op | source)
XLA Modules:
  0.0 114.9 jit_solution(16289502612741200093)
XLA Ops:
  0.0 0.8 copy.23
  0.8 3.9 %collective-permute-start.5 = (bf16[64,256]{1,0:T(8,128)(2,1)S(1)}, bf16[64,256]{1,0:T(8,128)(2,1)S(1)}, u32[]{:S(2)}, u32[]{:S(2)}) collective-permute-start(bf16[64,256]{1,0:T(8,128)(2,1)S(1)} %bitcast.36), channel_id=1, source_target_pairs={{0,64},{64,0},{128,192},{192,128},{1,65},{65,1},{129,193},{193,129... | collective-permute-start | bytes 98312 | tf_op jit(solution)/shard_map/ppermute | solution.py:22
  4.7 5.1 %collective-permute-start.6 = (bf16[64,256]{1,0:T(8,128)(2,1)S(1)}, bf16[64,256]{1,0:T(8,128)(2,1)S(1)}, u32[]{:S(2)}, u32[]{:S(2)}) collective-permute-start(bf16[64,256]{1,0:T(8,128)(2,1)S(1)} %bitcast.37), channel_id=1, source_target_pairs={{0,128},{64,192},{128,0},{192,64},{1,129},{65,193},{129,1},{193,65... | collective-permute-start | bytes 98312 | tf_op jit(solution)/shard_map/ppermute | solution.py:22
  9.8 1.3 %broadcast_in_dim.8 = s32[32,2,32]{2,1,0:T(2,128)} broadcast(s32[2,32]{1,0:T(2,128)} %bitcast.44), dimensions={1,2} | broadcast | bytes 8448 | tf_op jit(solution)/shard_map/broadcast_in_dim | solution.py:202
  11.1 8.7 %all-to-all-start = ((s32[32,2,32]{2,1,0:T(2,128)}), s32[32,2,32]{2,1,0:T(2,128)S(1)}, u32[]{:S(2)}, u32[]{:S(2)}) async-start(s32[32,2,32]{2,1,0:T(2,128)} %broadcast_in_dim.8), calls=%async_computation | async-start | bytes 65536 | tf_op jit(solution)/shard_map/all_to_all | solution.py:203
  19.8 1.0 broadcast_select_fusion.1
  20.9 2.7 %collective-permute-start.1 = (bf16[8,16,256]{2,1,0:T(8,128)(2,1)S(1)}, bf16[8,16,256]{2,1,0:T(8,128)(2,1)S(1)}, u32[]{:S(2)}, u32[]{:S(2)}) collective-permute-start(bf16[8,16,256]{2,1,0:T(8,128)(2,1)S(1)} %select_n.91), channel_id=1, source_target_pairs={{0,4},{4,0},{1,5},{5,1},{2,6},{6,2},{3,7},{7,3},{8,12},{12,8},{9,1... | collective-permute-start | bytes 196616 | tf_op jit(solution)/shard_map/ppermute | solution.py:22
  23.7 0.8 copy.18
  24.6 3.4 %all-to-all-done.wanted = s32[32,2,32]{2,1,0:T(2,128)S(1)} async-done(((s32[32,2,32]{2,1,0:T(2,128)}), s32[32,2,32]{2,1,0:T(2,128)S(1)}, u32[]{:S(2)}, u32[]{:S(2)}) %all-to-all-start) | async-done | bytes 8224 | tf_op jit(solution)/shard_map/all_to_all | solution.py:203
  27.9 2.5 %pack.1 = (bf16[32,2,2,16,128]{4,3,2,1,0:T(8,128)(2,1)}, s32[32,64]{1,0:T(8,128)S(1)}) custom-call(s32[2]{0:T(128)S(1)} %pad_add_fusion.2.me, s32[1]{0:T(128)} %bitcast.1.part, s32[32,2,32]{2,1,0:T(2,128)S(1)} %all-to-all-done.wanted, bf16[12,2,128,128]{3,2,1,0:T(8,128)(2,1)} %table.1, s32[32,64]{1,0:T(8,128)S(1)} %reshape.258.codes), custom_call_target="tpu_custom_call" | custom-call | tf_op jit(solution)/shard_map/pack/pallas_call | solution.py:39
  30.5 2.6 %collective-permute-start = (s32[4,1,8,64]{3,2,1,0:T(8,128)S(1)}, s32[4,1,8,64]{3,2,1,0:T(8,128)S(1)}, u32[]{:S(2)}, u32[]{:S(2)}) collective-permute-start(s32[4,1,8,64]{3,2,1,0:T(8,128)S(1)} %bitcast.31), channel_id=1, source_target_pairs={{0,4},{4,0},{1,5},{5,1},{2,6},{6,2},{3,7},{7,3},{8,12},{12,8},{9,1... | collective-permute-start | bytes 24584 | tf_op jit(solution)/shard_map/ppermute | solution.py:22
  33.1 0.8 copy.22
  34.0 4.2 %all-to-all-start.1 = ((bf16[32,2,2,16,128]{4,3,2,1,0:T(8,128)(2,1)}), bf16[32,2,2,16,128]{4,3,2,1,0:T(8,128)(2,1)S(1)}, u32[]{:S(2)}, u32[]{:S(2)}) async-start(bf16[32,2,2,16,128]{4,3,2,1,0:T(8,128)(2,1)} %get-tuple-element.13), calls=%async_computation.1 | async-start | bytes 1048576 | tf_op jit(solution)/shard_map/all_to_all | solution.py:210
  38.4 1.5 %collective-permute-start.8 = (bf16[256,256]{1,0:T(8,128)(2,1)S(1)}, bf16[256,256]{1,0:T(8,128)(2,1)S(1)}, u32[]{:S(2)}, u32[]{:S(2)}) collective-permute-start(bf16[256,256]{1,0:T(8,128)(2,1)S(1)} %pad_maximum_fusion.1), channel_id=1, source_target_pairs={{0,16},{16,0},{1,17},{17,1},{2,18},{18,2},{3,19},{19,3},{4,20},{20... | collective-permute-start | bytes 393224 | tf_op jit(solution)/shard_map/ppermute | solution.py:22
  39.9 1.3 %collective-permute-start.2 = (bf16[2,8,16,256]{3,2,1,0:T(8,128)(2,1)S(1)}, bf16[2,8,16,256]{3,2,1,0:T(8,128)(2,1)S(1)}, u32[]{:S(2)}, u32[]{:S(2)}) collective-permute-start(bf16[2,8,16,256]{3,2,1,0:T(8,128)(2,1)S(1)} %pad_maximum_fusion.refs_2_.refs_0_), channel_id=1, source_target_pairs={{0,1},{1,0},{2,3},{3,2},{4,5},{5,4},{6,7},{7,6},{8,9},{9,8},{10,11... | collective-permute-start | bytes 393224 | tf_op jit(solution)/shard_map/ppermute | solution.py:22
  41.2 2.5 %collective-permute-start.3 = (bf16[2,8,16,256]{3,2,1,0:T(8,128)(2,1)S(1)}, bf16[2,8,16,256]{3,2,1,0:T(8,128)(2,1)S(1)}, u32[]{:S(2)}, u32[]{:S(2)}) collective-permute-start(bf16[2,8,16,256]{3,2,1,0:T(8,128)(2,1)S(1)} %pad_maximum_fusion.refs_2_.refs_0_), channel_id=1, source_target_pairs={{0,2},{1,3},{2,0},{3,1},{4,6},{5,7},{6,4},{7,5},{8,10},{9,11},{10,... | collective-permute-start | bytes 393224 | tf_op jit(solution)/shard_map/ppermute | solution.py:22
  43.9 0.4 collective-permute-done.8
  44.3 1.7 %collective-permute-start.9 = (bf16[512,256]{1,0:T(8,128)(2,1)S(1)}, bf16[512,256]{1,0:T(8,128)(2,1)S(1)}, u32[]{:S(2)}, u32[]{:S(2)}) collective-permute-start(bf16[512,256]{1,0:T(8,128)(2,1)S(1)} %constant_dynamic-update-slice_fusion.first_rows), channel_id=1, source_target_pairs={{0,4},{4,0},{1,5},{5,1},{2,6},{6,2},{3,7},{7,3},{8,12},{12,8},{9,1... | collective-permute-start | bytes 786440 | tf_op jit(solution)/shard_map/ppermute | solution.py:22
  46.0 1.4 %fusion = (bf16[4096,128]{1,0:T(8,128)(2,1)S(1)}, bf16[4096,128]{1,0:T(8,128)(2,1)S(1)}) fusion(s32[4096]{0:T(1024)S(1)} %get-tuple-element.22, s32[4096]{0:T(1024)S(1)} %get-tuple-element.21), kind=kLoop, calls=%fused_computation.2 | loop fusion | flops 2097152 | bytes 2129920 | tf_op jit(solution)/shard_map/convert_element_type | solution.py:234
  47.4 0.6 copy-done.2
  48.1 1.4 %collective-permute-done.3.refs_4_.refs_2_ = bf16[2,8,16,256]{3,2,1,0:T(8,128)(2,1)S(1)} collective-permute-done((bf16[2,8,16,256]{3,2,1,0:T(8,128)(2,1)S(1)}, bf16[2,8,16,256]{3,2,1,0:T(8,128)(2,1)S(1)}, u32[]{:S(2)}, u32[]{:S(2)}) %collective-permute-start.3) | collective-permute-done | bytes 131104 | tf_op jit(solution)/shard_map/ppermute | solution.py:22
  49.4 0.6 copy-done.5
  50.1 1.9 %collective-permute-done.4.refs_5_.refs_3_ = bf16[2,8,16,256]{3,2,1,0:T(8,128)(2,1)S(1)} collective-permute-done((bf16[2,8,16,256]{3,2,1,0:T(8,128)(2,1)S(1)}, bf16[2,8,16,256]{3,2,1,0:T(8,128)(2,1)S(1)}, u32[]{:S(2)}, u32[]{:S(2)}) %collective-permute-start.4) | collective-permute-done | bytes 131104 | tf_op jit(solution)/shard_map/ppermute | solution.py:22
  52.0 0.6 copy-done.8
  52.6 2.4 %collective-permute-done.9.second_rows = bf16[512,256]{1,0:T(8,128)(2,1)S(1)} collective-permute-done((bf16[512,256]{1,0:T(8,128)(2,1)S(1)}, bf16[512,256]{1,0:T(8,128)(2,1)S(1)}, u32[]{:S(2)}, u32[]{:S(2)}) %collective-permute-start.9) | collective-permute-done | bytes 262176 | tf_op jit(solution)/shard_map/ppermute | solution.py:22
  55.0 0.7 copy-done
  55.7 0.9 copy-done.1
  56.7 0.9 copy-done.3
  57.6 0.9 copy-done.6
  58.5 0.9 copy-done.9
  59.4 1.3 %choose.1 = (bf16[8,2,2,16,128]{4,3,2,1,0:T(8,128)(2,1)}, bf16[8,2,2,16,128]{4,3,2,1,0:T(8,128)(2,1)}, bf16[1024,256]{1,0:T(8,128)(2,1)S(1)}) custom-call(s32[32]{0:T(128)S(1)} %reshape.261.terms, s32[1]{0:T(128)} %bitcast.12.half, bf16[64,2,16,128]{3,2,1,0:T(8,128)(2,1)S(1)} %bitcast.30, bf16[512,256]{1,0:T(8,128)(2,1)S(1)} %constant_dynamic-update-slice_fusion.first_rows, ...), custom_call_target="tpu_custom_call" | custom-call | tf_op jit(solution)/shard_map/choose/pallas_call | solution.py:79
  60.7 2.3 %collective-permute-start.17 = (bf16[1024,256]{1,0:T(8,128)(2,1)S(1)}, bf16[1024,256]{1,0:T(8,128)(2,1)S(1)}, u32[]{:S(2)}, u32[]{:S(2)}) collective-permute-start(bf16[1024,256]{1,0:T(8,128)(2,1)S(1)} %get-tuple-element.16.refs_8_), channel_id=1, source_target_pairs={{0,32},{32,0},{1,33},{33,1},{2,34},{34,2},{3,35},{35,3},{4,36},{36... | collective-permute-start | bytes 1572872 | tf_op jit(solution)/shard_map/ppermute | solution.py:22
  63.0 1.2 %collective-permute-start.10 = (bf16[8,2,2,16,128]{4,3,2,1,0:T(8,128)(2,1)}, bf16[8,2,2,16,128]{4,3,2,1,0:T(8,128)(2,1)S(1)}, u32[]{:S(2)}, u32[]{:S(2)}) collective-permute-start(bf16[8,2,2,16,128]{4,3,2,1,0:T(8,128)(2,1)} %get-tuple-element.14.refs_4_.refs_0_), channel_id=1, source_target_pairs={{0,1},{1,0},{2,3},{3,2},{4,5},{5,4},{6,7},{7,6},{8,9},{9,8},{10,11... | collective-permute-start | bytes 393224 | tf_op jit(solution)/shard_map/ppermute | solution.py:22
  64.2 1.6 %collective-permute-start.13 = (bf16[8,2,2,16,128]{4,3,2,1,0:T(8,128)(2,1)}, bf16[8,2,2,16,128]{4,3,2,1,0:T(8,128)(2,1)S(1)}, u32[]{:S(2)}, u32[]{:S(2)}) collective-permute-start(bf16[8,2,2,16,128]{4,3,2,1,0:T(8,128)(2,1)} %get-tuple-element.15), channel_id=1, source_target_pairs={{0,4},{4,0},{1,5},{5,1},{2,6},{6,2},{3,7},{7,3},{8,12},{12,8},{9,1... | collective-permute-start | bytes 393224 | tf_op jit(solution)/shard_map/ppermute | solution.py:22
  65.7 2.5 %collective-permute-start.11 = (bf16[8,2,2,16,128]{4,3,2,1,0:T(8,128)(2,1)}, bf16[8,2,2,16,128]{4,3,2,1,0:T(8,128)(2,1)}, u32[]{:S(2)}, u32[]{:S(2)}) collective-permute-start(bf16[8,2,2,16,128]{4,3,2,1,0:T(8,128)(2,1)} %get-tuple-element.14.refs_4_.refs_0_), channel_id=1, source_target_pairs={{0,2},{1,3},{2,0},{3,1},{4,6},{5,7},{6,4},{7,5},{8,10},{9,11},{10,... | collective-permute-start | bytes 393224 | tf_op jit(solution)/shard_map/ppermute | solution.py:22
  68.5 2.8 %collective-permute-start.18 = (bf16[1024,256]{1,0:T(8,128)(2,1)S(1)}, bf16[1024,256]{1,0:T(8,128)(2,1)S(1)}, u32[]{:S(2)}, u32[]{:S(2)}) collective-permute-start(bf16[1024,256]{1,0:T(8,128)(2,1)S(1)} %get-tuple-element.16.refs_8_), channel_id=1, source_target_pairs={{0,8},{8,0},{1,9},{9,1},{2,10},{10,2},{3,11},{11,3},{4,12},{12,4},... | collective-permute-start | bytes 1572872 | tf_op jit(solution)/shard_map/ppermute | solution.py:22
  71.3 1.4 %collective-permute-done.11.refs_2_ = bf16[8,2,2,16,128]{4,3,2,1,0:T(8,128)(2,1)} collective-permute-done((bf16[8,2,2,16,128]{4,3,2,1,0:T(8,128)(2,1)}, bf16[8,2,2,16,128]{4,3,2,1,0:T(8,128)(2,1)}, u32[]{:S(2)}, u32[]{:S(2)}) %collective-permute-start.11) | collective-permute-done | bytes 131104 | tf_op jit(solution)/shard_map/ppermute | solution.py:22
  72.7 2.3 %collective-permute-start.15 = (bf16[8,2,2,16,128]{4,3,2,1,0:T(8,128)(2,1)S(1)}, bf16[8,2,2,16,128]{4,3,2,1,0:T(8,128)(2,1)S(1)}, u32[]{:S(2)}, u32[]{:S(2)}) collective-permute-start(bf16[8,2,2,16,128]{4,3,2,1,0:T(8,128)(2,1)S(1)} %collective-permute-done.13.refs_4_), channel_id=1, source_target_pairs={{0,2},{1,3},{2,0},{3,1},{4,6},{5,7},{6,4},{7,5},{8,10},{9,11},{10,... | collective-permute-start | bytes 393224 | tf_op jit(solution)/shard_map/ppermute | solution.py:22
  75.0 0.5 collective-permute-done.12.refs_3_
  75.5 3.3 %collective-permute-start.19 = (bf16[1024,256]{1,0:T(8,128)(2,1)S(1)}, bf16[1024,256]{1,0:T(8,128)(2,1)S(1)}, u32[]{:S(2)}, u32[]{:S(2)}) collective-permute-start(bf16[1024,256]{1,0:T(8,128)(2,1)S(1)} %collective-permute-done.17.refs_9_), channel_id=1, source_target_pairs={{0,8},{8,0},{1,9},{9,1},{2,10},{10,2},{3,11},{11,3},{4,12},{12,4},... | collective-permute-start | bytes 1572872 | tf_op jit(solution)/shard_map/ppermute | solution.py:22
  78.8 0.9 copy-done.4
  79.7 0.9 copy-done.7
  80.6 0.9 copy-done.10
  81.5 9.0 %weigh.1.weights = bf16[4096,2048]{1,0:T(8,128)(2,1)S(1)} custom-call(bf16[4096,128]{1,0:T(8,128)(2,1)S(1)} %get-tuple-element.23.refs_0_.low, bf16[4096,128]{1,0:T(8,128)(2,1)S(1)} %get-tuple-element.24.refs_1_.high, bf16[2,8,16,256]{3,2,1,0:T(8,128)(2,1)S(1)} %pad_maximum_fusion.refs_2_.refs_0_, bf16[2,8,16,256]{3,2,1,0:T(8,128)(2,1)S(1)} %copy-done.4, ...), custom_call_target="tpu_custom_call" | custom-call | flops 17179869184 | bytes 16777216 | tf_op jit(solution)/shard_map/weigh/pallas_call | solution.py:114
  90.6 6.7 %amplitudes.1 = (f32[32,128]{1,0:T(8,128)S(1)}, f32[32,128]{1,0:T(8,128)S(1)}) custom-call(s32[2]{0:T(128)S(1)} %pad_add_fusion.1.me, bf16[4096,2048]{1,0:T(8,128)(2,1)S(1)} %weigh.1.weights, bf16[8,2,2,16,128]{4,3,2,1,0:T(8,128)(2,1)} %get-tuple-element.14.refs_4_.refs_0_, bf16[8,2,2,16,128]{4,3,2,1,0:T(8,128)(2,1)S(1)} %collective-permute-done.10.refs_1_, ...), custom_call_target="tpu_custom_call" | custom-call | tf_op jit(solution)/shard_map/amplitudes/pallas_call | solution.py:176
  97.4 1.2 %collective-permute-done.20 = f32[32,128]{1,0:T(8,128)S(1)} collective-permute-done((f32[32,128]{1,0:T(8,128)S(1)}, f32[32,128]{1,0:T(8,128)S(1)}, u32[]{:S(2)}, u32[]{:S(2)}) %collective-permute-start.20) | collective-permute-done | bytes 16416 | tf_op jit(solution)/shard_map/ppermute | solution.py:22
  98.6 15.6 %all_to_all.19 = f32[32,1,128]{2,1,0:T(1,128)S(1)} all-to-all(f32[32,1,128]{2,1,0:T(1,128)S(1)} %bitcast.40), channel_id=1, replica_groups=mesh['z4'=2,'z2'=2,'z1'=2,'yl'=2,'core'=2,'yh'=2,'x'=4] {'z1','yh','yl',..., dimensions={0} | all-to-all | bytes 32768 | tf_op jit(solution)/shard_map/all_to_all | solution.py:257
  114.3 0.6 copy.25
  (53 shorter events, 1.3 us)
Async XLA Ops:
  0.8 37.6 %collective-permute-start.5 = (bf16[64,256]{1,0:T(8,128)(2,1)S(1)}, bf16[64,256]{1,0:T(8,128)(2,1)S(1)}, u32[]{:S(2)}, u32[]{:S(2)}) collective-permute-start(bf16[64,256]{1,0:T(8,128)(2,1)S(1)} %bitcast.36), channel_id=1, source_target_pairs={{0,64},{64,0},{128,192},{192,128},{1,65},{65,1},{129,193},{193,129... | collective-permute-start | bytes 98312 | tf_op jit(solution)/shard_map/ppermute | solution.py:22
  4.7 33.7 %collective-permute-start.6 = (bf16[64,256]{1,0:T(8,128)(2,1)S(1)}, bf16[64,256]{1,0:T(8,128)(2,1)S(1)}, u32[]{:S(2)}, u32[]{:S(2)}) collective-permute-start(bf16[64,256]{1,0:T(8,128)(2,1)S(1)} %bitcast.37), channel_id=1, source_target_pairs={{0,128},{64,192},{128,0},{192,64},{1,129},{65,193},{129,1},{193,65... | collective-permute-start | bytes 98312 | tf_op jit(solution)/shard_map/ppermute | solution.py:22
  9.8 28.6 %collective-permute-start.7 = (bf16[64,256]{1,0:T(8,128)(2,1)S(1)}, bf16[64,256]{1,0:T(8,128)(2,1)S(1)}, u32[]{:S(2)}, u32[]{:S(2)}) collective-permute-start(bf16[64,256]{1,0:T(8,128)(2,1)S(1)} %bitcast.38), channel_id=1, source_target_pairs={{0,192},{64,128},{128,64},{192,0},{1,193},{65,129},{129,65},{193,1... | collective-permute-start | bytes 98312 | tf_op jit(solution)/shard_map/ppermute | solution.py:22
  11.1 16.8 %all-to-all-start = ((s32[32,2,32]{2,1,0:T(2,128)}), s32[32,2,32]{2,1,0:T(2,128)S(1)}, u32[]{:S(2)}, u32[]{:S(2)}) async-start(s32[32,2,32]{2,1,0:T(2,128)} %broadcast_in_dim.8), calls=%async_computation | async-start | bytes 65536 | tf_op jit(solution)/shard_map/all_to_all | solution.py:203
  20.9 19.0 %collective-permute-start.1 = (bf16[8,16,256]{2,1,0:T(8,128)(2,1)S(1)}, bf16[8,16,256]{2,1,0:T(8,128)(2,1)S(1)}, u32[]{:S(2)}, u32[]{:S(2)}) collective-permute-start(bf16[8,16,256]{2,1,0:T(8,128)(2,1)S(1)} %select_n.91), channel_id=1, source_target_pairs={{0,4},{4,0},{1,5},{5,1},{2,6},{6,2},{3,7},{7,3},{8,12},{12,8},{9,1... | collective-permute-start | bytes 196616 | tf_op jit(solution)/shard_map/ppermute | solution.py:22
  30.5 7.8 %collective-permute-start = (s32[4,1,8,64]{3,2,1,0:T(8,128)S(1)}, s32[4,1,8,64]{3,2,1,0:T(8,128)S(1)}, u32[]{:S(2)}, u32[]{:S(2)}) collective-permute-start(s32[4,1,8,64]{3,2,1,0:T(8,128)S(1)} %bitcast.31), channel_id=1, source_target_pairs={{0,4},{4,0},{1,5},{5,1},{2,6},{6,2},{3,7},{7,3},{8,12},{12,8},{9,1... | collective-permute-start | bytes 24584 | tf_op jit(solution)/shard_map/ppermute | solution.py:22
  34.0 21.7 %all-to-all-start.1 = ((bf16[32,2,2,16,128]{4,3,2,1,0:T(8,128)(2,1)}), bf16[32,2,2,16,128]{4,3,2,1,0:T(8,128)(2,1)S(1)}, u32[]{:S(2)}, u32[]{:S(2)}) async-start(bf16[32,2,2,16,128]{4,3,2,1,0:T(8,128)(2,1)} %get-tuple-element.13), calls=%async_computation.1 | async-start | bytes 1048576 | tf_op jit(solution)/shard_map/all_to_all | solution.py:210
  38.4 5.9 %collective-permute-start.8 = (bf16[256,256]{1,0:T(8,128)(2,1)S(1)}, bf16[256,256]{1,0:T(8,128)(2,1)S(1)}, u32[]{:S(2)}, u32[]{:S(2)}) collective-permute-start(bf16[256,256]{1,0:T(8,128)(2,1)S(1)} %pad_maximum_fusion.1), channel_id=1, source_target_pairs={{0,16},{16,0},{1,17},{17,1},{2,18},{18,2},{3,19},{19,3},{4,20},{20... | collective-permute-start | bytes 393224 | tf_op jit(solution)/shard_map/ppermute | solution.py:22
  39.9 7.5 %collective-permute-start.2 = (bf16[2,8,16,256]{3,2,1,0:T(8,128)(2,1)S(1)}, bf16[2,8,16,256]{3,2,1,0:T(8,128)(2,1)S(1)}, u32[]{:S(2)}, u32[]{:S(2)}) collective-permute-start(bf16[2,8,16,256]{3,2,1,0:T(8,128)(2,1)S(1)} %pad_maximum_fusion.refs_2_.refs_0_), channel_id=1, source_target_pairs={{0,1},{1,0},{2,3},{3,2},{4,5},{5,4},{6,7},{7,6},{8,9},{9,8},{10,11... | collective-permute-start | bytes 393224 | tf_op jit(solution)/shard_map/ppermute | solution.py:22
  41.2 8.2 %collective-permute-start.3 = (bf16[2,8,16,256]{3,2,1,0:T(8,128)(2,1)S(1)}, bf16[2,8,16,256]{3,2,1,0:T(8,128)(2,1)S(1)}, u32[]{:S(2)}, u32[]{:S(2)}) collective-permute-start(bf16[2,8,16,256]{3,2,1,0:T(8,128)(2,1)S(1)} %pad_maximum_fusion.refs_2_.refs_0_), channel_id=1, source_target_pairs={{0,2},{1,3},{2,0},{3,1},{4,6},{5,7},{6,4},{7,5},{8,10},{9,11},{10,... | collective-permute-start | bytes 393224 | tf_op jit(solution)/shard_map/ppermute | solution.py:22
  43.7 8.3 %collective-permute-start.4 = (bf16[2,8,16,256]{3,2,1,0:T(8,128)(2,1)S(1)}, bf16[2,8,16,256]{3,2,1,0:T(8,128)(2,1)S(1)}, u32[]{:S(2)}, u32[]{:S(2)}) collective-permute-start(bf16[2,8,16,256]{3,2,1,0:T(8,128)(2,1)S(1)} %pad_maximum_fusion.refs_2_.refs_0_), channel_id=1, source_target_pairs={{0,3},{1,2},{2,1},{3,0},{4,7},{5,6},{6,5},{7,4},{8,11},{9,10},{10,... | collective-permute-start | bytes 393224 | tf_op jit(solution)/shard_map/ppermute | solution.py:22
  44.3 10.7 %collective-permute-start.9 = (bf16[512,256]{1,0:T(8,128)(2,1)S(1)}, bf16[512,256]{1,0:T(8,128)(2,1)S(1)}, u32[]{:S(2)}, u32[]{:S(2)}) collective-permute-start(bf16[512,256]{1,0:T(8,128)(2,1)S(1)} %constant_dynamic-update-slice_fusion.first_rows), channel_id=1, source_target_pairs={{0,4},{4,0},{1,5},{5,1},{2,6},{6,2},{3,7},{7,3},{8,12},{12,8},{9,1... | collective-permute-start | bytes 786440 | tf_op jit(solution)/shard_map/ppermute | solution.py:22
  47.4 0.7 copy-start.2
  49.4 0.6 copy-start.5
  52.0 0.7 copy-start.8
  55.0 0.7 copy-start
  55.7 1.0 copy-start.1
  56.7 0.9 copy-start.3
  57.6 0.9 copy-start.6
  58.5 0.9 copy-start.9
  60.7 14.9 %collective-permute-start.17 = (bf16[1024,256]{1,0:T(8,128)(2,1)S(1)}, bf16[1024,256]{1,0:T(8,128)(2,1)S(1)}, u32[]{:S(2)}, u32[]{:S(2)}) collective-permute-start(bf16[1024,256]{1,0:T(8,128)(2,1)S(1)} %get-tuple-element.16.refs_8_), channel_id=1, source_target_pairs={{0,32},{32,0},{1,33},{33,1},{2,34},{34,2},{3,35},{35,3},{4,36},{36... | collective-permute-start | bytes 1572872 | tf_op jit(solution)/shard_map/ppermute | solution.py:22
  63.0 5.5 %collective-permute-start.10 = (bf16[8,2,2,16,128]{4,3,2,1,0:T(8,128)(2,1)}, bf16[8,2,2,16,128]{4,3,2,1,0:T(8,128)(2,1)S(1)}, u32[]{:S(2)}, u32[]{:S(2)}) collective-permute-start(bf16[8,2,2,16,128]{4,3,2,1,0:T(8,128)(2,1)} %get-tuple-element.14.refs_4_.refs_0_), channel_id=1, source_target_pairs={{0,1},{1,0},{2,3},{3,2},{4,5},{5,4},{6,7},{7,6},{8,9},{9,8},{10,11... | collective-permute-start | bytes 393224 | tf_op jit(solution)/shard_map/ppermute | solution.py:22
  64.2 7.1 %collective-permute-start.13 = (bf16[8,2,2,16,128]{4,3,2,1,0:T(8,128)(2,1)}, bf16[8,2,2,16,128]{4,3,2,1,0:T(8,128)(2,1)S(1)}, u32[]{:S(2)}, u32[]{:S(2)}) collective-permute-start(bf16[8,2,2,16,128]{4,3,2,1,0:T(8,128)(2,1)} %get-tuple-element.15), channel_id=1, source_target_pairs={{0,4},{4,0},{1,5},{5,1},{2,6},{6,2},{3,7},{7,3},{8,12},{12,8},{9,1... | collective-permute-start | bytes 393224 | tf_op jit(solution)/shard_map/ppermute | solution.py:22
  65.7 6.9 %collective-permute-start.11 = (bf16[8,2,2,16,128]{4,3,2,1,0:T(8,128)(2,1)}, bf16[8,2,2,16,128]{4,3,2,1,0:T(8,128)(2,1)}, u32[]{:S(2)}, u32[]{:S(2)}) collective-permute-start(bf16[8,2,2,16,128]{4,3,2,1,0:T(8,128)(2,1)} %get-tuple-element.14.refs_4_.refs_0_), channel_id=1, source_target_pairs={{0,2},{1,3},{2,0},{3,1},{4,6},{5,7},{6,4},{7,5},{8,10},{9,11},{10,... | collective-permute-start | bytes 393224 | tf_op jit(solution)/shard_map/ppermute | solution.py:22
  68.2 7.3 %collective-permute-start.12 = (bf16[8,2,2,16,128]{4,3,2,1,0:T(8,128)(2,1)}, bf16[8,2,2,16,128]{4,3,2,1,0:T(8,128)(2,1)}, u32[]{:S(2)}, u32[]{:S(2)}) collective-permute-start(bf16[8,2,2,16,128]{4,3,2,1,0:T(8,128)(2,1)} %get-tuple-element.14.refs_4_.refs_0_), channel_id=1, source_target_pairs={{0,3},{1,2},{2,1},{3,0},{4,7},{5,6},{6,5},{7,4},{8,11},{9,10},{10,... | collective-permute-start | bytes 393224 | tf_op jit(solution)/shard_map/ppermute | solution.py:22
  68.5 22.2 %collective-permute-start.18 = (bf16[1024,256]{1,0:T(8,128)(2,1)S(1)}, bf16[1024,256]{1,0:T(8,128)(2,1)S(1)}, u32[]{:S(2)}, u32[]{:S(2)}) collective-permute-start(bf16[1024,256]{1,0:T(8,128)(2,1)S(1)} %get-tuple-element.16.refs_8_), channel_id=1, source_target_pairs={{0,8},{8,0},{1,9},{9,1},{2,10},{10,2},{3,11},{11,3},{4,12},{12,4},... | collective-permute-start | bytes 1572872 | tf_op jit(solution)/shard_map/ppermute | solution.py:22
  71.3 19.3 %collective-permute-start.14 = (bf16[8,2,2,16,128]{4,3,2,1,0:T(8,128)(2,1)S(1)}, bf16[8,2,2,16,128]{4,3,2,1,0:T(8,128)(2,1)S(1)}, u32[]{:S(2)}, u32[]{:S(2)}) collective-permute-start(bf16[8,2,2,16,128]{4,3,2,1,0:T(8,128)(2,1)S(1)} %collective-permute-done.13.refs_4_), channel_id=1, source_target_pairs={{0,1},{1,0},{2,3},{3,2},{4,5},{5,4},{6,7},{7,6},{8,9},{9,8},{10,11... | collective-permute-start | bytes 393224 | tf_op jit(solution)/shard_map/ppermute | solution.py:22
  72.7 17.9 %collective-permute-start.15 = (bf16[8,2,2,16,128]{4,3,2,1,0:T(8,128)(2,1)S(1)}, bf16[8,2,2,16,128]{4,3,2,1,0:T(8,128)(2,1)S(1)}, u32[]{:S(2)}, u32[]{:S(2)}) collective-permute-start(bf16[8,2,2,16,128]{4,3,2,1,0:T(8,128)(2,1)S(1)} %collective-permute-done.13.refs_4_), channel_id=1, source_target_pairs={{0,2},{1,3},{2,0},{3,1},{4,6},{5,7},{6,4},{7,5},{8,10},{9,11},{10,... | collective-permute-start | bytes 393224 | tf_op jit(solution)/shard_map/ppermute | solution.py:22
  75.5 15.1 %collective-permute-start.16 = (bf16[8,2,2,16,128]{4,3,2,1,0:T(8,128)(2,1)S(1)}, bf16[8,2,2,16,128]{4,3,2,1,0:T(8,128)(2,1)S(1)}, u32[]{:S(2)}, u32[]{:S(2)}) collective-permute-start(bf16[8,2,2,16,128]{4,3,2,1,0:T(8,128)(2,1)S(1)} %collective-permute-done.13.refs_4_), channel_id=1, source_target_pairs={{0,3},{1,2},{2,1},{3,0},{4,7},{5,6},{6,5},{7,4},{8,11},{9,10},{10,... | collective-permute-start | bytes 393224 | tf_op jit(solution)/shard_map/ppermute | solution.py:22
  75.5 15.1 %collective-permute-start.19 = (bf16[1024,256]{1,0:T(8,128)(2,1)S(1)}, bf16[1024,256]{1,0:T(8,128)(2,1)S(1)}, u32[]{:S(2)}, u32[]{:S(2)}) collective-permute-start(bf16[1024,256]{1,0:T(8,128)(2,1)S(1)} %collective-permute-done.17.refs_9_), channel_id=1, source_target_pairs={{0,8},{8,0},{1,9},{9,1},{2,10},{10,2},{3,11},{11,3},{4,12},{12,4},... | collective-permute-start | bytes 1572872 | tf_op jit(solution)/shard_map/ppermute | solution.py:22
  78.8 0.9 copy-start.4
  79.7 0.9 copy-start.7
  80.6 0.9 copy-start.10
  97.4 1.2 %collective-permute-start.20 = (f32[32,128]{1,0:T(8,128)S(1)}, f32[32,128]{1,0:T(8,128)S(1)}, u32[]{:S(2)}, u32[]{:S(2)}) collective-permute-start(f32[32,128]{1,0:T(8,128)S(1)} %get-tuple-element.18), channel_id=1, source_target_pairs={{0,8},{8,0},{1,9},{9,1},{2,10},{10,2},{3,11},{11,3},{4,12},{12,4},... | collective-permute-start | bytes 49160 | tf_op jit(solution)/shard_map/ppermute | solution.py:22

commit v3 on v2

--- a/solution.py
+++ b/solution.py
@@ -1,3 +1,5 @@
+import functools
+
 import jax
 import jax.numpy as jnp
 from jax import lax
@@ -12,9 +14,14 @@
 PARTS = 8
 SPLIT = 2
 ROW_TILE = 1024
-WEIGHT_TILE = 2048
+WEIGHT_TILE = 1024
 VMEM = 20 * 1024 * 1024
+EARLY = pl.CostEstimate(flops=16_000_000_000, bytes_accessed=0, transcendentals=0)
 IN_VMEM = pl.BlockSpec(memory_space=pltpu.VMEM)
+
+
+def in_hbm(a):
+    return pltpu.with_memory_space_constraint(a, pltpu.HBM)
 
 
 def swap(a, axis, bit=1):
@@ -22,42 +29,97 @@
     return lax.ppermute(a, axis, [(i, i ^ bit) for i in range(count)])
 
 
-def pack_kernel(me, part, wanted, table, codes, send, ordered):
+def prepare_kernel(at, leaf, codes, kept, given, ordered):
+    slices, lines, _ = kept.shape
+    slices = slices - 1
+    kept[:slices] = leaf[pl.ds(at[0] * slices, slices)]
+    given[:slices] = leaf[pl.ds((1 - at[0]) * slices, slices)]
+    count = codes.shape[0]
+    for d in range(count):
+        to = d // 2 + d % 2 * (count // 2)
+        ordered[to : to + 1, :] = codes[pl.ds(d ^ at[1], 1), :]
+    code = jnp.concatenate([ordered[: count // 2], ordered[count // 2 :]], axis=1)
+    states = lines // 2 * PARTS
+    both = jnp.concatenate([code % states, code // states], axis=1).astype(F32).astype(BF)
+    given[slices] = both
+    kept[slices] = both
+
+
+def prepare(at, leaf, codes):
+    slices, lines, pair = leaf.shape
+    slices = slices // SPLIT
+    return pl.pallas_call(
+        prepare_kernel,
+        out_shape=(
+            jax.ShapeDtypeStruct((slices + 1, lines, pair), BF),
+            jax.ShapeDtypeStruct((slices + 1, lines, pair), BF),
+        ),
+        in_specs=[pl.BlockSpec(memory_space=pltpu.SMEM)] + [IN_VMEM] * 2,
+        out_specs=(IN_VMEM,) * 2,
+        scratch_shapes=[pltpu.VMEM(codes.shape, codes.dtype)],
+        compiler_params=pltpu.CompilerParams(vmem_limit_bytes=VMEM),
+        name="prepare",
+    )(at, leaf, codes)
+
+
+def join_kernel(parts, *refs):
+    pieces, whole = refs[:parts], refs[-1]
+    count = pieces[0].shape[0]
+    for i, piece in enumerate(pieces):
+        whole[i * count : (i + 1) * count] = piece[...]
+
+
+def join(pieces, after=(), cost=None):
+    shape = (len(pieces) * pieces[0].shape[0],) + pieces[0].shape[1:]
+    return pl.pallas_call(
+        functools.partial(join_kernel, len(pieces)),
+        out_shape=jax.ShapeDtypeStruct(shape, pieces[0].dtype),
+        in_specs=[IN_VMEM] * len(pieces) + [pl.BlockSpec(memory_space=pl.ANY)] * len(after),
+        out_specs=IN_VMEM,
+        compiler_params=pltpu.CompilerParams(vmem_limit_bytes=VMEM),
+        cost_estimate=cost,
+        name="join",
+    )(*pieces, *after)
+
+
+def pack_kernel(me, part, wanted, table, *refs):
+    pieces, (send, rows) = refs[:4], refs[-2:]
     takers, capacity = send.shape[0], send.shape[1]
-    for d in range(takers):
-        ordered[d : d + 1, :] = codes[pl.ds(d ^ me[1], 1), :]
     for d in range(takers):
         for c in range(capacity):
             send[d, c] = table[wanted[d, c, me[0]]]
-
-
-def pack(me, part, wanted, table, codes):
+    count = pieces[0].shape[0]
+    for i, piece in enumerate(pieces):
+        rows[i * count : (i + 1) * count] = piece[...]
+
+
+def pack(me, part, wanted, table, pieces, ready):
     blocks, _, width, _ = table.shape
     rows = width // PARTS
     takers, capacity, _ = wanted.shape
     shape = (takers, capacity, 2, rows, width)
+    joined = (len(pieces) * pieces[0].shape[0], pieces[0].shape[1])
+
+    def whole(shape):
+        return pl.BlockSpec(shape, lambda i, me, part: (0,) * len(shape))
+
     return pl.pallas_call(
         pack_kernel,
-        out_shape=(
-            jax.ShapeDtypeStruct(shape, BF),
-            jax.ShapeDtypeStruct(codes.shape, codes.dtype),
-        ),
+        out_shape=(jax.ShapeDtypeStruct(shape, BF), jax.ShapeDtypeStruct(joined, BF)),
         grid_spec=pltpu.PrefetchScalarGridSpec(
             num_scalar_prefetch=2,
             grid=(1,),
             in_specs=[
                 pl.BlockSpec(memory_space=pltpu.SMEM),
                 pl.BlockSpec((blocks, 2, rows, width), lambda i, me, part: (0, 0, part[0], 0)),
-                pl.BlockSpec(codes.shape, lambda i, me, part: (0, 0)),
-            ],
-            out_specs=(
-                pl.BlockSpec(shape, lambda i, me, part: (0, 0, 0, 0, 0)),
-                pl.BlockSpec(codes.shape, lambda i, me, part: (0, 0)),
-            ),
+            ]
+            + [whole(piece.shape) for piece in pieces]
+            + [pl.BlockSpec(memory_space=pl.ANY)] * len(ready),
+            out_specs=(whole(shape), whole(joined)),
         ),
         compiler_params=pltpu.CompilerParams(vmem_limit_bytes=VMEM),
         name="pack",
-    )(me, part, wanted, pltpu.with_memory_space_constraint(table, pltpu.HBM), codes)
+    )(me, part, wanted, in_hbm(table), *pieces, *ready)
 
 
 def choose_kernel(terms, half, slots, first_rows, second_rows, *refs):
@@ -66,14 +128,14 @@
     for out, first in ((kept, half[0] * slices), (given, (1 - half[0]) * slices)):
         for s in range(slices):
             for t in range(2):
-                out[s, t] = slots[terms[(first + s) * 2 + t]]
+                out[s, t] = slots[terms[t, first + s]]
     count = first_rows.shape[0]
     rows[:count] = first_rows[...]
     rows[count:] = second_rows[...]
 
 
 def choose(terms, half, slots, first_rows, second_rows, ready):
-    shape = (terms.shape[0] // 2 // SPLIT, 2) + slots.shape[1:]
+    shape = (terms.shape[1] // SPLIT, 2) + slots.shape[1:]
     count, pair = first_rows.shape
     scalars = [pl.BlockSpec(memory_space=pltpu.SMEM)] * 2
     return pl.pallas_call(
@@ -87,14 +149,29 @@
     )(terms, half, slots, first_rows, second_rows, *ready)
 
 
-def weight_kernel(low, high, *refs):
-    leaf, weights = refs[:-2], refs[-1]
-    halves, slices, _, pair = leaf[0].shape
+def weight_kernel(part, *refs):
+    leaf, weights = refs[:4], refs[-1]
+    halves, slices, lines, pair = leaf[0].shape
+    slices = slices - 1
     width = pair // 2
-
-    def tile(i, carry):
-        here = pl.ds(pl.multiple_of(i * WEIGHT_TILE, WEIGHT_TILE), WEIGHT_TILE)
-        pick_low, pick_high = low[here, :], high[here, :]
+    places = []
+    for half in range(halves):
+        state = leaf[0][half, slices].astype(F32).astype(jnp.int32)
+        count = lines // 2
+        place = ((state // count) ^ part[0]) * lines + state % count
+        places.append((place[:, :width], place[:, width:] + count))
+    row = lax.broadcasted_iota(jnp.int32, (PARTS * lines, width), 0)
+
+    def picks(which, p):
+        line = p // 8 * 4 + p % 4
+        place = places[p // 4 % 2][which][line : line + 1, :]
+        return (place == row).astype(F32).astype(BF).T
+
+    for i in range(weights.shape[0] // WEIGHT_TILE):
+        here = slice(i * WEIGHT_TILE, (i + 1) * WEIGHT_TILE)
+        tile = range(here.start // width, here.stop // width)
+        pick_low = jnp.concatenate([picks(0, p) for p in tile], axis=0)
+        pick_high = jnp.concatenate([picks(1, p) for p in tile], axis=0)
         for s in range(slices):
             table = jnp.concatenate([piece[h, s] for h in range(halves) for piece in leaf], axis=0)
             a = jnp.dot(pick_low, table, preferred_element_type=F32)
@@ -103,25 +180,25 @@
             at = s * pair
             weights[here, at : at + width] = (a_re * b_re - a_im * b_im).astype(BF)
             weights[here, at + width : at + pair] = (a_re * b_im + a_im * b_re).astype(BF)
-        return carry
-
-    lax.fori_loop(0, low.shape[0] // WEIGHT_TILE, tile, 0)
-
-
-def weigh(low, high, leaf, chosen):
-    rows = low.shape[0]
-    depth = leaf[0].shape[1] * leaf[0].shape[3]
+
+
+def weigh(part, leaf, after):
+    halves, slices, lines, pair = leaf[0].shape
+    rows = halves * lines * (pair // 2)
+    depth = (slices - 1) * pair
     return pl.pallas_call(
         weight_kernel,
         out_shape=pltpu.VMEM((rows, depth), BF),
-        in_specs=[IN_VMEM] * (2 + len(leaf)) + [pl.BlockSpec(memory_space=pl.ANY)],
+        in_specs=[pl.BlockSpec(memory_space=pltpu.SMEM)]
+        + [IN_VMEM] * len(leaf)
+        + [pl.BlockSpec(memory_space=pl.ANY)],
         out_specs=IN_VMEM,
         compiler_params=pltpu.CompilerParams(vmem_limit_bytes=VMEM),
         cost_estimate=pl.CostEstimate(
             flops=8 * rows * 256 * depth, bytes_accessed=2 * rows * depth, transcendentals=0
         ),
         name="weigh",
-    )(low, high, *leaf, chosen)
+    )(part, *leaf, after)
 
 
 def amp_kernel(me, weights, *refs):
@@ -201,52 +278,41 @@
     wanted = fetch_list.transpose(0, 2, 1)
     wanted = jnp.broadcast_to(wanted, (cut_count,) + wanted.shape[1:])
     wanted = lax.all_to_all(wanted, CUTS, 0, 0, tiled=True)
+    rows_here = panels.transpose(1, 0, 2, 3).reshape(own, 2 * width)
+    rows_here = [rows_here] + [swap(rows_here, ("z4", "z2"), bit) for bit in range(1, 4)]
     codes = leaf_codes.reshape(blocks, 2, 2, 2, 2, 2, local_rows).transpose(5, 3, 4, 1, 2, 6, 0)
-    codes = codes.reshape(cut_count, own)
-    me = [lax.axis_index(CUTS), lax.axis_index(("core", "z1", "yl", "z4", "z2"))]
-    sent, codes = pack(
-        jnp.stack(me).astype(jnp.int32), part.reshape(1), wanted, branch_table, codes
+    at = [yh, lax.axis_index(("core", "z1", "yl", "z4", "z2")).astype(jnp.int32)]
+    kept, given = prepare(
+        jnp.stack(at),
+        leaf_tables.reshape(-1, 2 * states, 2 * width),
+        codes.reshape(cut_count, own),
     )
+    me = lax.axis_index(CUTS).astype(jnp.int32).reshape(1)
+    sent, rows_here = pack(me, part.reshape(1), wanted, branch_table, rows_here, (given,))
     slots = lax.all_to_all(sent, CUTS, 0, 0, tiled=True)
     slots = slots.reshape((-1,) + slots.shape[2:])
 
-    slices = leaf_tables.shape[0] // SPLIT
-    leaf = leaf_tables.reshape(SPLIT, slices, 2 * states, 2 * width)
-    kept = jnp.where(yh == 0, leaf[0], leaf[1])
-    given = jnp.where(yh == 0, leaf[1], leaf[0])
-    leaf = jnp.stack([kept, swap(given, "yh")])
+    got_leaf = swap(given, "yh")
+    leaf = join([kept, got_leaf], cost=EARLY).reshape((-1,) + got_leaf.shape)
     leaf = [leaf] + [swap(leaf, "x", bit) for bit in range(1, lax.axis_size("x"))]
-
-    rows_here = panels.transpose(1, 0, 2, 3).reshape(own, 2 * width)
-    rows_here = jnp.concatenate(
-        [rows_here] + [swap(rows_here, ("z4", "z2"), bit) for bit in range(1, 4)], axis=0
-    )
+    leaf = [in_hbm(a) for a in leaf]
+
     rows_here = jnp.concatenate([rows_here, swap(rows_here, "yl")], axis=0)
     rows_there = swap(rows_here, "yh")
 
-    codes = codes.reshape(4, 1, cut_count // 4, own)
-    codes = jnp.concatenate([codes, swap(codes, "yh")], axis=1).reshape(-1, 1)
-    leaf_states = states * peers
-    low, high = codes % leaf_states, codes // leaf_states
-    low = ((low // states) ^ part) * (2 * states) + low % states
-    high = ((high // states) ^ part) * (2 * states) + states + high % states
-    column = lax.broadcasted_iota(jnp.int32, (1, 2 * leaf_states), 1)
-    low = (low == column).astype(BF)
-    high = (high == column).astype(BF)
-
     kept, given, rows_here = choose(
-        slice_terms.reshape(-1),
+        slice_terms.T,
         yh.reshape(1),
         slots,
-        rows_here,
-        rows_there,
-        (low, high, *leaf),
+        in_hbm(rows_here),
+        in_hbm(rows_there),
+        tuple(leaf),
     )
     got = swap(given, "yh")
     pieces = []
     for piece in (kept, got):
         pieces += [piece] + [swap(piece, "x", bit) for bit in range(1, lax.axis_size("x"))]
-    weights = weigh(low, high, leaf, kept)
+    weights = weigh(part.reshape(1), leaf, kept)
 
     rows_here = [rows_here, swap(rows_here, "z1")]
     rows_here = rows_here + [swap(a, "core") for a in rows_here]

time: 116 us -> 105 us (0.905)
  waiting for transfers between devices: 12.5 us -> 21.5 us
  local copies, waits for them, and re-layouts: 13.7 us -> 4.96 us
  starting transfers between devices: 50.7 us -> 42.9 us
  other arithmetic: 2.67 us -> 0.2 us
    unnamed x29 -> x17, local copies, waits for them, and re-layouts: 10.6 us -> 1.08 us
    ppermute x21 -> x20, starting transfers between devices: 37.7 us -> 29.5 us  [swap(): return lax.ppermute(a, axis, [(i, i ^ bit) for i in range(count)])]
    ppermute x21 -> x20, waiting for transfers between devices: 9.15 us -> 12.8 us  [swap(): return lax.ppermute(a, axis, [(i, i ^ bit) for i in range(count)])]
    all_to_all x1, waiting for transfers between devices: 0.01 us -> 3.24 us  [body(): slots = lax.all_to_all(sent, CUTS, 0, 0, tiled=True)]
    all_to_all x1, waiting for transfers between devices: 3.38 us -> 5.45 us  [body(): wanted = lax.all_to_all(wanted, CUTS, 0, 0, tiled=True)]
    convert_element_type x1 -> x0, other arithmetic: 1.38 us -> none  [body(): low = (low == column).astype(BF)]
  transfers between devices with their start and end apart: 23 -> 22, of which waited for: 8 -> 9; matrix products, arithmetic and copies ran while one was open for 5% -> 3% of each run, Pallas kernels for 10% -> 10%
where the time goes in v3:
time: 105 us
  starting transfers between devices  42.9 us (41%)
  waiting for transfers between devices  21.5 us (20%)
  Pallas kernels  19.9 us (19%)
  blocking collectives  15 us (14%)
  local copies, waits for them, and re-layouts  4.96 us (5%)
    ppermute x20, starting transfers between devices, swap(): return lax.ppermute(a, axis, [(i, i ^ bit) for i in range(count)])  29.5 us
    all_to_all x1, blocking collectives, body(): amps = lax.all_to_all(amps, order, 0, 0, tiled=True)  15 us
    ppermute x20, waiting for transfers between devices, swap(): return lax.ppermute(a, axis, [(i, i ^ bit) for i in range(count)])  12.8 us
    pallas_call x1, Pallas kernels, weigh(): pl.pallas_call(weight_kernel, out_shape=pltpu.VMEM((rows, depth), BF), in...  10.1 us
    all_to_all x1, starting transfers between devices, body(): wanted = lax.all_to_all(wanted, CUTS, 0, 0, tiled=True)  8.7 us
    pallas_call x1, Pallas kernels, amplitudes_of(): pl.pallas_call(amp_kernel, out_shape=(jax.ShapeDtypeStruct((rows // each...  6.13 us
    all_to_all x1, waiting for transfers between devices, body(): wanted = lax.all_to_all(wanted, CUTS, 0, 0, tiled=True)  5.45 us
    all_to_all x1, starting transfers between devices, body(): slots = lax.all_to_all(sent, CUTS, 0, 0, tiled=True)  4.72 us
  transfers between devices with their start and end apart: 22, of which 9 were waited for; matrix products, arithmetic and copies ran while one was open for 3% of the time, Pallas kernels for 10%

profile of v3, /device:TPU:1, one launch (start us, length us, event | category | flops | bytes accessed | tf_op | source)
XLA Modules:
  0.0 104.8 jit_solution(1578719453120900386)
XLA Ops:
  0.0 0.8 copy.16
  0.8 3.9 %collective-permute-start.4 = (bf16[64,256]{1,0:T(8,128)(2,1)S(1)}, bf16[64,256]{1,0:T(8,128)(2,1)S(1)}, u32[]{:S(2)}, u32[]{:S(2)}) collective-permute-start(bf16[64,256]{1,0:T(8,128)(2,1)S(1)} %bitcast.30), channel_id=1, source_target_pairs={{0,64},{64,0},{128,192},{192,128},{1,65},{65,1},{129,193},{193,129... | collective-permute-start | bytes 98312 | tf_op jit(solution)/shard_map/ppermute | solution.py:29
  4.7 5.1 %collective-permute-start.5 = (bf16[64,256]{1,0:T(8,128)(2,1)S(1)}, bf16[64,256]{1,0:T(8,128)(2,1)S(1)}, u32[]{:S(2)}, u32[]{:S(2)}) collective-permute-start(bf16[64,256]{1,0:T(8,128)(2,1)S(1)} %bitcast.31), channel_id=1, source_target_pairs={{0,128},{64,192},{128,0},{192,64},{1,129},{65,193},{129,1},{193,65... | collective-permute-start | bytes 98312 | tf_op jit(solution)/shard_map/ppermute | solution.py:29
  9.8 0.0 collective-permute-start.6
  9.8 1.3 %broadcast_in_dim.8 = s32[32,2,32]{2,1,0:T(2,128)} broadcast(s32[2,32]{1,0:T(2,128)} %bitcast.40), dimensions={1,2} | broadcast | bytes 8448 | tf_op jit(solution)/shard_map/broadcast_in_dim | solution.py:279
  11.1 8.7 %all-to-all-start = ((s32[32,2,32]{2,1,0:T(2,128)}), s32[32,2,32]{2,1,0:T(2,128)S(1)}, u32[]{:S(2)}, u32[]{:S(2)}) async-start(s32[32,2,32]{2,1,0:T(2,128)} %broadcast_in_dim.8), calls=%async_computation | async-start | bytes 65536 | tf_op jit(solution)/shard_map/all_to_all | solution.py:280
  19.9 0.1 pad_add_fusion.1.at
  19.9 0.8 copy.14
  20.7 0.1 reshape.31.codes
  20.8 1.0 reshape.29.leaf
  21.9 0.6 prepare.1
  22.5 5.5 %all-to-all-done.wanted = s32[32,2,32]{2,1,0:T(2,128)S(1)} async-done(((s32[32,2,32]{2,1,0:T(2,128)}), s32[32,2,32]{2,1,0:T(2,128)S(1)}, u32[]{:S(2)}, u32[]{:S(2)}) %all-to-all-start) | async-done | bytes 8224 | tf_op jit(solution)/shard_map/all_to_all | solution.py:280
  28.0 0.0 collective-permute-done.4.refs_1_
  28.0 2.0 %pack.1 = (bf16[32,2,2,16,128]{4,3,2,1,0:T(8,128)(2,1)}, bf16[256,256]{1,0:T(8,128)(2,1)S(1)}) custom-call(s32[1]{0:T(128)} %bitcast.8.me, s32[1]{0:T(128)} %bitcast.1.part, s32[32,2,32]{2,1,0:T(2,128)S(1)} %all-to-all-done.wanted, bf16[12,2,128,128]{3,2,1,0:T(8,128)(2,1)} %table.1, bf16[64,256]{1,0:T(8,128)(2,1)S(1)} %bitcast.33, ...), custom_call_target="tpu_custom_call" | custom-call | tf_op jit(solution)/shard_map/pack/pallas_call | solution.py:106
  29.9 0.4 collective-permute-start.7
  30.3 2.6 %collective-permute-start = (bf16[9,16,256]{2,1,0:T(8,128)(2,1)S(1)}, bf16[9,16,256]{2,1,0:T(8,128)(2,1)S(1)}, u32[]{:S(2)}, u32[]{:S(2)}) collective-permute-start(bf16[9,16,256]{2,1,0:T(8,128)(2,1)S(1)} %get-tuple-element.15.refs_4_), channel_id=1, source_target_pairs={{0,4},{4,0},{1,5},{5,1},{2,6},{6,2},{3,7},{7,3},{8,12},{12,8},{9,1... | collective-permute-start | bytes 221192 | tf_op jit(solution)/shard_map/ppermute | solution.py:29
  32.9 4.7 %all-to-all-start.1 = ((bf16[32,2,2,16,128]{4,3,2,1,0:T(8,128)(2,1)}), bf16[32,2,2,16,128]{4,3,2,1,0:T(8,128)(2,1)S(1)}, u32[]{:S(2)}, u32[]{:S(2)}) async-start(bf16[32,2,2,16,128]{4,3,2,1,0:T(8,128)(2,1)} %get-tuple-element.16), calls=%async_computation.1 | async-start | bytes 1048576 | tf_op jit(solution)/shard_map/all_to_all | solution.py:292
  37.7 0.4 collective-permute-start.8
  38.2 0.2 copy-done.2
  38.4 1.2 %collective-permute-start.1 = (bf16[2,9,16,256]{3,2,1,0:T(8,128)(2,1)S(1)}, bf16[2,9,16,256]{3,2,1,0:T(8,128)(2,1)S(1)}, u32[]{:S(2)}, u32[]{:S(2)}) collective-permute-start(bf16[2,9,16,256]{3,2,1,0:T(8,128)(2,1)S(1)} %bitcast.25), channel_id=1, source_target_pairs={{0,1},{1,0},{2,3},{3,2},{4,5},{5,4},{6,7},{7,6},{8,9},{9,8},{10,11... | collective-permute-start | bytes 442376 | tf_op jit(solution)/shard_map/ppermute | solution.py:29
  39.6 2.5 %collective-permute-start.2 = (bf16[2,9,16,256]{3,2,1,0:T(8,128)(2,1)S(1)}, bf16[2,9,16,256]{3,2,1,0:T(8,128)(2,1)S(1)}, u32[]{:S(2)}, u32[]{:S(2)}) collective-permute-start(bf16[2,9,16,256]{3,2,1,0:T(8,128)(2,1)S(1)} %bitcast.26), channel_id=1, source_target_pairs={{0,2},{1,3},{2,0},{3,1},{4,6},{5,7},{6,4},{7,5},{8,10},{9,11},{10,... | collective-permute-start | bytes 442376 | tf_op jit(solution)/shard_map/ppermute | solution.py:29
  42.1 0.2 collective-permute-start.3
  42.3 0.4 collective-permute-done.1.refs_1_
  42.7 5.0 %collective-permute-done.2.refs_2_ = bf16[2,9,16,256]{3,2,1,0:T(8,128)(2,1)S(1)} collective-permute-done((bf16[2,9,16,256]{3,2,1,0:T(8,128)(2,1)S(1)}, bf16[2,9,16,256]{3,2,1,0:T(8,128)(2,1)S(1)}, u32[]{:S(2)}, u32[]{:S(2)}) %collective-permute-start.2) | collective-permute-done | bytes 147488 | tf_op jit(solution)/shard_map/ppermute | solution.py:29
  47.7 2.5 %collective-permute-done.3.refs_3_ = bf16[2,9,16,256]{3,2,1,0:T(8,128)(2,1)S(1)} collective-permute-done((bf16[2,9,16,256]{3,2,1,0:T(8,128)(2,1)S(1)}, bf16[2,9,16,256]{3,2,1,0:T(8,128)(2,1)S(1)}, u32[]{:S(2)}, u32[]{:S(2)}) %collective-permute-start.3) | collective-permute-done | bytes 147488 | tf_op jit(solution)/shard_map/ppermute | solution.py:29
  50.2 1.2 %collective-permute-done.8.second_rows = bf16[512,256]{1,0:T(8,128)(2,1)S(1)} collective-permute-done((bf16[512,256]{1,0:T(8,128)(2,1)S(1)}, bf16[512,256]{1,0:T(8,128)(2,1)S(1)}, u32[]{:S(2)}, u32[]{:S(2)}) %collective-permute-start.8) | collective-permute-done | bytes 262176 | tf_op jit(solution)/shard_map/ppermute | solution.py:29
  51.5 3.2 %all-to-all-done.1 = bf16[32,2,2,16,128]{4,3,2,1,0:T(8,128)(2,1)S(1)} async-done(((bf16[32,2,2,16,128]{4,3,2,1,0:T(8,128)(2,1)}), bf16[32,2,2,16,128]{4,3,2,1,0:T(8,128)(2,1)S(1)}, u32[]{:S(2)}, u32[]{:S(2)}) %all-to-all-start.1) | async-done | bytes 524320 | tf_op jit(solution)/shard_map/all_to_all | solution.py:292
  54.8 1.1 %choose.1 = (bf16[8,2,2,16,128]{4,3,2,1,0:T(8,128)(2,1)S(1)}, bf16[8,2,2,16,128]{4,3,2,1,0:T(8,128)(2,1)S(1)}, bf16[1024,256]{1,0:T(8,128)(2,1)S(1)}) custom-call(s32[2,16]{1,0:T(2,128)S(1)} %bitcast.34, s32[1]{0:T(128)} %bitcast.2.half, bf16[64,2,16,128]{3,2,1,0:T(8,128)(2,1)S(1)} %bitcast.24, bf16[512,256]{1,0:T(8,128)(2,1)} %copy-done.2, ...), custom_call_target="tpu_custom_call" | custom-call | tf_op jit(solution)/shard_map/choose/pallas_call | solution.py:141
  55.9 0.9 collective-permute-start.16
  56.8 0.3 collective-permute-start.12
  57.1 2.7 %collective-permute-start.10 = (bf16[8,2,2,16,128]{4,3,2,1,0:T(8,128)(2,1)S(1)}, bf16[8,2,2,16,128]{4,3,2,1,0:T(8,128)(2,1)S(1)}, u32[]{:S(2)}, u32[]{:S(2)}) collective-permute-start(bf16[8,2,2,16,128]{4,3,2,1,0:T(8,128)(2,1)S(1)} %get-tuple-element.18.refs_4_.refs_0_), channel_id=1, source_target_pairs={{0,2},{1,3},{2,0},{3,1},{4,6},{5,7},{6,4},{7,5},{8,10},{9,11},{10,... | collective-permute-start | bytes 393224 | tf_op jit(solution)/shard_map/ppermute | solution.py:29
  59.9 0.9 collective-permute-start.11
  60.7 0.1 pad_add_fusion.me
  60.8 1.3 %collective-permute-done.12.refs_4_ = bf16[8,2,2,16,128]{4,3,2,1,0:T(8,128)(2,1)S(1)} collective-permute-done((bf16[8,2,2,16,128]{4,3,2,1,0:T(8,128)(2,1)S(1)}, bf16[8,2,2,16,128]{4,3,2,1,0:T(8,128)(2,1)S(1)}, u32[]{:S(2)}, u32[]{:S(2)}) %collective-permute-start.12) | collective-permute-done | bytes 131104 | tf_op jit(solution)/shard_map/ppermute | solution.py:29
  62.1 2.2 %collective-permute-start.17 = (bf16[1024,256]{1,0:T(8,128)(2,1)S(1)}, bf16[1024,256]{1,0:T(8,128)(2,1)S(1)}, u32[]{:S(2)}, u32[]{:S(2)}) collective-permute-start(bf16[1024,256]{1,0:T(8,128)(2,1)S(1)} %get-tuple-element.20.refs_8_), channel_id=1, source_target_pairs={{0,8},{8,0},{1,9},{9,1},{2,10},{10,2},{3,11},{11,3},{4,12},{12,4},... | collective-permute-start | bytes 1572872 | tf_op jit(solution)/shard_map/ppermute | solution.py:29
  64.3 1.2 %collective-permute-start.13 = (bf16[8,2,2,16,128]{4,3,2,1,0:T(8,128)(2,1)S(1)}, bf16[8,2,2,16,128]{4,3,2,1,0:T(8,128)(2,1)S(1)}, u32[]{:S(2)}, u32[]{:S(2)}) collective-permute-start(bf16[8,2,2,16,128]{4,3,2,1,0:T(8,128)(2,1)S(1)} %collective-permute-done.12.refs_4_), channel_id=1, source_target_pairs={{0,1},{1,0},{2,3},{3,2},{4,5},{5,4},{6,7},{7,6},{8,9},{9,8},{10,11... | collective-permute-start | bytes 393224 | tf_op jit(solution)/shard_map/ppermute | solution.py:29
  65.5 1.1 %collective-permute-done.11.refs_3_ = bf16[8,2,2,16,128]{4,3,2,1,0:T(8,128)(2,1)S(1)} collective-permute-done((bf16[8,2,2,16,128]{4,3,2,1,0:T(8,128)(2,1)S(1)}, bf16[8,2,2,16,128]{4,3,2,1,0:T(8,128)(2,1)S(1)}, u32[]{:S(2)}, u32[]{:S(2)}) %collective-permute-start.11) | collective-permute-done | bytes 131104 | tf_op jit(solution)/shard_map/ppermute | solution.py:29
  66.7 1.3 %collective-permute-start.14 = (bf16[8,2,2,16,128]{4,3,2,1,0:T(8,128)(2,1)S(1)}, bf16[8,2,2,16,128]{4,3,2,1,0:T(8,128)(2,1)S(1)}, u32[]{:S(2)}, u32[]{:S(2)}) collective-permute-start(bf16[8,2,2,16,128]{4,3,2,1,0:T(8,128)(2,1)S(1)} %collective-permute-done.12.refs_4_), channel_id=1, source_target_pairs={{0,2},{1,3},{2,0},{3,1},{4,6},{5,7},{6,4},{7,5},{8,10},{9,11},{10,... | collective-permute-start | bytes 393224 | tf_op jit(solution)/shard_map/ppermute | solution.py:29
  68.0 1.8 %collective-permute-start.15 = (bf16[8,2,2,16,128]{4,3,2,1,0:T(8,128)(2,1)S(1)}, bf16[8,2,2,16,128]{4,3,2,1,0:T(8,128)(2,1)S(1)}, u32[]{:S(2)}, u32[]{:S(2)}) collective-permute-start(bf16[8,2,2,16,128]{4,3,2,1,0:T(8,128)(2,1)S(1)} %collective-permute-done.12.refs_4_), channel_id=1, source_target_pairs={{0,3},{1,2},{2,1},{3,0},{4,7},{5,6},{6,5},{7,4},{8,11},{9,10},{10,... | collective-permute-start | bytes 393224 | tf_op jit(solution)/shard_map/ppermute | solution.py:29
  69.8 1.7 %collective-permute-start.18 = (bf16[1024,256]{1,0:T(8,128)(2,1)S(1)}, bf16[1024,256]{1,0:T(8,128)(2,1)S(1)}, u32[]{:S(2)}, u32[]{:S(2)}) collective-permute-start(bf16[1024,256]{1,0:T(8,128)(2,1)S(1)} %collective-permute-done.16.refs_9_), channel_id=1, source_target_pairs={{0,8},{8,0},{1,9},{9,1},{2,10},{10,2},{3,11},{11,3},{4,12},{12,4},... | collective-permute-start | bytes 1572872 | tf_op jit(solution)/shard_map/ppermute | solution.py:29
  71.5 10.1 %weigh.1.weights = bf16[4096,2048]{1,0:T(8,128)(2,1)S(1)} custom-call(s32[1]{0:T(128)} %bitcast.1.part, bf16[2,9,16,256]{3,2,1,0:T(8,128)(2,1)} %bitcast.29, bf16[2,9,16,256]{3,2,1,0:T(8,128)(2,1)} %copy-done.4, bf16[2,9,16,256]{3,2,1,0:T(8,128)(2,1)} %copy-done.5, bf16[2,9,16,256]{3,2,1,0:T(8,128)(2,1)} %copy-done.6, ...), custom_call_target="tpu_custom_call" | custom-call | flops 17179869184 | bytes 16777216 | tf_op jit(solution)/shard_map/weigh/pallas_call | solution.py:189
  81.7 6.1 %amplitudes.1 = (f32[32,128]{1,0:T(8,128)S(1)}, f32[32,128]{1,0:T(8,128)S(1)}) custom-call(s32[2]{0:T(128)S(1)} %pad_add_fusion.me, bf16[4096,2048]{1,0:T(8,128)(2,1)S(1)} %weigh.1.weights, bf16[8,2,2,16,128]{4,3,2,1,0:T(8,128)(2,1)S(1)} %get-tuple-element.18.refs_4_.refs_0_, bf16[8,2,2,16,128]{4,3,2,1,0:T(8,128)(2,1)S(1)} %collective-permute-done.9.refs_1_, ...), custom_call_target="tpu_custom_call" | custom-call | tf_op jit(solution)/shard_map/amplitudes/pallas_call | solution.py:253
  87.8 0.1 collective-permute-start.19
  87.9 1.2 %collective-permute-done.19 = f32[32,128]{1,0:T(8,128)S(1)} collective-permute-done((f32[32,128]{1,0:T(8,128)S(1)}, f32[32,128]{1,0:T(8,128)S(1)}, u32[]{:S(2)}, u32[]{:S(2)}) %collective-permute-start.19) | collective-permute-done | bytes 16416 | tf_op jit(solution)/shard_map/ppermute | solution.py:29
  89.1 15.0 %all_to_all.19 = f32[32,1,128]{2,1,0:T(1,128)S(1)} all-to-all(f32[32,1,128]{2,1,0:T(1,128)S(1)} %bitcast.37), channel_id=1, replica_groups=mesh['z4'=2,'z2'=2,'z1'=2,'yl'=2,'core'=2,'yh'=2,'x'=4] {'z1','yh','yl',..., dimensions={0} | all-to-all | bytes 32768 | tf_op jit(solution)/shard_map/all_to_all | solution.py:323
  104.1 0.1 reduce_sum.9
  104.1 0.1 reshape.36
  104.2 0.6 copy.18
  (32 shorter events, 0.1 us)
Async XLA Ops:
  0.8 27.2 %collective-permute-start.4 = (bf16[64,256]{1,0:T(8,128)(2,1)S(1)}, bf16[64,256]{1,0:T(8,128)(2,1)S(1)}, u32[]{:S(2)}, u32[]{:S(2)}) collective-permute-start(bf16[64,256]{1,0:T(8,128)(2,1)S(1)} %bitcast.30), channel_id=1, source_target_pairs={{0,64},{64,0},{128,192},{192,128},{1,65},{65,1},{129,193},{193,129... | collective-permute-start | bytes 98312 | tf_op jit(solution)/shard_map/ppermute | solution.py:29
  4.7 23.2 %collective-permute-start.5 = (bf16[64,256]{1,0:T(8,128)(2,1)S(1)}, bf16[64,256]{1,0:T(8,128)(2,1)S(1)}, u32[]{:S(2)}, u32[]{:S(2)}) collective-permute-start(bf16[64,256]{1,0:T(8,128)(2,1)S(1)} %bitcast.31), channel_id=1, source_target_pairs={{0,128},{64,192},{128,0},{192,64},{1,129},{65,193},{129,1},{193,65... | collective-permute-start | bytes 98312 | tf_op jit(solution)/shard_map/ppermute | solution.py:29
  9.8 18.1 %collective-permute-start.6 = (bf16[64,256]{1,0:T(8,128)(2,1)S(1)}, bf16[64,256]{1,0:T(8,128)(2,1)S(1)}, u32[]{:S(2)}, u32[]{:S(2)}) collective-permute-start(bf16[64,256]{1,0:T(8,128)(2,1)S(1)} %bitcast.32), channel_id=1, source_target_pairs={{0,192},{64,128},{128,64},{192,0},{1,193},{65,129},{129,65},{193,1... | collective-permute-start | bytes 98312 | tf_op jit(solution)/shard_map/ppermute | solution.py:29
  11.1 16.8 %all-to-all-start = ((s32[32,2,32]{2,1,0:T(2,128)}), s32[32,2,32]{2,1,0:T(2,128)S(1)}, u32[]{:S(2)}, u32[]{:S(2)}) async-start(s32[32,2,32]{2,1,0:T(2,128)} %broadcast_in_dim.8), calls=%async_computation | async-start | bytes 65536 | tf_op jit(solution)/shard_map/all_to_all | solution.py:280
  29.9 7.7 %collective-permute-start.7 = (bf16[256,256]{1,0:T(8,128)(2,1)S(1)}, bf16[256,256]{1,0:T(8,128)(2,1)S(1)}, u32[]{:S(2)}, u32[]{:S(2)}) collective-permute-start(bf16[256,256]{1,0:T(8,128)(2,1)S(1)} %get-tuple-element.17), channel_id=1, source_target_pairs={{0,16},{16,0},{1,17},{17,1},{2,18},{18,2},{3,19},{19,3},{4,20},{20... | collective-permute-start | bytes 393224 | tf_op jit(solution)/shard_map/ppermute | solution.py:29
  30.3 7.9 %collective-permute-start = (bf16[9,16,256]{2,1,0:T(8,128)(2,1)S(1)}, bf16[9,16,256]{2,1,0:T(8,128)(2,1)S(1)}, u32[]{:S(2)}, u32[]{:S(2)}) collective-permute-start(bf16[9,16,256]{2,1,0:T(8,128)(2,1)S(1)} %get-tuple-element.15.refs_4_), channel_id=1, source_target_pairs={{0,4},{4,0},{1,5},{5,1},{2,6},{6,2},{3,7},{7,3},{8,12},{12,8},{9,1... | collective-permute-start | bytes 221192 | tf_op jit(solution)/shard_map/ppermute | solution.py:29
  32.9 21.8 %all-to-all-start.1 = ((bf16[32,2,2,16,128]{4,3,2,1,0:T(8,128)(2,1)}), bf16[32,2,2,16,128]{4,3,2,1,0:T(8,128)(2,1)S(1)}, u32[]{:S(2)}, u32[]{:S(2)}) async-start(bf16[32,2,2,16,128]{4,3,2,1,0:T(8,128)(2,1)} %get-tuple-element.16), calls=%async_computation.1 | async-start | bytes 1048576 | tf_op jit(solution)/shard_map/all_to_all | solution.py:292
  37.7 0.7 copy-start.2
  37.7 13.8 %collective-permute-start.8 = (bf16[512,256]{1,0:T(8,128)(2,1)S(1)}, bf16[512,256]{1,0:T(8,128)(2,1)S(1)}, u32[]{:S(2)}, u32[]{:S(2)}) collective-permute-start(bf16[512,256]{1,0:T(8,128)(2,1)S(1)} %constant_dynamic-update-slice_fusion.first_rows), channel_id=1, source_target_pairs={{0,4},{4,0},{1,5},{5,1},{2,6},{6,2},{3,7},{7,3},{8,12},{12,8},{9,1... | collective-permute-start | bytes 786440 | tf_op jit(solution)/shard_map/ppermute | solution.py:29
  38.1 16.6 %copy-start.1 = (s32[16,2]{0,1:T(2,128)S(1)}, s32[16,2]{0,1:T(2,128)}, u32[]{:S(2)}) copy-start(s32[16,2]{0,1:T(2,128)} %param.11) | copy-start | bytes 388
  38.4 16.3 %copy-start = (bf16[18,16,256]{2,1,0:T(8,128)(2,1)}, bf16[18,16,256]{2,1,0:T(8,128)(2,1)S(1)}, u32[]{:S(2)}) copy-start(bf16[18,16,256]{2,1,0:T(8,128)(2,1)S(1)} %join.1) | copy-start | bytes 442372
  38.4 4.3 %collective-permute-start.1 = (bf16[2,9,16,256]{3,2,1,0:T(8,128)(2,1)S(1)}, bf16[2,9,16,256]{3,2,1,0:T(8,128)(2,1)S(1)}, u32[]{:S(2)}, u32[]{:S(2)}) collective-permute-start(bf16[2,9,16,256]{3,2,1,0:T(8,128)(2,1)S(1)} %bitcast.25), channel_id=1, source_target_pairs={{0,1},{1,0},{2,3},{3,2},{4,5},{5,4},{6,7},{7,6},{8,9},{9,8},{10,11... | collective-permute-start | bytes 442376 | tf_op jit(solution)/shard_map/ppermute | solution.py:29
  39.6 8.1 %collective-permute-start.2 = (bf16[2,9,16,256]{3,2,1,0:T(8,128)(2,1)S(1)}, bf16[2,9,16,256]{3,2,1,0:T(8,128)(2,1)S(1)}, u32[]{:S(2)}, u32[]{:S(2)}) collective-permute-start(bf16[2,9,16,256]{3,2,1,0:T(8,128)(2,1)S(1)} %bitcast.26), channel_id=1, source_target_pairs={{0,2},{1,3},{2,0},{3,1},{4,6},{5,7},{6,4},{7,5},{8,10},{9,11},{10,... | collective-permute-start | bytes 442376 | tf_op jit(solution)/shard_map/ppermute | solution.py:29
  42.1 8.2 %collective-permute-start.3 = (bf16[2,9,16,256]{3,2,1,0:T(8,128)(2,1)S(1)}, bf16[2,9,16,256]{3,2,1,0:T(8,128)(2,1)S(1)}, u32[]{:S(2)}, u32[]{:S(2)}) collective-permute-start(bf16[2,9,16,256]{3,2,1,0:T(8,128)(2,1)S(1)} %bitcast.27), channel_id=1, source_target_pairs={{0,3},{1,2},{2,1},{3,0},{4,7},{5,6},{6,5},{7,4},{8,11},{9,10},{10,... | collective-permute-start | bytes 442376 | tf_op jit(solution)/shard_map/ppermute | solution.py:29
  42.7 12.0 %copy-start.4 = (bf16[2,9,16,256]{3,2,1,0:T(8,128)(2,1)}, bf16[2,9,16,256]{3,2,1,0:T(8,128)(2,1)S(1)}, u32[]{:S(2)}) copy-start(bf16[2,9,16,256]{3,2,1,0:T(8,128)(2,1)S(1)} %collective-permute-done.1.refs_1_) | copy-start | bytes 442372
  47.7 7.0 %copy-start.5 = (bf16[2,9,16,256]{3,2,1,0:T(8,128)(2,1)}, bf16[2,9,16,256]{3,2,1,0:T(8,128)(2,1)S(1)}, u32[]{:S(2)}) copy-start(bf16[2,9,16,256]{3,2,1,0:T(8,128)(2,1)S(1)} %collective-permute-done.2.refs_2_) | copy-start | bytes 442372
  50.2 4.5 %copy-start.6 = (bf16[2,9,16,256]{3,2,1,0:T(8,128)(2,1)}, bf16[2,9,16,256]{3,2,1,0:T(8,128)(2,1)S(1)}, u32[]{:S(2)}) copy-start(bf16[2,9,16,256]{3,2,1,0:T(8,128)(2,1)S(1)} %collective-permute-done.3.refs_3_) | copy-start | bytes 442372
  51.5 3.3 %copy-start.3 = (bf16[512,256]{1,0:T(8,128)(2,1)}, bf16[512,256]{1,0:T(8,128)(2,1)S(1)}, u32[]{:S(2)}) copy-start(bf16[512,256]{1,0:T(8,128)(2,1)S(1)} %collective-permute-done.8.second_rows) | copy-start | bytes 786436
  55.9 13.9 %collective-permute-start.16 = (bf16[1024,256]{1,0:T(8,128)(2,1)S(1)}, bf16[1024,256]{1,0:T(8,128)(2,1)S(1)}, u32[]{:S(2)}, u32[]{:S(2)}) collective-permute-start(bf16[1024,256]{1,0:T(8,128)(2,1)S(1)} %get-tuple-element.20.refs_8_), channel_id=1, source_target_pairs={{0,32},{32,0},{1,33},{33,1},{2,34},{34,2},{3,35},{35,3},{4,36},{36... | collective-permute-start | bytes 1572872 | tf_op jit(solution)/shard_map/ppermute | solution.py:29
  56.8 5.3 %collective-permute-start.12 = (bf16[8,2,2,16,128]{4,3,2,1,0:T(8,128)(2,1)S(1)}, bf16[8,2,2,16,128]{4,3,2,1,0:T(8,128)(2,1)S(1)}, u32[]{:S(2)}, u32[]{:S(2)}) collective-permute-start(bf16[8,2,2,16,128]{4,3,2,1,0:T(8,128)(2,1)S(1)} %get-tuple-element.19), channel_id=1, source_target_pairs={{0,4},{4,0},{1,5},{5,1},{2,6},{6,2},{3,7},{7,3},{8,12},{12,8},{9,1... | collective-permute-start | bytes 393224 | tf_op jit(solution)/shard_map/ppermute | solution.py:29
  57.1 7.2 %collective-permute-start.10 = (bf16[8,2,2,16,128]{4,3,2,1,0:T(8,128)(2,1)S(1)}, bf16[8,2,2,16,128]{4,3,2,1,0:T(8,128)(2,1)S(1)}, u32[]{:S(2)}, u32[]{:S(2)}) collective-permute-start(bf16[8,2,2,16,128]{4,3,2,1,0:T(8,128)(2,1)S(1)} %get-tuple-element.18.refs_4_.refs_0_), channel_id=1, source_target_pairs={{0,2},{1,3},{2,0},{3,1},{4,6},{5,7},{6,4},{7,5},{8,10},{9,11},{10,... | collective-permute-start | bytes 393224 | tf_op jit(solution)/shard_map/ppermute | solution.py:29
  59.9 6.8 %collective-permute-start.11 = (bf16[8,2,2,16,128]{4,3,2,1,0:T(8,128)(2,1)S(1)}, bf16[8,2,2,16,128]{4,3,2,1,0:T(8,128)(2,1)S(1)}, u32[]{:S(2)}, u32[]{:S(2)}) collective-permute-start(bf16[8,2,2,16,128]{4,3,2,1,0:T(8,128)(2,1)S(1)} %get-tuple-element.18.refs_4_.refs_0_), channel_id=1, source_target_pairs={{0,3},{1,2},{2,1},{3,0},{4,7},{5,6},{6,5},{7,4},{8,11},{9,10},{10,... | collective-permute-start | bytes 393224 | tf_op jit(solution)/shard_map/ppermute | solution.py:29
  60.7 7.3 %collective-permute-start.9 = (bf16[8,2,2,16,128]{4,3,2,1,0:T(8,128)(2,1)S(1)}, bf16[8,2,2,16,128]{4,3,2,1,0:T(8,128)(2,1)S(1)}, u32[]{:S(2)}, u32[]{:S(2)}) collective-permute-start(bf16[8,2,2,16,128]{4,3,2,1,0:T(8,128)(2,1)S(1)} %get-tuple-element.18.refs_4_.refs_0_), channel_id=1, source_target_pairs={{0,1},{1,0},{2,3},{3,2},{4,5},{5,4},{6,7},{7,6},{8,9},{9,8},{10,11... | collective-permute-start | bytes 393224 | tf_op jit(solution)/shard_map/ppermute | solution.py:29
  62.1 19.6 %collective-permute-start.17 = (bf16[1024,256]{1,0:T(8,128)(2,1)S(1)}, bf16[1024,256]{1,0:T(8,128)(2,1)S(1)}, u32[]{:S(2)}, u32[]{:S(2)}) collective-permute-start(bf16[1024,256]{1,0:T(8,128)(2,1)S(1)} %get-tuple-element.20.refs_8_), channel_id=1, source_target_pairs={{0,8},{8,0},{1,9},{9,1},{2,10},{10,2},{3,11},{11,3},{4,12},{12,4},... | collective-permute-start | bytes 1572872 | tf_op jit(solution)/shard_map/ppermute | solution.py:29
  64.3 17.3 %collective-permute-start.13 = (bf16[8,2,2,16,128]{4,3,2,1,0:T(8,128)(2,1)S(1)}, bf16[8,2,2,16,128]{4,3,2,1,0:T(8,128)(2,1)S(1)}, u32[]{:S(2)}, u32[]{:S(2)}) collective-permute-start(bf16[8,2,2,16,128]{4,3,2,1,0:T(8,128)(2,1)S(1)} %collective-permute-done.12.refs_4_), channel_id=1, source_target_pairs={{0,1},{1,0},{2,3},{3,2},{4,5},{5,4},{6,7},{7,6},{8,9},{9,8},{10,11... | collective-permute-start | bytes 393224 | tf_op jit(solution)/shard_map/ppermute | solution.py:29
  66.7 15.0 %collective-permute-start.14 = (bf16[8,2,2,16,128]{4,3,2,1,0:T(8,128)(2,1)S(1)}, bf16[8,2,2,16,128]{4,3,2,1,0:T(8,128)(2,1)S(1)}, u32[]{:S(2)}, u32[]{:S(2)}) collective-permute-start(bf16[8,2,2,16,128]{4,3,2,1,0:T(8,128)(2,1)S(1)} %collective-permute-done.12.refs_4_), channel_id=1, source_target_pairs={{0,2},{1,3},{2,0},{3,1},{4,6},{5,7},{6,4},{7,5},{8,10},{9,11},{10,... | collective-permute-start | bytes 393224 | tf_op jit(solution)/shard_map/ppermute | solution.py:29
  68.0 13.7 %collective-permute-start.15 = (bf16[8,2,2,16,128]{4,3,2,1,0:T(8,128)(2,1)S(1)}, bf16[8,2,2,16,128]{4,3,2,1,0:T(8,128)(2,1)S(1)}, u32[]{:S(2)}, u32[]{:S(2)}) collective-permute-start(bf16[8,2,2,16,128]{4,3,2,1,0:T(8,128)(2,1)S(1)} %collective-permute-done.12.refs_4_), channel_id=1, source_target_pairs={{0,3},{1,2},{2,1},{3,0},{4,7},{5,6},{6,5},{7,4},{8,11},{9,10},{10,... | collective-permute-start | bytes 393224 | tf_op jit(solution)/shard_map/ppermute | solution.py:29
  69.8 11.9 %collective-permute-start.18 = (bf16[1024,256]{1,0:T(8,128)(2,1)S(1)}, bf16[1024,256]{1,0:T(8,128)(2,1)S(1)}, u32[]{:S(2)}, u32[]{:S(2)}) collective-permute-start(bf16[1024,256]{1,0:T(8,128)(2,1)S(1)} %collective-permute-done.16.refs_9_), channel_id=1, source_target_pairs={{0,8},{8,0},{1,9},{9,1},{2,10},{10,2},{3,11},{11,3},{4,12},{12,4},... | collective-permute-start | bytes 1572872 | tf_op jit(solution)/shard_map/ppermute | solution.py:29
  87.8 1.2 %collective-permute-start.19 = (f32[32,128]{1,0:T(8,128)S(1)}, f32[32,128]{1,0:T(8,128)S(1)}, u32[]{:S(2)}, u32[]{:S(2)}) collective-permute-start(f32[32,128]{1,0:T(8,128)S(1)} %get-tuple-element.22), channel_id=1, source_target_pairs={{0,8},{8,0},{1,9},{9,1},{2,10},{10,2},{3,11},{11,3},{4,12},{12,4},... | collective-permute-start | bytes 49160 | tf_op jit(solution)/shard_map/ppermute | solution.py:29

commit v4 on v3

--- a/solution.py
+++ b/solution.py
@@ -122,31 +122,27 @@
     )(me, part, wanted, in_hbm(table), *pieces, *ready)
 
 
-def choose_kernel(terms, half, slots, first_rows, second_rows, *refs):
-    kept, given, rows = refs[-3:]
+def choose_kernel(terms, half, slots, *refs):
+    kept, given = refs[-2:]
     slices = kept.shape[0]
     for out, first in ((kept, half[0] * slices), (given, (1 - half[0]) * slices)):
         for s in range(slices):
             for t in range(2):
                 out[s, t] = slots[terms[t, first + s]]
-    count = first_rows.shape[0]
-    rows[:count] = first_rows[...]
-    rows[count:] = second_rows[...]
-
-
-def choose(terms, half, slots, first_rows, second_rows, ready):
+
+
+def choose(terms, half, slots, ready):
     shape = (terms.shape[1] // SPLIT, 2) + slots.shape[1:]
-    count, pair = first_rows.shape
-    scalars = [pl.BlockSpec(memory_space=pltpu.SMEM)] * 2
     return pl.pallas_call(
         choose_kernel,
-        out_shape=(jax.ShapeDtypeStruct(shape, BF),) * 2
-        + (jax.ShapeDtypeStruct((2 * count, pair), BF),),
-        in_specs=scalars + [IN_VMEM] * 3 + [pl.BlockSpec(memory_space=pl.ANY)] * len(ready),
-        out_specs=(IN_VMEM,) * 3,
+        out_shape=(jax.ShapeDtypeStruct(shape, BF),) * 2,
+        in_specs=[pl.BlockSpec(memory_space=pltpu.SMEM)] * 2
+        + [IN_VMEM]
+        + [pl.BlockSpec(memory_space=pl.ANY)] * len(ready),
+        out_specs=(IN_VMEM,) * 2,
         compiler_params=pltpu.CompilerParams(vmem_limit_bytes=VMEM),
         name="choose",
-    )(terms, half, slots, first_rows, second_rows, *ready)
+    )(terms, half, slots, *ready)
 
 
 def weight_kernel(part, *refs):
@@ -297,23 +293,16 @@
     leaf = [leaf] + [swap(leaf, "x", bit) for bit in range(1, lax.axis_size("x"))]
     leaf = [in_hbm(a) for a in leaf]
 
-    rows_here = jnp.concatenate([rows_here, swap(rows_here, "yl")], axis=0)
-    rows_there = swap(rows_here, "yh")
-
-    kept, given, rows_here = choose(
-        slice_terms.T,
-        yh.reshape(1),
-        slots,
-        in_hbm(rows_here),
-        in_hbm(rows_there),
-        tuple(leaf),
-    )
+    rows_here = join([rows_here, swap(rows_here, "yl")])
+
+    kept, given = choose(slice_terms.T, yh.reshape(1), slots, tuple(leaf))
     got = swap(given, "yh")
     pieces = []
     for piece in (kept, got):
         pieces += [piece] + [swap(piece, "x", bit) for bit in range(1, lax.axis_size("x"))]
     weights = weigh(part.reshape(1), leaf, kept)
 
+    rows_here = join([rows_here, swap(rows_here, "yh")], (kept,))
     rows_here = [rows_here, swap(rows_here, "z1")]
     rows_here = rows_here + [swap(a, "core") for a in rows_here]
 

time: 105 us -> 104 us (level)
    ppermute x20, waiting for transfers between devices: 12.8 us -> 10.4 us  [swap(): return lax.ppermute(a, axis, [(i, i ^ bit) for i in range(count)])]
    all_to_all x1, waiting for transfers between devices: 3.24 us -> 4.81 us  [body(): slots = lax.all_to_all(sent, CUTS, 0, 0, tiled=True)]
  transfers between devices with their start and end apart: 22 -> 22, of which waited for: 9 -> 8; matrix products, arithmetic and copies ran while one was open for 3% -> 3% of each run, Pallas kernels for 10% -> 11%
where the time goes in v4:
time: 104 us
  starting transfers between devices  43.6 us (42%)
  waiting for transfers between devices  20.6 us (20%)
  Pallas kernels  19.6 us (19%)
  blocking collectives  15 us (14%)
  local copies, waits for them, and re-layouts  4.69 us (5%)
    ppermute x20, starting transfers between devices, swap(): return lax.ppermute(a, axis, [(i, i ^ bit) for i in range(count)])  30.2 us
    all_to_all x1, blocking collectives, body(): amps = lax.all_to_all(amps, order, 0, 0, tiled=True)  15 us
    ppermute x20, waiting for transfers between devices, swap(): return lax.ppermute(a, axis, [(i, i ^ bit) for i in range(count)])  10.4 us
    pallas_call x1, Pallas kernels, weigh(): pl.pallas_call(weight_kernel, out_shape=pltpu.VMEM((rows, depth), BF), in...  10.1 us
    all_to_all x1, starting transfers between devices, body(): wanted = lax.all_to_all(wanted, CUTS, 0, 0, tiled=True)  8.7 us
    pallas_call x1, Pallas kernels, amplitudes_of(): pl.pallas_call(amp_kernel, out_shape=(jax.ShapeDtypeStruct((rows // each...  6.2 us
    all_to_all x1, waiting for transfers between devices, body(): wanted = lax.all_to_all(wanted, CUTS, 0, 0, tiled=True)  5.45 us
    all_to_all x1, waiting for transfers between devices, body(): slots = lax.all_to_all(sent, CUTS, 0, 0, tiled=True)  4.81 us
  transfers between devices with their start and end apart: 22, of which 8 were waited for; matrix products, arithmetic and copies ran while one was open for 3% of the time, Pallas kernels for 11%

profile of v4, /device:TPU:1, one launch (start us, length us, event | category | flops | bytes accessed | tf_op | source)
XLA Modules:
  0.0 104.0 jit_solution(9619131840559126393)
XLA Ops:
  0.0 0.8 copy.16
  0.8 3.9 %collective-permute-start.4 = (bf16[64,256]{1,0:T(8,128)(2,1)S(1)}, bf16[64,256]{1,0:T(8,128)(2,1)S(1)}, u32[]{:S(2)}, u32[]{:S(2)}) collective-permute-start(bf16[64,256]{1,0:T(8,128)(2,1)S(1)} %bitcast.30), channel_id=1, source_target_pairs={{0,64},{64,0},{128,192},{192,128},{1,65},{65,1},{129,193},{193,129... | collective-permute-start | bytes 98312 | tf_op jit(solution)/shard_map/ppermute | solution.py:29
  4.7 5.1 %collective-permute-start.5 = (bf16[64,256]{1,0:T(8,128)(2,1)S(1)}, bf16[64,256]{1,0:T(8,128)(2,1)S(1)}, u32[]{:S(2)}, u32[]{:S(2)}) collective-permute-start(bf16[64,256]{1,0:T(8,128)(2,1)S(1)} %bitcast.31), channel_id=1, source_target_pairs={{0,128},{64,192},{128,0},{192,64},{1,129},{65,193},{129,1},{193,65... | collective-permute-start | bytes 98312 | tf_op jit(solution)/shard_map/ppermute | solution.py:29
  9.8 0.0 collective-permute-start.6
  9.8 1.3 %broadcast_in_dim.8 = s32[32,2,32]{2,1,0:T(2,128)} broadcast(s32[2,32]{1,0:T(2,128)} %bitcast.40), dimensions={1,2} | broadcast | bytes 8448 | tf_op jit(solution)/shard_map/broadcast_in_dim | solution.py:275
  11.1 8.7 %all-to-all-start = ((s32[32,2,32]{2,1,0:T(2,128)}), s32[32,2,32]{2,1,0:T(2,128)S(1)}, u32[]{:S(2)}, u32[]{:S(2)}) async-start(s32[32,2,32]{2,1,0:T(2,128)} %broadcast_in_dim.8), calls=%async_computation | async-start | bytes 65536 | tf_op jit(solution)/shard_map/all_to_all | solution.py:276
  19.8 0.1 pad_add_fusion.1.at
  19.9 0.8 copy.14
  20.7 0.1 reshape.31.codes
  20.8 1.0 reshape.29.leaf
  21.9 0.6 prepare.1
  22.5 5.5 %all-to-all-done.wanted = s32[32,2,32]{2,1,0:T(2,128)S(1)} async-done(((s32[32,2,32]{2,1,0:T(2,128)}), s32[32,2,32]{2,1,0:T(2,128)S(1)}, u32[]{:S(2)}, u32[]{:S(2)}) %all-to-all-start) | async-done | bytes 8224 | tf_op jit(solution)/shard_map/all_to_all | solution.py:276
  27.9 0.0 collective-permute-done.5.refs_2_
  28.0 0.0 collective-permute-done.6.refs_3_
  28.0 2.0 %pack.1 = (bf16[32,2,2,16,128]{4,3,2,1,0:T(8,128)(2,1)}, bf16[256,256]{1,0:T(8,128)(2,1)S(1)}) custom-call(s32[1]{0:T(128)} %bitcast.8.me, s32[1]{0:T(128)} %bitcast.1.part, s32[32,2,32]{2,1,0:T(2,128)S(1)} %all-to-all-done.wanted, bf16[12,2,128,128]{3,2,1,0:T(8,128)(2,1)} %table.1, bf16[64,256]{1,0:T(8,128)(2,1)S(1)} %bitcast.33, ...), custom_call_target="tpu_custom_call" | custom-call | tf_op jit(solution)/shard_map/pack/pallas_call | solution.py:106
  29.9 0.3 collective-permute-start.14
  30.3 2.6 %collective-permute-start = (bf16[9,16,256]{2,1,0:T(8,128)(2,1)S(1)}, bf16[9,16,256]{2,1,0:T(8,128)(2,1)S(1)}, u32[]{:S(2)}, u32[]{:S(2)}) collective-permute-start(bf16[9,16,256]{2,1,0:T(8,128)(2,1)S(1)} %get-tuple-element.14.refs_4_), channel_id=1, source_target_pairs={{0,4},{4,0},{1,5},{5,1},{2,6},{6,2},{3,7},{7,3},{8,12},{12,8},{9,1... | collective-permute-start | bytes 221192 | tf_op jit(solution)/shard_map/ppermute | solution.py:29
  32.9 4.7 %all-to-all-start.1 = ((bf16[32,2,2,16,128]{4,3,2,1,0:T(8,128)(2,1)}), bf16[32,2,2,16,128]{4,3,2,1,0:T(8,128)(2,1)S(1)}, u32[]{:S(2)}, u32[]{:S(2)}) async-start(bf16[32,2,2,16,128]{4,3,2,1,0:T(8,128)(2,1)} %get-tuple-element.15), calls=%async_computation.1 | async-start | bytes 1048576 | tf_op jit(solution)/shard_map/all_to_all | solution.py:288
  37.7 0.4 collective-permute-start.15
  38.1 1.3 %collective-permute-start.1 = (bf16[2,9,16,256]{3,2,1,0:T(8,128)(2,1)S(1)}, bf16[2,9,16,256]{3,2,1,0:T(8,128)(2,1)S(1)}, u32[]{:S(2)}, u32[]{:S(2)}) collective-permute-start(bf16[2,9,16,256]{3,2,1,0:T(8,128)(2,1)S(1)} %bitcast.25), channel_id=1, source_target_pairs={{0,1},{1,0},{2,3},{3,2},{4,5},{5,4},{6,7},{7,6},{8,9},{9,8},{10,11... | collective-permute-start | bytes 442376 | tf_op jit(solution)/shard_map/ppermute | solution.py:29
  39.4 2.5 %collective-permute-start.2 = (bf16[2,9,16,256]{3,2,1,0:T(8,128)(2,1)S(1)}, bf16[2,9,16,256]{3,2,1,0:T(8,128)(2,1)S(1)}, u32[]{:S(2)}, u32[]{:S(2)}) collective-permute-start(bf16[2,9,16,256]{3,2,1,0:T(8,128)(2,1)S(1)} %bitcast.26), channel_id=1, source_target_pairs={{0,2},{1,3},{2,0},{3,1},{4,6},{5,7},{6,4},{7,5},{8,10},{9,11},{10,... | collective-permute-start | bytes 442376 | tf_op jit(solution)/shard_map/ppermute | solution.py:29
  41.9 0.2 collective-permute-start.3
  42.1 0.4 collective-permute-done.1.refs_1_
  42.5 4.9 %collective-permute-done.2.refs_2_ = bf16[2,9,16,256]{3,2,1,0:T(8,128)(2,1)S(1)} collective-permute-done((bf16[2,9,16,256]{3,2,1,0:T(8,128)(2,1)S(1)}, bf16[2,9,16,256]{3,2,1,0:T(8,128)(2,1)S(1)}, u32[]{:S(2)}, u32[]{:S(2)}) %collective-permute-start.2) | collective-permute-done | bytes 147488 | tf_op jit(solution)/shard_map/ppermute | solution.py:29
  47.4 2.5 %collective-permute-done.3.refs_3_ = bf16[2,9,16,256]{3,2,1,0:T(8,128)(2,1)S(1)} collective-permute-done((bf16[2,9,16,256]{3,2,1,0:T(8,128)(2,1)S(1)}, bf16[2,9,16,256]{3,2,1,0:T(8,128)(2,1)S(1)}, u32[]{:S(2)}, u32[]{:S(2)}) %collective-permute-start.3) | collective-permute-done | bytes 147488 | tf_op jit(solution)/shard_map/ppermute | solution.py:29
  49.9 4.8 %all-to-all-done.1 = bf16[32,2,2,16,128]{4,3,2,1,0:T(8,128)(2,1)S(1)} async-done(((bf16[32,2,2,16,128]{4,3,2,1,0:T(8,128)(2,1)}), bf16[32,2,2,16,128]{4,3,2,1,0:T(8,128)(2,1)S(1)}, u32[]{:S(2)}, u32[]{:S(2)}) %all-to-all-start.1) | async-done | bytes 524320 | tf_op jit(solution)/shard_map/all_to_all | solution.py:288
  54.8 0.6 choose.1
  55.4 0.9 collective-permute-start.16
  56.3 0.3 collective-permute-start.10
  56.7 1.2 %collective-permute-start.7 = (bf16[8,2,2,16,128]{4,3,2,1,0:T(8,128)(2,1)S(1)}, bf16[8,2,2,16,128]{4,3,2,1,0:T(8,128)(2,1)S(1)}, u32[]{:S(2)}, u32[]{:S(2)}) collective-permute-start(bf16[8,2,2,16,128]{4,3,2,1,0:T(8,128)(2,1)S(1)} %get-tuple-element.16.refs_4_.refs_2_.refs_0_), channel_id=1, source_target_pairs={{0,1},{1,0},{2,3},{3,2},{4,5},{5,4},{6,7},{7,6},{8,9},{9,8},{10,11... | collective-permute-start | bytes 393224 | tf_op jit(solution)/shard_map/ppermute | solution.py:29
  57.9 2.5 %collective-permute-start.8 = (bf16[8,2,2,16,128]{4,3,2,1,0:T(8,128)(2,1)S(1)}, bf16[8,2,2,16,128]{4,3,2,1,0:T(8,128)(2,1)S(1)}, u32[]{:S(2)}, u32[]{:S(2)}) collective-permute-start(bf16[8,2,2,16,128]{4,3,2,1,0:T(8,128)(2,1)S(1)} %get-tuple-element.16.refs_4_.refs_2_.refs_0_), channel_id=1, source_target_pairs={{0,2},{1,3},{2,0},{3,1},{4,6},{5,7},{6,4},{7,5},{8,10},{9,11},{10,... | collective-permute-start | bytes 393224 | tf_op jit(solution)/shard_map/ppermute | solution.py:29
  60.3 0.2 collective-permute-start.9
  60.5 0.1 pad_add_fusion.me
  60.6 1.0 collective-permute-done.10.refs_4_
  61.6 2.2 %collective-permute-start.17 = (bf16[1024,256]{1,0:T(8,128)(2,1)S(1)}, bf16[1024,256]{1,0:T(8,128)(2,1)S(1)}, u32[]{:S(2)}, u32[]{:S(2)}) collective-permute-start(bf16[1024,256]{1,0:T(8,128)(2,1)S(1)} %join.5.refs_8_), channel_id=1, source_target_pairs={{0,8},{8,0},{1,9},{9,1},{2,10},{10,2},{3,11},{11,3},{4,12},{12,4},... | collective-permute-start | bytes 1572872 | tf_op jit(solution)/shard_map/ppermute | solution.py:29
  63.9 1.2 %collective-permute-start.11 = (bf16[8,2,2,16,128]{4,3,2,1,0:T(8,128)(2,1)S(1)}, bf16[8,2,2,16,128]{4,3,2,1,0:T(8,128)(2,1)S(1)}, u32[]{:S(2)}, u32[]{:S(2)}) collective-permute-start(bf16[8,2,2,16,128]{4,3,2,1,0:T(8,128)(2,1)S(1)} %collective-permute-done.10.refs_4_), channel_id=1, source_target_pairs={{0,1},{1,0},{2,3},{3,2},{4,5},{5,4},{6,7},{7,6},{8,9},{9,8},{10,11... | collective-permute-start | bytes 393224 | tf_op jit(solution)/shard_map/ppermute | solution.py:29
  65.1 2.5 %collective-permute-start.12 = (bf16[8,2,2,16,128]{4,3,2,1,0:T(8,128)(2,1)S(1)}, bf16[8,2,2,16,128]{4,3,2,1,0:T(8,128)(2,1)S(1)}, u32[]{:S(2)}, u32[]{:S(2)}) collective-permute-start(bf16[8,2,2,16,128]{4,3,2,1,0:T(8,128)(2,1)S(1)} %collective-permute-done.10.refs_4_), channel_id=1, source_target_pairs={{0,2},{1,3},{2,0},{3,1},{4,6},{5,7},{6,4},{7,5},{8,10},{9,11},{10,... | collective-permute-start | bytes 393224 | tf_op jit(solution)/shard_map/ppermute | solution.py:29
  67.5 0.3 collective-permute-done.9.refs_3_
  67.8 0.8 collective-permute-start.13
  68.6 2.0 %collective-permute-start.18 = (bf16[1024,256]{1,0:T(8,128)(2,1)S(1)}, bf16[1024,256]{1,0:T(8,128)(2,1)S(1)}, u32[]{:S(2)}, u32[]{:S(2)}) collective-permute-start(bf16[1024,256]{1,0:T(8,128)(2,1)S(1)} %collective-permute-done.16.refs_9_), channel_id=1, source_target_pairs={{0,8},{8,0},{1,9},{9,1},{2,10},{10,2},{3,11},{11,3},{4,12},{12,4},... | collective-permute-start | bytes 1572872 | tf_op jit(solution)/shard_map/ppermute | solution.py:29
  70.6 10.1 %weigh.1.weights = bf16[4096,2048]{1,0:T(8,128)(2,1)S(1)} custom-call(s32[1]{0:T(128)} %bitcast.1.part, bf16[2,9,16,256]{3,2,1,0:T(8,128)(2,1)} %bitcast.29, bf16[2,9,16,256]{3,2,1,0:T(8,128)(2,1)} %copy-done.2, bf16[2,9,16,256]{3,2,1,0:T(8,128)(2,1)} %copy-done.3, bf16[2,9,16,256]{3,2,1,0:T(8,128)(2,1)} %copy-done.4, ...), custom_call_target="tpu_custom_call" | custom-call | flops 17179869184 | bytes 16777216 | tf_op jit(solution)/shard_map/weigh/pallas_call | solution.py:185
  80.7 6.2 %amplitudes.1 = (f32[32,128]{1,0:T(8,128)S(1)}, f32[32,128]{1,0:T(8,128)S(1)}) custom-call(s32[2]{0:T(128)S(1)} %pad_add_fusion.me, bf16[4096,2048]{1,0:T(8,128)(2,1)S(1)} %weigh.1.weights, bf16[8,2,2,16,128]{4,3,2,1,0:T(8,128)(2,1)S(1)} %get-tuple-element.16.refs_4_.refs_2_.refs_0_, bf16[8,2,2,16,128]{4,3,2,1,0:T(8,128)(2,1)S(1)} %collective-permute-done.7.refs_1_, ...), custom_call_target="tpu_custom_call" | custom-call | tf_op jit(solution)/shard_map/amplitudes/pallas_call | solution.py:249
  86.9 0.1 collective-permute-start.19
  87.0 1.2 %collective-permute-done.19 = f32[32,128]{1,0:T(8,128)S(1)} collective-permute-done((f32[32,128]{1,0:T(8,128)S(1)}, f32[32,128]{1,0:T(8,128)S(1)}, u32[]{:S(2)}, u32[]{:S(2)}) %collective-permute-start.19) | collective-permute-done | bytes 16416 | tf_op jit(solution)/shard_map/ppermute | solution.py:29
  88.2 15.0 %all_to_all.19 = f32[32,1,128]{2,1,0:T(1,128)S(1)} all-to-all(f32[32,1,128]{2,1,0:T(1,128)S(1)} %bitcast.37), channel_id=1, replica_groups=mesh['z4'=2,'z2'=2,'z1'=2,'yl'=2,'core'=2,'yh'=2,'x'=4] {'z1','yh','yl',..., dimensions={0} | all-to-all | bytes 32768 | tf_op jit(solution)/shard_map/all_to_all | solution.py:312
  103.2 0.1 reduce_sum.9
  103.3 0.1 reshape.36
  103.4 0.6 copy.18
  (28 shorter events, 0.1 us)
Async XLA Ops:
  0.8 27.1 %collective-permute-start.4 = (bf16[64,256]{1,0:T(8,128)(2,1)S(1)}, bf16[64,256]{1,0:T(8,128)(2,1)S(1)}, u32[]{:S(2)}, u32[]{:S(2)}) collective-permute-start(bf16[64,256]{1,0:T(8,128)(2,1)S(1)} %bitcast.30), channel_id=1, source_target_pairs={{0,64},{64,0},{128,192},{192,128},{1,65},{65,1},{129,193},{193,129... | collective-permute-start | bytes 98312 | tf_op jit(solution)/shard_map/ppermute | solution.py:29
  4.7 23.2 %collective-permute-start.5 = (bf16[64,256]{1,0:T(8,128)(2,1)S(1)}, bf16[64,256]{1,0:T(8,128)(2,1)S(1)}, u32[]{:S(2)}, u32[]{:S(2)}) collective-permute-start(bf16[64,256]{1,0:T(8,128)(2,1)S(1)} %bitcast.31), channel_id=1, source_target_pairs={{0,128},{64,192},{128,0},{192,64},{1,129},{65,193},{129,1},{193,65... | collective-permute-start | bytes 98312 | tf_op jit(solution)/shard_map/ppermute | solution.py:29
  9.8 18.1 %collective-permute-start.6 = (bf16[64,256]{1,0:T(8,128)(2,1)S(1)}, bf16[64,256]{1,0:T(8,128)(2,1)S(1)}, u32[]{:S(2)}, u32[]{:S(2)}) collective-permute-start(bf16[64,256]{1,0:T(8,128)(2,1)S(1)} %bitcast.32), channel_id=1, source_target_pairs={{0,192},{64,128},{128,64},{192,0},{1,193},{65,129},{129,65},{193,1... | collective-permute-start | bytes 98312 | tf_op jit(solution)/shard_map/ppermute | solution.py:29
  11.1 16.8 %all-to-all-start = ((s32[32,2,32]{2,1,0:T(2,128)}), s32[32,2,32]{2,1,0:T(2,128)S(1)}, u32[]{:S(2)}, u32[]{:S(2)}) async-start(s32[32,2,32]{2,1,0:T(2,128)} %broadcast_in_dim.8), calls=%async_computation | async-start | bytes 65536 | tf_op jit(solution)/shard_map/all_to_all | solution.py:276
  29.9 7.7 %collective-permute-start.14 = (bf16[256,256]{1,0:T(8,128)(2,1)S(1)}, bf16[256,256]{1,0:T(8,128)(2,1)S(1)}, u32[]{:S(2)}, u32[]{:S(2)}) collective-permute-start(bf16[256,256]{1,0:T(8,128)(2,1)S(1)} %get-tuple-element.18.refs_0_), channel_id=1, source_target_pairs={{0,16},{16,0},{1,17},{17,1},{2,18},{18,2},{3,19},{19,3},{4,20},{20... | collective-permute-start | bytes 393224 | tf_op jit(solution)/shard_map/ppermute | solution.py:29
  30.3 7.8 %collective-permute-start = (bf16[9,16,256]{2,1,0:T(8,128)(2,1)S(1)}, bf16[9,16,256]{2,1,0:T(8,128)(2,1)S(1)}, u32[]{:S(2)}, u32[]{:S(2)}) collective-permute-start(bf16[9,16,256]{2,1,0:T(8,128)(2,1)S(1)} %get-tuple-element.14.refs_4_), channel_id=1, source_target_pairs={{0,4},{4,0},{1,5},{5,1},{2,6},{6,2},{3,7},{7,3},{8,12},{12,8},{9,1... | collective-permute-start | bytes 221192 | tf_op jit(solution)/shard_map/ppermute | solution.py:29
  32.9 21.8 %all-to-all-start.1 = ((bf16[32,2,2,16,128]{4,3,2,1,0:T(8,128)(2,1)}), bf16[32,2,2,16,128]{4,3,2,1,0:T(8,128)(2,1)S(1)}, u32[]{:S(2)}, u32[]{:S(2)}) async-start(bf16[32,2,2,16,128]{4,3,2,1,0:T(8,128)(2,1)} %get-tuple-element.15), calls=%async_computation.1 | async-start | bytes 1048576 | tf_op jit(solution)/shard_map/all_to_all | solution.py:288
  37.7 17.7 %collective-permute-start.15 = (bf16[512,256]{1,0:T(8,128)(2,1)S(1)}, bf16[512,256]{1,0:T(8,128)(2,1)S(1)}, u32[]{:S(2)}, u32[]{:S(2)}) collective-permute-start(bf16[512,256]{1,0:T(8,128)(2,1)S(1)} %join.4.refs_0_), channel_id=1, source_target_pairs={{0,4},{4,0},{1,5},{5,1},{2,6},{6,2},{3,7},{7,3},{8,12},{12,8},{9,1... | collective-permute-start | bytes 786440 | tf_op jit(solution)/shard_map/ppermute | solution.py:29
  38.1 16.6 %copy-start.1 = (s32[16,2]{0,1:T(2,128)S(1)}, s32[16,2]{0,1:T(2,128)}, u32[]{:S(2)}) copy-start(s32[16,2]{0,1:T(2,128)} %param.11) | copy-start | bytes 388
  38.1 16.6 %copy-start = (bf16[18,16,256]{2,1,0:T(8,128)(2,1)}, bf16[18,16,256]{2,1,0:T(8,128)(2,1)S(1)}, u32[]{:S(2)}) copy-start(bf16[18,16,256]{2,1,0:T(8,128)(2,1)S(1)} %join.3) | copy-start | bytes 442372
  38.1 4.4 %collective-permute-start.1 = (bf16[2,9,16,256]{3,2,1,0:T(8,128)(2,1)S(1)}, bf16[2,9,16,256]{3,2,1,0:T(8,128)(2,1)S(1)}, u32[]{:S(2)}, u32[]{:S(2)}) collective-permute-start(bf16[2,9,16,256]{3,2,1,0:T(8,128)(2,1)S(1)} %bitcast.25), channel_id=1, source_target_pairs={{0,1},{1,0},{2,3},{3,2},{4,5},{5,4},{6,7},{7,6},{8,9},{9,8},{10,11... | collective-permute-start | bytes 442376 | tf_op jit(solution)/shard_map/ppermute | solution.py:29
  39.4 7.9 %collective-permute-start.2 = (bf16[2,9,16,256]{3,2,1,0:T(8,128)(2,1)S(1)}, bf16[2,9,16,256]{3,2,1,0:T(8,128)(2,1)S(1)}, u32[]{:S(2)}, u32[]{:S(2)}) collective-permute-start(bf16[2,9,16,256]{3,2,1,0:T(8,128)(2,1)S(1)} %bitcast.26), channel_id=1, source_target_pairs={{0,2},{1,3},{2,0},{3,1},{4,6},{5,7},{6,4},{7,5},{8,10},{9,11},{10,... | collective-permute-start | bytes 442376 | tf_op jit(solution)/shard_map/ppermute | solution.py:29
  41.9 8.0 %collective-permute-start.3 = (bf16[2,9,16,256]{3,2,1,0:T(8,128)(2,1)S(1)}, bf16[2,9,16,256]{3,2,1,0:T(8,128)(2,1)S(1)}, u32[]{:S(2)}, u32[]{:S(2)}) collective-permute-start(bf16[2,9,16,256]{3,2,1,0:T(8,128)(2,1)S(1)} %bitcast.27), channel_id=1, source_target_pairs={{0,3},{1,2},{2,1},{3,0},{4,7},{5,6},{6,5},{7,4},{8,11},{9,10},{10,... | collective-permute-start | bytes 442376 | tf_op jit(solution)/shard_map/ppermute | solution.py:29
  42.5 12.2 %copy-start.2 = (bf16[2,9,16,256]{3,2,1,0:T(8,128)(2,1)}, bf16[2,9,16,256]{3,2,1,0:T(8,128)(2,1)S(1)}, u32[]{:S(2)}) copy-start(bf16[2,9,16,256]{3,2,1,0:T(8,128)(2,1)S(1)} %collective-permute-done.1.refs_1_) | copy-start | bytes 442372
  47.4 7.3 %copy-start.3 = (bf16[2,9,16,256]{3,2,1,0:T(8,128)(2,1)}, bf16[2,9,16,256]{3,2,1,0:T(8,128)(2,1)S(1)}, u32[]{:S(2)}) copy-start(bf16[2,9,16,256]{3,2,1,0:T(8,128)(2,1)S(1)} %collective-permute-done.2.refs_2_) | copy-start | bytes 442372
  49.9 4.8 %copy-start.4 = (bf16[2,9,16,256]{3,2,1,0:T(8,128)(2,1)}, bf16[2,9,16,256]{3,2,1,0:T(8,128)(2,1)S(1)}, u32[]{:S(2)}) copy-start(bf16[2,9,16,256]{3,2,1,0:T(8,128)(2,1)S(1)} %collective-permute-done.3.refs_3_) | copy-start | bytes 442372
  55.4 13.2 %collective-permute-start.16 = (bf16[1024,256]{1,0:T(8,128)(2,1)S(1)}, bf16[1024,256]{1,0:T(8,128)(2,1)S(1)}, u32[]{:S(2)}, u32[]{:S(2)}) collective-permute-start(bf16[1024,256]{1,0:T(8,128)(2,1)S(1)} %join.5.refs_8_), channel_id=1, source_target_pairs={{0,32},{32,0},{1,33},{33,1},{2,34},{34,2},{3,35},{35,3},{4,36},{36... | collective-permute-start | bytes 1572872 | tf_op jit(solution)/shard_map/ppermute | solution.py:29
  56.3 5.3 %collective-permute-start.10 = (bf16[8,2,2,16,128]{4,3,2,1,0:T(8,128)(2,1)S(1)}, bf16[8,2,2,16,128]{4,3,2,1,0:T(8,128)(2,1)S(1)}, u32[]{:S(2)}, u32[]{:S(2)}) collective-permute-start(bf16[8,2,2,16,128]{4,3,2,1,0:T(8,128)(2,1)S(1)} %get-tuple-element.17), channel_id=1, source_target_pairs={{0,4},{4,0},{1,5},{5,1},{2,6},{6,2},{3,7},{7,3},{8,12},{12,8},{9,1... | collective-permute-start | bytes 393224 | tf_op jit(solution)/shard_map/ppermute | solution.py:29
  56.7 7.2 %collective-permute-start.7 = (bf16[8,2,2,16,128]{4,3,2,1,0:T(8,128)(2,1)S(1)}, bf16[8,2,2,16,128]{4,3,2,1,0:T(8,128)(2,1)S(1)}, u32[]{:S(2)}, u32[]{:S(2)}) collective-permute-start(bf16[8,2,2,16,128]{4,3,2,1,0:T(8,128)(2,1)S(1)} %get-tuple-element.16.refs_4_.refs_2_.refs_0_), channel_id=1, source_target_pairs={{0,1},{1,0},{2,3},{3,2},{4,5},{5,4},{6,7},{7,6},{8,9},{9,8},{10,11... | collective-permute-start | bytes 393224 | tf_op jit(solution)/shard_map/ppermute | solution.py:29
  57.9 7.2 %collective-permute-start.8 = (bf16[8,2,2,16,128]{4,3,2,1,0:T(8,128)(2,1)S(1)}, bf16[8,2,2,16,128]{4,3,2,1,0:T(8,128)(2,1)S(1)}, u32[]{:S(2)}, u32[]{:S(2)}) collective-permute-start(bf16[8,2,2,16,128]{4,3,2,1,0:T(8,128)(2,1)S(1)} %get-tuple-element.16.refs_4_.refs_2_.refs_0_), channel_id=1, source_target_pairs={{0,2},{1,3},{2,0},{3,1},{4,6},{5,7},{6,4},{7,5},{8,10},{9,11},{10,... | collective-permute-start | bytes 393224 | tf_op jit(solution)/shard_map/ppermute | solution.py:29
  60.3 7.5 %collective-permute-start.9 = (bf16[8,2,2,16,128]{4,3,2,1,0:T(8,128)(2,1)S(1)}, bf16[8,2,2,16,128]{4,3,2,1,0:T(8,128)(2,1)S(1)}, u32[]{:S(2)}, u32[]{:S(2)}) collective-permute-start(bf16[8,2,2,16,128]{4,3,2,1,0:T(8,128)(2,1)S(1)} %get-tuple-element.16.refs_4_.refs_2_.refs_0_), channel_id=1, source_target_pairs={{0,3},{1,2},{2,1},{3,0},{4,7},{5,6},{6,5},{7,4},{8,11},{9,10},{10,... | collective-permute-start | bytes 393224 | tf_op jit(solution)/shard_map/ppermute | solution.py:29
  61.6 19.1 %collective-permute-start.17 = (bf16[1024,256]{1,0:T(8,128)(2,1)S(1)}, bf16[1024,256]{1,0:T(8,128)(2,1)S(1)}, u32[]{:S(2)}, u32[]{:S(2)}) collective-permute-start(bf16[1024,256]{1,0:T(8,128)(2,1)S(1)} %join.5.refs_8_), channel_id=1, source_target_pairs={{0,8},{8,0},{1,9},{9,1},{2,10},{10,2},{3,11},{11,3},{4,12},{12,4},... | collective-permute-start | bytes 1572872 | tf_op jit(solution)/shard_map/ppermute | solution.py:29
  63.9 16.8 %collective-permute-start.11 = (bf16[8,2,2,16,128]{4,3,2,1,0:T(8,128)(2,1)S(1)}, bf16[8,2,2,16,128]{4,3,2,1,0:T(8,128)(2,1)S(1)}, u32[]{:S(2)}, u32[]{:S(2)}) collective-permute-start(bf16[8,2,2,16,128]{4,3,2,1,0:T(8,128)(2,1)S(1)} %collective-permute-done.10.refs_4_), channel_id=1, source_target_pairs={{0,1},{1,0},{2,3},{3,2},{4,5},{5,4},{6,7},{7,6},{8,9},{9,8},{10,11... | collective-permute-start | bytes 393224 | tf_op jit(solution)/shard_map/ppermute | solution.py:29
  65.1 15.6 %collective-permute-start.12 = (bf16[8,2,2,16,128]{4,3,2,1,0:T(8,128)(2,1)S(1)}, bf16[8,2,2,16,128]{4,3,2,1,0:T(8,128)(2,1)S(1)}, u32[]{:S(2)}, u32[]{:S(2)}) collective-permute-start(bf16[8,2,2,16,128]{4,3,2,1,0:T(8,128)(2,1)S(1)} %collective-permute-done.10.refs_4_), channel_id=1, source_target_pairs={{0,2},{1,3},{2,0},{3,1},{4,6},{5,7},{6,4},{7,5},{8,10},{9,11},{10,... | collective-permute-start | bytes 393224 | tf_op jit(solution)/shard_map/ppermute | solution.py:29
  67.8 12.9 %collective-permute-start.13 = (bf16[8,2,2,16,128]{4,3,2,1,0:T(8,128)(2,1)S(1)}, bf16[8,2,2,16,128]{4,3,2,1,0:T(8,128)(2,1)S(1)}, u32[]{:S(2)}, u32[]{:S(2)}) collective-permute-start(bf16[8,2,2,16,128]{4,3,2,1,0:T(8,128)(2,1)S(1)} %collective-permute-done.10.refs_4_), channel_id=1, source_target_pairs={{0,3},{1,2},{2,1},{3,0},{4,7},{5,6},{6,5},{7,4},{8,11},{9,10},{10,... | collective-permute-start | bytes 393224 | tf_op jit(solution)/shard_map/ppermute | solution.py:29
  68.6 12.1 %collective-permute-start.18 = (bf16[1024,256]{1,0:T(8,128)(2,1)S(1)}, bf16[1024,256]{1,0:T(8,128)(2,1)S(1)}, u32[]{:S(2)}, u32[]{:S(2)}) collective-permute-start(bf16[1024,256]{1,0:T(8,128)(2,1)S(1)} %collective-permute-done.16.refs_9_), channel_id=1, source_target_pairs={{0,8},{8,0},{1,9},{9,1},{2,10},{10,2},{3,11},{11,3},{4,12},{12,4},... | collective-permute-start | bytes 1572872 | tf_op jit(solution)/shard_map/ppermute | solution.py:29
  86.9 1.2 %collective-permute-start.19 = (f32[32,128]{1,0:T(8,128)S(1)}, f32[32,128]{1,0:T(8,128)S(1)}, u32[]{:S(2)}, u32[]{:S(2)}) collective-permute-start(f32[32,128]{1,0:T(8,128)S(1)} %get-tuple-element.20), channel_id=1, source_target_pairs={{0,8},{8,0},{1,9},{9,1},{2,10},{10,2},{3,11},{11,3},{4,12},{12,4},... | collective-permute-start | bytes 49160 | tf_op jit(solution)/shard_map/ppermute | solution.py:29

commit v5 on v4

--- a/solution.py
+++ b/solution.py
@@ -27,6 +27,22 @@
 def swap(a, axis, bit=1):
     count = lax.axis_size(axis)
     return lax.ppermute(a, axis, [(i, i ^ bit) for i in range(count)])
+
+
+def repeat_kernel(lists, send):
+    for d in range(send.shape[0]):
+        send[d] = lists[...]
+
+
+def repeat(lists, count):
+    return pl.pallas_call(
+        repeat_kernel,
+        out_shape=jax.ShapeDtypeStruct((count,) + lists.shape, lists.dtype),
+        in_specs=[IN_VMEM],
+        out_specs=IN_VMEM,
+        compiler_params=pltpu.CompilerParams(vmem_limit_bytes=VMEM),
+        name="repeat",
+    )(lists)
 
 
 def prepare_kernel(at, leaf, codes, kept, given, ordered):
@@ -271,8 +287,7 @@
     states = leaf_tables.shape[2]
     order = ("z1", "yh", "yl", "z4", "z2")
 
-    wanted = fetch_list.transpose(0, 2, 1)
-    wanted = jnp.broadcast_to(wanted, (cut_count,) + wanted.shape[1:])
+    wanted = repeat(fetch_list.transpose(0, 2, 1)[0], cut_count)
     wanted = lax.all_to_all(wanted, CUTS, 0, 0, tiled=True)
     rows_here = panels.transpose(1, 0, 2, 3).reshape(own, 2 * width)
     rows_here = [rows_here] + [swap(rows_here, ("z4", "z2"), bit) for bit in range(1, 4)]

time: 104 us -> 104 us (level)
    broadcast_in_dim x1 -> x0, local copies, waits for them, and re-layouts: 1.29 us -> none  [body(): wanted = jnp.broadcast_to(wanted, (cut_count,) + wanted.shape[1:])]
  transfers between devices with their start and end apart: 22 -> 22, of which waited for: 8 -> 8; matrix products, arithmetic and copies ran while one was open for 3% -> 2% of each run, Pallas kernels for 11% -> 12%
where the time goes in v5:
time: 104 us
  starting transfers between devices  43.6 us (42%)
  waiting for transfers between devices  20.6 us (20%)
  Pallas kernels  20.2 us (19%)
  blocking collectives  15.1 us (15%)
  local copies, waits for them, and re-layouts  4.07 us (4%)
    ppermute x20, starting transfers between devices, swap(): return lax.ppermute(a, axis, [(i, i ^ bit) for i in range(count)])  30.2 us
    all_to_all x1, blocking collectives, body(): amps = lax.all_to_all(amps, order, 0, 0, tiled=True)  15.1 us
    ppermute x20, waiting for transfers between devices, swap(): return lax.ppermute(a, axis, [(i, i ^ bit) for i in range(count)])  10.4 us
    pallas_call x1, Pallas kernels, weigh(): pl.pallas_call(weight_kernel, out_shape=pltpu.VMEM((rows, depth), BF), in...  10.1 us
    all_to_all x1, starting transfers between devices, body(): wanted = lax.all_to_all(wanted, CUTS, 0, 0, tiled=True)  8.7 us
    pallas_call x1, Pallas kernels, amplitudes_of(): pl.pallas_call(amp_kernel, out_shape=(jax.ShapeDtypeStruct((rows // each...  6.2 us
    all_to_all x1, waiting for transfers between devices, body(): wanted = lax.all_to_all(wanted, CUTS, 0, 0, tiled=True)  5.45 us
    all_to_all x1, waiting for transfers between devices, body(): slots = lax.all_to_all(sent, CUTS, 0, 0, tiled=True)  4.8 us
  transfers between devices with their start and end apart: 22, of which 8 were waited for; matrix products, arithmetic and copies ran while one was open for 2% of the time, Pallas kernels for 12%

profile of v5, /device:TPU:1, one launch (start us, length us, event | category | flops | bytes accessed | tf_op | source)
XLA Modules:
  0.0 104.0 jit_solution(14239342481795352040)
XLA Ops:
  0.0 0.8 copy.16
  0.8 3.9 %collective-permute-start.4 = (bf16[64,256]{1,0:T(8,128)(2,1)S(1)}, bf16[64,256]{1,0:T(8,128)(2,1)S(1)}, u32[]{:S(2)}, u32[]{:S(2)}) collective-permute-start(bf16[64,256]{1,0:T(8,128)(2,1)S(1)} %bitcast.30), channel_id=1, source_target_pairs={{0,64},{64,0},{128,192},{192,128},{1,65},{65,1},{129,193},{193,129... | collective-permute-start | bytes 98312 | tf_op jit(solution)/shard_map/ppermute | solution.py:29
  4.7 5.1 %collective-permute-start.5 = (bf16[64,256]{1,0:T(8,128)(2,1)S(1)}, bf16[64,256]{1,0:T(8,128)(2,1)S(1)}, u32[]{:S(2)}, u32[]{:S(2)}) collective-permute-start(bf16[64,256]{1,0:T(8,128)(2,1)S(1)} %bitcast.31), channel_id=1, source_target_pairs={{0,128},{64,192},{128,0},{192,64},{1,129},{65,193},{129,1},{193,65... | collective-permute-start | bytes 98312 | tf_op jit(solution)/shard_map/ppermute | solution.py:29
  9.8 0.0 collective-permute-start.6
  9.8 0.7 copy-done.2
  10.5 0.6 repeat.1
  11.1 8.7 %all-to-all-start = ((s32[32,2,32]{2,1,0:T(2,128)}), s32[32,2,32]{2,1,0:T(2,128)S(1)}, u32[]{:S(2)}, u32[]{:S(2)}) async-start(s32[32,2,32]{2,1,0:T(2,128)} %repeat.1), calls=%async_computation | async-start | bytes 65536 | tf_op jit(solution)/shard_map/all_to_all | solution.py:291
  19.8 0.1 pad_add_fusion.1.at
  19.9 0.8 copy.14
  20.7 0.1 reshape.31.codes
  20.8 1.0 reshape.29.leaf
  21.8 0.6 prepare.1
  22.5 5.5 %all-to-all-done.wanted = s32[32,2,32]{2,1,0:T(2,128)S(1)} async-done(((s32[32,2,32]{2,1,0:T(2,128)}), s32[32,2,32]{2,1,0:T(2,128)S(1)}, u32[]{:S(2)}, u32[]{:S(2)}) %all-to-all-start) | async-done | bytes 8224 | tf_op jit(solution)/shard_map/all_to_all | solution.py:291
  27.9 0.0 collective-permute-done.4.refs_1_
  28.0 2.0 %pack.1 = (bf16[32,2,2,16,128]{4,3,2,1,0:T(8,128)(2,1)}, bf16[256,256]{1,0:T(8,128)(2,1)S(1)}) custom-call(s32[1]{0:T(128)} %bitcast.8.me, s32[1]{0:T(128)} %bitcast.1.part, s32[32,2,32]{2,1,0:T(2,128)S(1)} %all-to-all-done.wanted, bf16[12,2,128,128]{3,2,1,0:T(8,128)(2,1)} %table.1, bf16[64,256]{1,0:T(8,128)(2,1)S(1)} %bitcast.33, ...), custom_call_target="tpu_custom_call" | custom-call | tf_op jit(solution)/shard_map/pack/pallas_call | solution.py:122
  29.9 0.4 collective-permute-start.14
  30.3 2.6 %collective-permute-start = (bf16[9,16,256]{2,1,0:T(8,128)(2,1)S(1)}, bf16[9,16,256]{2,1,0:T(8,128)(2,1)S(1)}, u32[]{:S(2)}, u32[]{:S(2)}) collective-permute-start(bf16[9,16,256]{2,1,0:T(8,128)(2,1)S(1)} %get-tuple-element.14.refs_4_), channel_id=1, source_target_pairs={{0,4},{4,0},{1,5},{5,1},{2,6},{6,2},{3,7},{7,3},{8,12},{12,8},{9,1... | collective-permute-start | bytes 221192 | tf_op jit(solution)/shard_map/ppermute | solution.py:29
  32.9 4.7 %all-to-all-start.1 = ((bf16[32,2,2,16,128]{4,3,2,1,0:T(8,128)(2,1)}), bf16[32,2,2,16,128]{4,3,2,1,0:T(8,128)(2,1)S(1)}, u32[]{:S(2)}, u32[]{:S(2)}) async-start(bf16[32,2,2,16,128]{4,3,2,1,0:T(8,128)(2,1)} %get-tuple-element.15), calls=%async_computation.1 | async-start | bytes 1048576 | tf_op jit(solution)/shard_map/all_to_all | solution.py:303
  37.7 0.4 collective-permute-start.15
  38.1 1.3 %collective-permute-start.1 = (bf16[2,9,16,256]{3,2,1,0:T(8,128)(2,1)S(1)}, bf16[2,9,16,256]{3,2,1,0:T(8,128)(2,1)S(1)}, u32[]{:S(2)}, u32[]{:S(2)}) collective-permute-start(bf16[2,9,16,256]{3,2,1,0:T(8,128)(2,1)S(1)} %bitcast.25), channel_id=1, source_target_pairs={{0,1},{1,0},{2,3},{3,2},{4,5},{5,4},{6,7},{7,6},{8,9},{9,8},{10,11... | collective-permute-start | bytes 442376 | tf_op jit(solution)/shard_map/ppermute | solution.py:29
  39.4 2.5 %collective-permute-start.2 = (bf16[2,9,16,256]{3,2,1,0:T(8,128)(2,1)S(1)}, bf16[2,9,16,256]{3,2,1,0:T(8,128)(2,1)S(1)}, u32[]{:S(2)}, u32[]{:S(2)}) collective-permute-start(bf16[2,9,16,256]{3,2,1,0:T(8,128)(2,1)S(1)} %bitcast.26), channel_id=1, source_target_pairs={{0,2},{1,3},{2,0},{3,1},{4,6},{5,7},{6,4},{7,5},{8,10},{9,11},{10,... | collective-permute-start | bytes 442376 | tf_op jit(solution)/shard_map/ppermute | solution.py:29
  41.9 0.2 collective-permute-start.3
  42.1 0.4 collective-permute-done.1.refs_1_
  42.5 4.9 %collective-permute-done.2.refs_2_ = bf16[2,9,16,256]{3,2,1,0:T(8,128)(2,1)S(1)} collective-permute-done((bf16[2,9,16,256]{3,2,1,0:T(8,128)(2,1)S(1)}, bf16[2,9,16,256]{3,2,1,0:T(8,128)(2,1)S(1)}, u32[]{:S(2)}, u32[]{:S(2)}) %collective-permute-start.2) | collective-permute-done | bytes 147488 | tf_op jit(solution)/shard_map/ppermute | solution.py:29
  47.4 2.5 %collective-permute-done.3.refs_3_ = bf16[2,9,16,256]{3,2,1,0:T(8,128)(2,1)S(1)} collective-permute-done((bf16[2,9,16,256]{3,2,1,0:T(8,128)(2,1)S(1)}, bf16[2,9,16,256]{3,2,1,0:T(8,128)(2,1)S(1)}, u32[]{:S(2)}, u32[]{:S(2)}) %collective-permute-start.3) | collective-permute-done | bytes 147488 | tf_op jit(solution)/shard_map/ppermute | solution.py:29
  49.9 4.8 %all-to-all-done.1 = bf16[32,2,2,16,128]{4,3,2,1,0:T(8,128)(2,1)S(1)} async-done(((bf16[32,2,2,16,128]{4,3,2,1,0:T(8,128)(2,1)}), bf16[32,2,2,16,128]{4,3,2,1,0:T(8,128)(2,1)S(1)}, u32[]{:S(2)}, u32[]{:S(2)}) %all-to-all-start.1) | async-done | bytes 524320 | tf_op jit(solution)/shard_map/all_to_all | solution.py:303
  54.7 0.6 choose.1
  55.4 0.9 collective-permute-start.16
  56.3 0.3 collective-permute-start.10
  56.7 1.2 %collective-permute-start.7 = (bf16[8,2,2,16,128]{4,3,2,1,0:T(8,128)(2,1)S(1)}, bf16[8,2,2,16,128]{4,3,2,1,0:T(8,128)(2,1)S(1)}, u32[]{:S(2)}, u32[]{:S(2)}) collective-permute-start(bf16[8,2,2,16,128]{4,3,2,1,0:T(8,128)(2,1)S(1)} %get-tuple-element.16.refs_4_.refs_2_.refs_0_), channel_id=1, source_target_pairs={{0,1},{1,0},{2,3},{3,2},{4,5},{5,4},{6,7},{7,6},{8,9},{9,8},{10,11... | collective-permute-start | bytes 393224 | tf_op jit(solution)/shard_map/ppermute | solution.py:29
  57.9 2.5 %collective-permute-start.8 = (bf16[8,2,2,16,128]{4,3,2,1,0:T(8,128)(2,1)S(1)}, bf16[8,2,2,16,128]{4,3,2,1,0:T(8,128)(2,1)S(1)}, u32[]{:S(2)}, u32[]{:S(2)}) collective-permute-start(bf16[8,2,2,16,128]{4,3,2,1,0:T(8,128)(2,1)S(1)} %get-tuple-element.16.refs_4_.refs_2_.refs_0_), channel_id=1, source_target_pairs={{0,2},{1,3},{2,0},{3,1},{4,6},{5,7},{6,4},{7,5},{8,10},{9,11},{10,... | collective-permute-start | bytes 393224 | tf_op jit(solution)/shard_map/ppermute | solution.py:29
  60.3 0.2 collective-permute-start.9
  60.5 0.1 pad_add_fusion.me
  60.6 1.0 collective-permute-done.10.refs_4_
  61.6 2.2 %collective-permute-start.17 = (bf16[1024,256]{1,0:T(8,128)(2,1)S(1)}, bf16[1024,256]{1,0:T(8,128)(2,1)S(1)}, u32[]{:S(2)}, u32[]{:S(2)}) collective-permute-start(bf16[1024,256]{1,0:T(8,128)(2,1)S(1)} %join.5.refs_8_), channel_id=1, source_target_pairs={{0,8},{8,0},{1,9},{9,1},{2,10},{10,2},{3,11},{11,3},{4,12},{12,4},... | collective-permute-start | bytes 1572872 | tf_op jit(solution)/shard_map/ppermute | solution.py:29
  63.9 1.2 %collective-permute-start.11 = (bf16[8,2,2,16,128]{4,3,2,1,0:T(8,128)(2,1)S(1)}, bf16[8,2,2,16,128]{4,3,2,1,0:T(8,128)(2,1)S(1)}, u32[]{:S(2)}, u32[]{:S(2)}) collective-permute-start(bf16[8,2,2,16,128]{4,3,2,1,0:T(8,128)(2,1)S(1)} %collective-permute-done.10.refs_4_), channel_id=1, source_target_pairs={{0,1},{1,0},{2,3},{3,2},{4,5},{5,4},{6,7},{7,6},{8,9},{9,8},{10,11... | collective-permute-start | bytes 393224 | tf_op jit(solution)/shard_map/ppermute | solution.py:29
  65.1 2.5 %collective-permute-start.12 = (bf16[8,2,2,16,128]{4,3,2,1,0:T(8,128)(2,1)S(1)}, bf16[8,2,2,16,128]{4,3,2,1,0:T(8,128)(2,1)S(1)}, u32[]{:S(2)}, u32[]{:S(2)}) collective-permute-start(bf16[8,2,2,16,128]{4,3,2,1,0:T(8,128)(2,1)S(1)} %collective-permute-done.10.refs_4_), channel_id=1, source_target_pairs={{0,2},{1,3},{2,0},{3,1},{4,6},{5,7},{6,4},{7,5},{8,10},{9,11},{10,... | collective-permute-start | bytes 393224 | tf_op jit(solution)/shard_map/ppermute | solution.py:29
  67.5 0.3 collective-permute-done.9.refs_3_
  67.8 0.8 collective-permute-start.13
  68.6 2.0 %collective-permute-start.18 = (bf16[1024,256]{1,0:T(8,128)(2,1)S(1)}, bf16[1024,256]{1,0:T(8,128)(2,1)S(1)}, u32[]{:S(2)}, u32[]{:S(2)}) collective-permute-start(bf16[1024,256]{1,0:T(8,128)(2,1)S(1)} %collective-permute-done.16.refs_9_), channel_id=1, source_target_pairs={{0,8},{8,0},{1,9},{9,1},{2,10},{10,2},{3,11},{11,3},{4,12},{12,4},... | collective-permute-start | bytes 1572872 | tf_op jit(solution)/shard_map/ppermute | solution.py:29
  70.6 10.1 %weigh.1.weights = bf16[4096,2048]{1,0:T(8,128)(2,1)S(1)} custom-call(s32[1]{0:T(128)} %bitcast.1.part, bf16[2,9,16,256]{3,2,1,0:T(8,128)(2,1)} %bitcast.29, bf16[2,9,16,256]{3,2,1,0:T(8,128)(2,1)} %copy-done.3, bf16[2,9,16,256]{3,2,1,0:T(8,128)(2,1)} %copy-done.4, bf16[2,9,16,256]{3,2,1,0:T(8,128)(2,1)} %copy-done.5, ...), custom_call_target="tpu_custom_call" | custom-call | flops 17179869184 | bytes 16777216 | tf_op jit(solution)/shard_map/weigh/pallas_call | solution.py:201
  80.7 6.2 %amplitudes.1 = (f32[32,128]{1,0:T(8,128)S(1)}, f32[32,128]{1,0:T(8,128)S(1)}) custom-call(s32[2]{0:T(128)S(1)} %pad_add_fusion.me, bf16[4096,2048]{1,0:T(8,128)(2,1)S(1)} %weigh.1.weights, bf16[8,2,2,16,128]{4,3,2,1,0:T(8,128)(2,1)S(1)} %get-tuple-element.16.refs_4_.refs_2_.refs_0_, bf16[8,2,2,16,128]{4,3,2,1,0:T(8,128)(2,1)S(1)} %collective-permute-done.7.refs_1_, ...), custom_call_target="tpu_custom_call" | custom-call | tf_op jit(solution)/shard_map/amplitudes/pallas_call | solution.py:265
  86.9 0.1 collective-permute-start.19
  87.0 1.2 %collective-permute-done.19 = f32[32,128]{1,0:T(8,128)S(1)} collective-permute-done((f32[32,128]{1,0:T(8,128)S(1)}, f32[32,128]{1,0:T(8,128)S(1)}, u32[]{:S(2)}, u32[]{:S(2)}) %collective-permute-start.19) | collective-permute-done | bytes 16416 | tf_op jit(solution)/shard_map/ppermute | solution.py:29
  88.2 15.1 %all_to_all.19 = f32[32,1,128]{2,1,0:T(1,128)S(1)} all-to-all(f32[32,1,128]{2,1,0:T(1,128)S(1)} %bitcast.38), channel_id=1, replica_groups=mesh['z4'=2,'z2'=2,'z1'=2,'yl'=2,'core'=2,'yh'=2,'x'=4] {'z1','yh','yl',..., dimensions={0} | all-to-all | bytes 32768 | tf_op jit(solution)/shard_map/all_to_all | solution.py:327
  103.2 0.1 reduce_sum.9
  103.3 0.1 reshape.36
  103.4 0.6 copy.18
  (30 shorter events, 0.1 us)
Async XLA Ops:
  0.8 27.1 %collective-permute-start.4 = (bf16[64,256]{1,0:T(8,128)(2,1)S(1)}, bf16[64,256]{1,0:T(8,128)(2,1)S(1)}, u32[]{:S(2)}, u32[]{:S(2)}) collective-permute-start(bf16[64,256]{1,0:T(8,128)(2,1)S(1)} %bitcast.30), channel_id=1, source_target_pairs={{0,64},{64,0},{128,192},{192,128},{1,65},{65,1},{129,193},{193,129... | collective-permute-start | bytes 98312 | tf_op jit(solution)/shard_map/ppermute | solution.py:29
  4.7 23.2 %collective-permute-start.5 = (bf16[64,256]{1,0:T(8,128)(2,1)S(1)}, bf16[64,256]{1,0:T(8,128)(2,1)S(1)}, u32[]{:S(2)}, u32[]{:S(2)}) collective-permute-start(bf16[64,256]{1,0:T(8,128)(2,1)S(1)} %bitcast.31), channel_id=1, source_target_pairs={{0,128},{64,192},{128,0},{192,64},{1,129},{65,193},{129,1},{193,65... | collective-permute-start | bytes 98312 | tf_op jit(solution)/shard_map/ppermute | solution.py:29
  9.8 18.1 %collective-permute-start.6 = (bf16[64,256]{1,0:T(8,128)(2,1)S(1)}, bf16[64,256]{1,0:T(8,128)(2,1)S(1)}, u32[]{:S(2)}, u32[]{:S(2)}) collective-permute-start(bf16[64,256]{1,0:T(8,128)(2,1)S(1)} %bitcast.32), channel_id=1, source_target_pairs={{0,192},{64,128},{128,64},{192,0},{1,193},{65,129},{129,65},{193,1... | collective-permute-start | bytes 98312 | tf_op jit(solution)/shard_map/ppermute | solution.py:29
  9.8 0.7 copy-start.2
  11.1 16.8 %all-to-all-start = ((s32[32,2,32]{2,1,0:T(2,128)}), s32[32,2,32]{2,1,0:T(2,128)S(1)}, u32[]{:S(2)}, u32[]{:S(2)}) async-start(s32[32,2,32]{2,1,0:T(2,128)} %repeat.1), calls=%async_computation | async-start | bytes 65536 | tf_op jit(solution)/shard_map/all_to_all | solution.py:291
  29.9 7.7 %collective-permute-start.14 = (bf16[256,256]{1,0:T(8,128)(2,1)S(1)}, bf16[256,256]{1,0:T(8,128)(2,1)S(1)}, u32[]{:S(2)}, u32[]{:S(2)}) collective-permute-start(bf16[256,256]{1,0:T(8,128)(2,1)S(1)} %get-tuple-element.18.refs_0_), channel_id=1, source_target_pairs={{0,16},{16,0},{1,17},{17,1},{2,18},{18,2},{3,19},{19,3},{4,20},{20... | collective-permute-start | bytes 393224 | tf_op jit(solution)/shard_map/ppermute | solution.py:29
  30.3 7.8 %collective-permute-start = (bf16[9,16,256]{2,1,0:T(8,128)(2,1)S(1)}, bf16[9,16,256]{2,1,0:T(8,128)(2,1)S(1)}, u32[]{:S(2)}, u32[]{:S(2)}) collective-permute-start(bf16[9,16,256]{2,1,0:T(8,128)(2,1)S(1)} %get-tuple-element.14.refs_4_), channel_id=1, source_target_pairs={{0,4},{4,0},{1,5},{5,1},{2,6},{6,2},{3,7},{7,3},{8,12},{12,8},{9,1... | collective-permute-start | bytes 221192 | tf_op jit(solution)/shard_map/ppermute | solution.py:29
  32.9 21.8 %all-to-all-start.1 = ((bf16[32,2,2,16,128]{4,3,2,1,0:T(8,128)(2,1)}), bf16[32,2,2,16,128]{4,3,2,1,0:T(8,128)(2,1)S(1)}, u32[]{:S(2)}, u32[]{:S(2)}) async-start(bf16[32,2,2,16,128]{4,3,2,1,0:T(8,128)(2,1)} %get-tuple-element.15), calls=%async_computation.1 | async-start | bytes 1048576 | tf_op jit(solution)/shard_map/all_to_all | solution.py:303
  37.7 17.7 %collective-permute-start.15 = (bf16[512,256]{1,0:T(8,128)(2,1)S(1)}, bf16[512,256]{1,0:T(8,128)(2,1)S(1)}, u32[]{:S(2)}, u32[]{:S(2)}) collective-permute-start(bf16[512,256]{1,0:T(8,128)(2,1)S(1)} %join.4.refs_0_), channel_id=1, source_target_pairs={{0,4},{4,0},{1,5},{5,1},{2,6},{6,2},{3,7},{7,3},{8,12},{12,8},{9,1... | collective-permute-start | bytes 786440 | tf_op jit(solution)/shard_map/ppermute | solution.py:29
  38.1 16.6 %copy-start.1 = (s32[16,2]{0,1:T(2,128)S(1)}, s32[16,2]{0,1:T(2,128)}, u32[]{:S(2)}) copy-start(s32[16,2]{0,1:T(2,128)} %param.11) | copy-start | bytes 388
  38.1 16.6 %copy-start = (bf16[18,16,256]{2,1,0:T(8,128)(2,1)}, bf16[18,16,256]{2,1,0:T(8,128)(2,1)S(1)}, u32[]{:S(2)}) copy-start(bf16[18,16,256]{2,1,0:T(8,128)(2,1)S(1)} %join.3) | copy-start | bytes 442372
  38.1 4.4 %collective-permute-start.1 = (bf16[2,9,16,256]{3,2,1,0:T(8,128)(2,1)S(1)}, bf16[2,9,16,256]{3,2,1,0:T(8,128)(2,1)S(1)}, u32[]{:S(2)}, u32[]{:S(2)}) collective-permute-start(bf16[2,9,16,256]{3,2,1,0:T(8,128)(2,1)S(1)} %bitcast.25), channel_id=1, source_target_pairs={{0,1},{1,0},{2,3},{3,2},{4,5},{5,4},{6,7},{7,6},{8,9},{9,8},{10,11... | collective-permute-start | bytes 442376 | tf_op jit(solution)/shard_map/ppermute | solution.py:29
  39.4 8.0 %collective-permute-start.2 = (bf16[2,9,16,256]{3,2,1,0:T(8,128)(2,1)S(1)}, bf16[2,9,16,256]{3,2,1,0:T(8,128)(2,1)S(1)}, u32[]{:S(2)}, u32[]{:S(2)}) collective-permute-start(bf16[2,9,16,256]{3,2,1,0:T(8,128)(2,1)S(1)} %bitcast.26), channel_id=1, source_target_pairs={{0,2},{1,3},{2,0},{3,1},{4,6},{5,7},{6,4},{7,5},{8,10},{9,11},{10,... | collective-permute-start | bytes 442376 | tf_op jit(solution)/shard_map/ppermute | solution.py:29
  41.9 8.0 %collective-permute-start.3 = (bf16[2,9,16,256]{3,2,1,0:T(8,128)(2,1)S(1)}, bf16[2,9,16,256]{3,2,1,0:T(8,128)(2,1)S(1)}, u32[]{:S(2)}, u32[]{:S(2)}) collective-permute-start(bf16[2,9,16,256]{3,2,1,0:T(8,128)(2,1)S(1)} %bitcast.27), channel_id=1, source_target_pairs={{0,3},{1,2},{2,1},{3,0},{4,7},{5,6},{6,5},{7,4},{8,11},{9,10},{10,... | collective-permute-start | bytes 442376 | tf_op jit(solution)/shard_map/ppermute | solution.py:29
  42.5 12.2 %copy-start.3 = (bf16[2,9,16,256]{3,2,1,0:T(8,128)(2,1)}, bf16[2,9,16,256]{3,2,1,0:T(8,128)(2,1)S(1)}, u32[]{:S(2)}) copy-start(bf16[2,9,16,256]{3,2,1,0:T(8,128)(2,1)S(1)} %collective-permute-done.1.refs_1_) | copy-start | bytes 442372
  47.4 7.3 %copy-start.4 = (bf16[2,9,16,256]{3,2,1,0:T(8,128)(2,1)}, bf16[2,9,16,256]{3,2,1,0:T(8,128)(2,1)S(1)}, u32[]{:S(2)}) copy-start(bf16[2,9,16,256]{3,2,1,0:T(8,128)(2,1)S(1)} %collective-permute-done.2.refs_2_) | copy-start | bytes 442372
  49.9 4.8 %copy-start.5 = (bf16[2,9,16,256]{3,2,1,0:T(8,128)(2,1)}, bf16[2,9,16,256]{3,2,1,0:T(8,128)(2,1)S(1)}, u32[]{:S(2)}) copy-start(bf16[2,9,16,256]{3,2,1,0:T(8,128)(2,1)S(1)} %collective-permute-done.3.refs_3_) | copy-start | bytes 442372
  55.4 13.2 %collective-permute-start.16 = (bf16[1024,256]{1,0:T(8,128)(2,1)S(1)}, bf16[1024,256]{1,0:T(8,128)(2,1)S(1)}, u32[]{:S(2)}, u32[]{:S(2)}) collective-permute-start(bf16[1024,256]{1,0:T(8,128)(2,1)S(1)} %join.5.refs_8_), channel_id=1, source_target_pairs={{0,32},{32,0},{1,33},{33,1},{2,34},{34,2},{3,35},{35,3},{4,36},{36... | collective-permute-start | bytes 1572872 | tf_op jit(solution)/shard_map/ppermute | solution.py:29
  56.3 5.3 %collective-permute-start.10 = (bf16[8,2,2,16,128]{4,3,2,1,0:T(8,128)(2,1)S(1)}, bf16[8,2,2,16,128]{4,3,2,1,0:T(8,128)(2,1)S(1)}, u32[]{:S(2)}, u32[]{:S(2)}) collective-permute-start(bf16[8,2,2,16,128]{4,3,2,1,0:T(8,128)(2,1)S(1)} %get-tuple-element.17), channel_id=1, source_target_pairs={{0,4},{4,0},{1,5},{5,1},{2,6},{6,2},{3,7},{7,3},{8,12},{12,8},{9,1... | collective-permute-start | bytes 393224 | tf_op jit(solution)/shard_map/ppermute | solution.py:29
  56.7 7.2 %collective-permute-start.7 = (bf16[8,2,2,16,128]{4,3,2,1,0:T(8,128)(2,1)S(1)}, bf16[8,2,2,16,128]{4,3,2,1,0:T(8,128)(2,1)S(1)}, u32[]{:S(2)}, u32[]{:S(2)}) collective-permute-start(bf16[8,2,2,16,128]{4,3,2,1,0:T(8,128)(2,1)S(1)} %get-tuple-element.16.refs_4_.refs_2_.refs_0_), channel_id=1, source_target_pairs={{0,1},{1,0},{2,3},{3,2},{4,5},{5,4},{6,7},{7,6},{8,9},{9,8},{10,11... | collective-permute-start | bytes 393224 | tf_op jit(solution)/shard_map/ppermute | solution.py:29
  57.9 7.2 %collective-permute-start.8 = (bf16[8,2,2,16,128]{4,3,2,1,0:T(8,128)(2,1)S(1)}, bf16[8,2,2,16,128]{4,3,2,1,0:T(8,128)(2,1)S(1)}, u32[]{:S(2)}, u32[]{:S(2)}) collective-permute-start(bf16[8,2,2,16,128]{4,3,2,1,0:T(8,128)(2,1)S(1)} %get-tuple-element.16.refs_4_.refs_2_.refs_0_), channel_id=1, source_target_pairs={{0,2},{1,3},{2,0},{3,1},{4,6},{5,7},{6,4},{7,5},{8,10},{9,11},{10,... | collective-permute-start | bytes 393224 | tf_op jit(solution)/shard_map/ppermute | solution.py:29
  60.3 7.5 %collective-permute-start.9 = (bf16[8,2,2,16,128]{4,3,2,1,0:T(8,128)(2,1)S(1)}, bf16[8,2,2,16,128]{4,3,2,1,0:T(8,128)(2,1)S(1)}, u32[]{:S(2)}, u32[]{:S(2)}) collective-permute-start(bf16[8,2,2,16,128]{4,3,2,1,0:T(8,128)(2,1)S(1)} %get-tuple-element.16.refs_4_.refs_2_.refs_0_), channel_id=1, source_target_pairs={{0,3},{1,2},{2,1},{3,0},{4,7},{5,6},{6,5},{7,4},{8,11},{9,10},{10,... | collective-permute-start | bytes 393224 | tf_op jit(solution)/shard_map/ppermute | solution.py:29
  61.6 19.1 %collective-permute-start.17 = (bf16[1024,256]{1,0:T(8,128)(2,1)S(1)}, bf16[1024,256]{1,0:T(8,128)(2,1)S(1)}, u32[]{:S(2)}, u32[]{:S(2)}) collective-permute-start(bf16[1024,256]{1,0:T(8,128)(2,1)S(1)} %join.5.refs_8_), channel_id=1, source_target_pairs={{0,8},{8,0},{1,9},{9,1},{2,10},{10,2},{3,11},{11,3},{4,12},{12,4},... | collective-permute-start | bytes 1572872 | tf_op jit(solution)/shard_map/ppermute | solution.py:29
  63.9 16.8 %collective-permute-start.11 = (bf16[8,2,2,16,128]{4,3,2,1,0:T(8,128)(2,1)S(1)}, bf16[8,2,2,16,128]{4,3,2,1,0:T(8,128)(2,1)S(1)}, u32[]{:S(2)}, u32[]{:S(2)}) collective-permute-start(bf16[8,2,2,16,128]{4,3,2,1,0:T(8,128)(2,1)S(1)} %collective-permute-done.10.refs_4_), channel_id=1, source_target_pairs={{0,1},{1,0},{2,3},{3,2},{4,5},{5,4},{6,7},{7,6},{8,9},{9,8},{10,11... | collective-permute-start | bytes 393224 | tf_op jit(solution)/shard_map/ppermute | solution.py:29
  65.1 15.6 %collective-permute-start.12 = (bf16[8,2,2,16,128]{4,3,2,1,0:T(8,128)(2,1)S(1)}, bf16[8,2,2,16,128]{4,3,2,1,0:T(8,128)(2,1)S(1)}, u32[]{:S(2)}, u32[]{:S(2)}) collective-permute-start(bf16[8,2,2,16,128]{4,3,2,1,0:T(8,128)(2,1)S(1)} %collective-permute-done.10.refs_4_), channel_id=1, source_target_pairs={{0,2},{1,3},{2,0},{3,1},{4,6},{5,7},{6,4},{7,5},{8,10},{9,11},{10,... | collective-permute-start | bytes 393224 | tf_op jit(solution)/shard_map/ppermute | solution.py:29
  67.8 12.9 %collective-permute-start.13 = (bf16[8,2,2,16,128]{4,3,2,1,0:T(8,128)(2,1)S(1)}, bf16[8,2,2,16,128]{4,3,2,1,0:T(8,128)(2,1)S(1)}, u32[]{:S(2)}, u32[]{:S(2)}) collective-permute-start(bf16[8,2,2,16,128]{4,3,2,1,0:T(8,128)(2,1)S(1)} %collective-permute-done.10.refs_4_), channel_id=1, source_target_pairs={{0,3},{1,2},{2,1},{3,0},{4,7},{5,6},{6,5},{7,4},{8,11},{9,10},{10,... | collective-permute-start | bytes 393224 | tf_op jit(solution)/shard_map/ppermute | solution.py:29
  68.6 12.1 %collective-permute-start.18 = (bf16[1024,256]{1,0:T(8,128)(2,1)S(1)}, bf16[1024,256]{1,0:T(8,128)(2,1)S(1)}, u32[]{:S(2)}, u32[]{:S(2)}) collective-permute-start(bf16[1024,256]{1,0:T(8,128)(2,1)S(1)} %collective-permute-done.16.refs_9_), channel_id=1, source_target_pairs={{0,8},{8,0},{1,9},{9,1},{2,10},{10,2},{3,11},{11,3},{4,12},{12,4},... | collective-permute-start | bytes 1572872 | tf_op jit(solution)/shard_map/ppermute | solution.py:29
  86.9 1.2 %collective-permute-start.19 = (f32[32,128]{1,0:T(8,128)S(1)}, f32[32,128]{1,0:T(8,128)S(1)}, u32[]{:S(2)}, u32[]{:S(2)}) collective-permute-start(f32[32,128]{1,0:T(8,128)S(1)} %get-tuple-element.20), channel_id=1, source_target_pairs={{0,8},{8,0},{1,9},{9,1},{2,10},{10,2},{3,11},{11,3},{4,12},{12,4},... | collective-permute-start | bytes 49160 | tf_op jit(solution)/shard_map/ppermute | solution.py:29
